TPU v7x, 32 devices: a whole 2x2x4 slice. The times are simulated.
32 devices in a mesh: dp: 8 (over y, x, core), seq: 4 (over z).
Axes of the slice: x: 2, y: 2, z: 4, core: 2. Of those that a mesh axis runs over, the one named last changes fastest.
Arguments:
- inputs: bfloat16 [8, 512, 2048], P('dp', 'seq'), may hold values from -6 to 6
- cotangent: bfloat16 [8, 512, 2048], P('dp', 'seq'), may hold values from -6 to 6
- segments: int32 [8, 512], P('dp', 'seq'), may hold values from 0 to 16, as said below
- labels: int32 [8, 512], P('dp', 'seq'), may hold values from 0 to 1
- step_ends: int32 [8, 512], P('dp', 'seq'), may hold values 0 or 1
- attend_gain: bfloat16 [2048], P(('dp', 'seq')), may hold values from 0.5 to 1.5
- attend_shift: bfloat16 [2048], P(('dp', 'seq')), may hold values from -1 to 1
- project_in: bfloat16 [2048, 6144], P(('dp', 'seq')), may hold values from -0.1875 to 0.1875
- project_bias: bfloat16 [4096], P(('dp', 'seq')), may hold values from -1 to 1
- project_out: bfloat16 [2048, 2048], P(('dp', 'seq')), may hold values from -1 to 1
- output_bias: bfloat16 [2048], P(('dp', 'seq')), may hold values from -1 to 1
- dense_gain: bfloat16 [2048], P(('dp', 'seq')), may hold values from 0.5 to 1.5
- dense_shift: bfloat16 [2048], P(('dp', 'seq')), may hold values from -1 to 1
- up_weight: bfloat16 [2048, 8192], P(('dp', 'seq')), may hold values from -0.125 to 0.125
- up_bias: bfloat16 [8192], P(('dp', 'seq')), may hold values from -1 to 1
- down_weight: bfloat16 [8192, 2048], P(('dp', 'seq')), may hold values from -0.0625 to 0.0625
- down_bias: bfloat16 [2048], P(('dp', 'seq')), may hold values from -1 to 1
- reward_weight: bfloat16 [2048], P(('dp', 'seq')), may hold values from -0.125 to 0.125
Outputs:
- outputs: bfloat16 [8, 512, 2048], P('dp', 'seq')
- rewards: float32 [8, 512], P('dp', 'seq')
- inputs_gradient: float32 [8, 512, 2048], P('dp', 'seq')
- attend_gain_gradient: float32 [2048], P(('dp', 'seq'))
- attend_shift_gradient: float32 [2048], P(('dp', 'seq'))
- project_in_gradient: float32 [2048, 6144], P(('dp', 'seq'))
- project_bias_gradient: float32 [4096], P(('dp', 'seq'))
- project_out_gradient: float32 [2048, 2048], P(('dp', 'seq'))
- output_bias_gradient: float32 [2048], P(('dp', 'seq'))
- dense_gain_gradient: float32 [2048], P(('dp', 'seq'))
- dense_shift_gradient: float32 [2048], P(('dp', 'seq'))
- up_weight_gradient: float32 [2048, 8192], P(('dp', 'seq'))
- up_bias_gradient: float32 [8192], P(('dp', 'seq'))
- down_weight_gradient: float32 [8192, 2048], P(('dp', 'seq'))
- down_bias_gradient: float32 [2048], P(('dp', 'seq'))
- reward_weight_gradient: float32 [2048], P(('dp', 'seq'))
Inputs may be any that keep to these rules, and one draw needn't show every extreme that they name: `segments`: in each row, the positions before a prefix length of 64 to 128 hold 0; then come 4 to 16 solutions numbered 1 upward in order, each a run of one or more positions; one row has 16 solutions.
All inputs are finite; a program needn't handle non-finite values. No bound on the sum of `step_ends` on one device may be relied on, other than what follows from the above.
Results may differ from a plain program's by a relative error of at most 0.013.
Values may be sent and summed in bfloat16 or wider, within the bound.
No kernel may reach another device: no remote copies, remote signals or barrier semaphores. Data moves between devices by JAX's collectives and lax.ppermute only.
A program may use at most 272 MiB of HBM per device.

v0:
```python
from functools import partial

import jax
import jax.numpy as jnp
from jax import lax
from jax.experimental import pallas as pl
from jax.experimental.pallas import tpu as pltpu
from jax.sharding import PartitionSpec as P

HEADS = 16
EPSILON = 1e-05
MASKED = -1e30
LOW = jnp.bfloat16
WIDE = jnp.float32
EVERY = ("dp", "seq")


def product(left, right):
    return jnp.dot(left, right, preferred_element_type=WIDE)


def inner_rows(left, right):
    return jnp.einsum("ta,tb->ab", left, right, preferred_element_type=WIDE)


def against_rows(left, right):
    return jnp.einsum("tb,ab->ta", left, right, preferred_element_type=WIDE)


def normal_parts(field):
    center = field - jnp.mean(field, axis=-1, keepdims=True)
    spread = jnp.mean(center * center, axis=-1, keepdims=True)
    inverse = lax.rsqrt(spread + EPSILON)
    return center * inverse, inverse


def normalize_back(upstream, normal, inverse, gain):
    scaled = upstream * gain
    mean_scaled = jnp.mean(scaled, axis=-1, keepdims=True)
    mean_cross = jnp.mean(scaled * normal, axis=-1, keepdims=True)
    return inverse * (scaled - mean_scaled - normal * mean_cross)


def ring_next():
    size = lax.axis_size("seq")
    return [(place, (place + 1) % size) for place in range(size)]


def after(value, done):
    return lax.optimization_barrier((value, tuple(done)))[0]


def fence(steady, work, *operands):
    shapes = jax.eval_shape(work, *operands)
    return lax.cond(
        steady,
        work,
        lambda *_: jax.tree.map(lambda shape: jnp.zeros(shape.shape, shape.dtype), shapes),
        *operands,
    )


def idle(gate):
    return []


def pieces_of(block, cut):
    rows = block.shape[0] // cut
    return [block[piece * rows : (piece + 1) * rows] for piece in range(cut)]


def ring_move(halves):
    return [lax.ppermute(half, "seq", ring_next()) for half in halves]


def ring_gather(block, flights=(idle,) * 3, use=None, plan=(), cut=2):
    blocks, results = [pieces_of(block, cut)], []
    for k in range(lax.axis_size("seq") - 1):
        moved = ring_move(blocks[-1])
        done = []
        if use is not None:
            for _ in range(plan[k]):
                results.append(use(len(results), blocks[len(results)]))
                done += jax.tree.leaves(results[-1])
        done += flights[k](blocks[-1])
        if done:
            moved[-1] = after(moved[-1], done)
        blocks.append(moved)
    return blocks if use is None else (blocks, results)


def ring_sum(part, flights=(idle,) * 3, cut=2):
    size = lax.axis_size("seq")
    sent = pieces_of(part(1, ()).astype(LOW), cut)
    for step, k in enumerate(list(range(2, size)) + [0]):
        kind = LOW if step < size - 2 else WIDE
        moved = ring_move(sent)
        term = part(k, sent)
        done = [term] + flights[step](sent)
        total = []
        for piece, (came, own) in enumerate(zip(moved, pieces_of(term, cut))):
            came = after(came, total + (done if piece == cut - 1 else []))
            total.append((came.astype(WIDE) + own).astype(kind))
        sent = total
    return jnp.concatenate(sent) if cut > 1 else sent[0]


def ring_step(total, part, kind=LOW):
    moved = lax.ppermute(total.astype(LOW), "seq", ring_next())
    return (moved.astype(WIDE) + part.astype(WIDE)).astype(kind)


def deal_kernel(pieces, wide, riders, me_ref, from_ref, *refs):
    rider_refs, to_refs, packed = refs[:riders], refs[riders:-1], refs[-1]
    ranks = len(to_refs)
    columns = from_ref.shape[1] // ranks
    if riders:
        packed[...] = jnp.zeros_like(packed)
        row = 0
        for rider_ref in rider_refs:
            lines, width = rider_ref.shape
            packed[row : row + lines, :width] = rider_ref[...].astype(WIDE)
            row += lines
    for shift, to_ref in enumerate(to_refs):
        to = lax.rem(me_ref[0] + shift, ranks)
        for place in range(columns // wide):
            start = pl.multiple_of(pieces(to, place) * wide, wide)
            to_ref[:, place * wide : (place + 1) * wide] = from_ref[:, pl.ds(start, wide)]
        if riders:
            to_ref[:, columns:] = packed[...].astype(to_ref.dtype)


def deal(matrix, pieces, wide, riders=()):
    ranks, me = lax.axis_size("seq"), lax.axis_index("seq")
    rows, columns = matrix.shape
    if wide % 128 == 0:
        each = columns // ranks + (128 if riders else 0)
        return pl.pallas_call(
            partial(deal_kernel, pieces, wide, len(riders)),
            out_shape=[jax.ShapeDtypeStruct((rows, each), matrix.dtype)] * ranks,
            grid_spec=pltpu.PrefetchScalarGridSpec(
                num_scalar_prefetch=1,
                grid=(1,),
                in_specs=[pl.BlockSpec((rows, columns), lambda i, me: (0, 0))]
                + [pl.BlockSpec(rider.shape, lambda i, me: (0, 0)) for rider in riders],
                out_specs=[pl.BlockSpec((rows, each), lambda i, me: (0, 0))] * ranks,
                scratch_shapes=[pltpu.VMEM((rows, 128), WIDE)],
            ),
            name="deal",
        )(me[None], matrix, *riders)
    dealt = jnp.stack(
        [
            jnp.concatenate(
                [
                    matrix[:, pieces(to, place) * wide :][:, :wide]
                    for place in range(columns // ranks // wide)
                ],
                axis=1,
            )
            for to in range(ranks)
        ]
    )
    return [
        lax.dynamic_index_in_dim(dealt, (me + shift) % ranks, 0, keepdims=False)
        for shift in range(ranks)
    ]


def collect_kernel(pieces, wide, me_ref, *refs):
    from_refs, to_ref = refs[:-1], refs[-1]
    ranks = len(from_refs)
    for shift, from_ref in enumerate(from_refs):
        source = lax.rem(me_ref[0] + ranks - shift, ranks)
        for place in range(from_ref.shape[1] // wide):
            start = pl.multiple_of(pieces(source, place) * wide, wide)
            to_ref[:, pl.ds(start, wide)] = from_ref[:, place * wide : (place + 1) * wide].astype(
                to_ref.dtype
            )


def collect(blocks, pieces, wide):
    ranks, me = lax.axis_size("seq"), lax.axis_index("seq")
    rows, columns = blocks[0].shape
    if wide % 128 == 0:
        return pl.pallas_call(
            partial(collect_kernel, pieces, wide),
            out_shape=jax.ShapeDtypeStruct((rows, columns * ranks), WIDE),
            grid_spec=pltpu.PrefetchScalarGridSpec(
                num_scalar_prefetch=1,
                grid=(1,),
                in_specs=[pl.BlockSpec((rows, columns), lambda i, me: (0, 0))] * ranks,
                out_specs=pl.BlockSpec((rows, columns * ranks), lambda i, me: (0, 0)),
            ),
            name="collect",
        )(me[None], *blocks)
    held = by_number(blocks)
    found = {
        pieces(to, place): held[to, :, place * wide : (place + 1) * wide]
        for to in range(ranks)
        for place in range(columns // wide)
    }
    return jnp.concatenate([found[piece] for piece in sorted(found)], axis=1).astype(WIDE)


def place_kernel(sources, to_row_ref, *refs):
    held, in_sem, out_sem = refs[-3:]
    from_refs, to_ref = refs[:-4], refs[-4]
    loads, stores = [], []
    at = 0
    for number, (array, row, rows, column, width, to_column) in enumerate(sources):
        start = pl.multiple_of(to_row_ref[number], rows)
        piece = held.at[pl.ds(at, rows), pl.ds(0, width)]
        source = from_refs[array].at[pl.ds(row, rows), pl.ds(column, width)]
        target = to_ref.at[pl.ds(start, rows), pl.ds(to_column, width)]
        loads.append(pltpu.make_async_copy(source, piece, in_sem.at[number]))
        stores.append(pltpu.make_async_copy(piece, target, out_sem.at[number]))
        at += rows
    for load in loads:
        load.start()
    for load, store in zip(loads, stores):
        load.wait()
        store.start()
    for store in stores:
        store.wait()


def place(arrays, sources, to_rows, shape):
    count = len(sources)
    wide = max(width for _, _, _, _, width, _ in sources)
    total = sum(rows for _, _, rows, _, _, _ in sources)
    return pl.pallas_call(
        partial(place_kernel, sources),
        out_shape=jax.ShapeDtypeStruct(shape, arrays[0].dtype),
        grid_spec=pltpu.PrefetchScalarGridSpec(
            num_scalar_prefetch=1,
            grid=(1,),
            in_specs=[pl.BlockSpec(memory_space=pl.ANY)] * len(arrays),
            out_specs=pl.BlockSpec(memory_space=pl.ANY),
            scratch_shapes=[
                pltpu.VMEM((total, wide), arrays[0].dtype),
                pltpu.SemaphoreType.DMA((count,)),
                pltpu.SemaphoreType.DMA((count,)),
            ],
        ),
        compiler_params=pltpu.CompilerParams(vmem_limit_bytes=total * wide * 2 + 4 * 2**20),
        name="place",
    )(to_rows, *arrays)


def to_ring(table):
    size = lax.axis_size("seq")
    me = lax.axis_index("seq")
    return jnp.stack(
        [lax.dynamic_index_in_dim(table, (me - k) % size, 0, keepdims=False) for k in range(size)]
    )


def head_of(rank, place):
    groups, ranks = lax.axis_size("dp"), lax.axis_size("seq")
    blocks = groups * ranks // HEADS
    if blocks <= ranks:
        held = groups // blocks
        return (rank % blocks * held + place) * (ranks // blocks) + rank // blocks
    return place * ranks + rank


def heads_of():
    ranks = lax.axis_size("seq")
    return [[head_of(rank, place) for place in range(HEADS // ranks)] for rank in range(ranks)]


def head_pieces(rank, place):
    held = HEADS // lax.axis_size("seq")
    return place // held * HEADS + head_of(rank, place % held)


def hidden_pieces(rank, place):
    return place * lax.axis_size("seq") + rank


def own_heads():
    numbers = jnp.array(heads_of())
    mine = lax.dynamic_index_in_dim(numbers, lax.axis_index("seq"), 0, keepdims=False)
    return (mine[:, None] == jnp.arange(HEADS)[None, :]).astype(WIDE)


def exact(left, right):
    return jnp.dot(left, right, precision=lax.Precision.HIGHEST, preferred_element_type=WIDE)


def out_route():
    groups, ranks = lax.axis_size("dp"), lax.axis_size("seq")
    blocks = groups * ranks // HEADS
    route = []
    for group in range(groups):
        for rank in range(ranks):
            if blocks <= ranks:
                held = groups // blocks
                high, low = divmod(group, held)
                pair, part = divmod(rank, blocks)
                target = (part * held + low, pair * blocks + high)
            else:
                span = blocks // ranks
                head, extra = divmod(group, span)
                high, low = divmod(head, ranks)
                target = ((high * ranks + rank) * span + extra, low)
            route.append((group * ranks + rank, target[0] * ranks + target[1]))
    return route


def out_parts():
    groups, ranks = lax.axis_size("dp"), lax.axis_size("seq")
    blocks = groups * ranks // HEADS
    if blocks <= ranks:
        return ((blocks, groups // blocks), (1, 0))
    return ((HEADS // ranks, ranks, blocks // ranks), (0, 2, 1))


def out_rows(table, rows):
    split, order = out_parts()
    ranks = lax.axis_size("seq")
    width = table.shape[1]
    whole = table.reshape(split + (ranks, rows, width))
    at = len(split)
    return whole.transpose(order + (at + 1, at, at + 2)).reshape(-1, ranks * width)


def gather_groups(block):
    return lax.all_gather(block, "dp", axis=0, tiled=True)


def swap_bit(block, axis, bit):
    return lax.ppermute(
        block, axis, [(place, place ^ (1 << bit)) for place in range(lax.axis_size(axis))]
    )


def bits_of(axis):
    return range(lax.axis_size(axis).bit_length() - 1)


def pair_kernel(lefts, rights, rows, kept, me_ref, *refs):
    left_refs, right_refs, rest = refs[:lefts], refs[lefts : lefts + rights], refs[lefts + rights :]
    side = lax.rem(me_ref[0], 2)
    blocks = []
    for number in range(left_refs[0].shape[1] // rows // 2):
        group = (me_ref[0] // 2 ^ number) * 2 + (side if kept else 1 - side)
        columns = pl.ds(pl.multiple_of(group * rows, rows), rows)
        blocks.append(jnp.concatenate([ref[:, columns] for ref in left_refs]))
    left, right = jnp.concatenate(blocks, axis=1), joined(right_refs)
    total = lax.dot_general(left, right, (((0,), (0,)), ((), ())), preferred_element_type=WIDE)
    if not kept:
        rest[0][...] = total.astype(LOW)
        return
    half = total.shape[1] // 2
    for number in range(len(blocks)):
        part = slice(number * rows, (number + 1) * rows)
        low = (total[part] + rest[0][part, :].astype(WIDE)).astype(LOW)
        rest[1 + number][...] = low[:, :half]
        rest[1 + len(blocks) + number][...] = low[:, half:]


def pair_product(lefts, rights, rows, got=None):
    groups, me = lax.axis_size("dp"), lax.axis_index("dp")
    pairs, width = groups // 2, rights[0].shape[1]
    kept = got is not None
    operands = [*lefts, *rights, *([got] if kept else [])]
    if kept:
        out_shape = [pltpu.HBM((rows, width // 2), LOW)] * (2 * pairs)
    else:
        out_shape = [pltpu.HBM((pairs * rows, width), LOW)]
    results = pl.pallas_call(
        partial(pair_kernel, len(lefts), len(rights), rows, kept),
        out_shape=out_shape,
        grid_spec=pltpu.PrefetchScalarGridSpec(
            num_scalar_prefetch=1,
            grid=(1,),
            in_specs=[whole_block(array) for array in operands],
            out_specs=[whole_block(result) for result in out_shape],
        ),
        compiler_params=pltpu.CompilerParams(vmem_limit_bytes=48 * 2**20),
        cost_estimate=SMALL,
        name="pair_product",
    )(me[None], *operands)
    return list(results) if kept else results[0]


GELU_SCALE = (2 / jnp.pi) ** 0.5
GELU_CUBE = 0.044715


def gelu_parts(value):
    square = value * value
    bent = jnp.tanh(GELU_SCALE * value * (1 + GELU_CUBE * square))
    slope = 0.5 * (1 + bent) + 0.5 * value * (1 - bent * bent) * GELU_SCALE * (
        1 + 3 * GELU_CUBE * square
    )
    return 0.5 * value * (1 + bent), slope


def joined(refs):
    return jnp.concatenate([ref[...] for ref in refs])


CHUNK = 256


def stream_kernel(work, inputs, results, *refs):
    weight_ref, operands = refs[0], refs[1 : 1 + inputs]
    result_refs, (held, sem, *total) = refs[1 + inputs : 1 + inputs + results], refs[1 + inputs + results :]
    copies = []
    for number in range(held.shape[1] // CHUNK):
        part = pl.ds(number * CHUNK, CHUNK)
        copies.append(
            pltpu.make_async_copy(weight_ref.at[:, part], held.at[:, part], sem.at[number])
        )
    for copy in copies:
        copy.start()
    for number, copy in enumerate(copies):
        copy.wait()
        columns = slice(number * CHUNK, (number + 1) * CHUNK)
        work(number, columns, held[:, columns], operands, result_refs, *total)


def stream(name, work, weight, extent, operands, results, total=None):
    shape = (weight.shape[0], extent)
    scratch = [pltpu.VMEM(shape, weight.dtype), pltpu.SemaphoreType.DMA((extent // CHUNK,))]
    if total is not None:
        scratch.append(pltpu.VMEM(total, WIDE))
    return pl.pallas_call(
        partial(stream_kernel, work, len(operands), len(results)),
        out_shape=results,
        grid=(1,),
        in_specs=[pl.BlockSpec(memory_space=pl.ANY)]
        + [pl.BlockSpec(array.shape, lambda number: (0, 0)) for array in operands],
        out_specs=[pl.BlockSpec(result.shape, lambda number: (0, 0)) for result in results],
        scratch_shapes=scratch,
        compiler_params=pltpu.CompilerParams(vmem_limit_bytes=32 * 2**20),
        cost_estimate=pl.CostEstimate(
            flops=2 * operands[0].shape[0] * shape[0] * shape[1],
            bytes_accessed=2 * shape[0] * shape[1],
            transcendentals=0,
        ),
        name=name,
    )(pltpu.with_memory_space_constraint(weight, pltpu.HBM), *operands)


def column_block(rows, wide):
    return pl.BlockSpec((rows, wide), lambda number: (0, number))


def project_kernel(left_ref, weight_ref, bias_ref, to_ref):
    total = jnp.dot(left_ref[...], weight_ref[...], preferred_element_type=WIDE)
    to_ref[...] = (total + bias_ref[...]).astype(to_ref.dtype)


def project(left, weight, bias):
    (rows, depth), width = left.shape, bias.shape[0]
    return pl.pallas_call(
        project_kernel,
        out_shape=jax.ShapeDtypeStruct((rows, width), LOW),
        grid=(width // CHUNK,),
        in_specs=[whole_block(left), column_block(depth, CHUNK), column_block(1, CHUNK)],
        out_specs=column_block(rows, CHUNK),
        compiler_params=pltpu.CompilerParams(vmem_limit_bytes=16 * 2**20),
        name="project",
    )(left, pltpu.with_memory_space_constraint(weight, pltpu.HBM), bias[None])


def upward_product(lefts, weight, bias):
    def work(number, columns, chunk, operands, results):
        total = jnp.dot(joined(operands[:-1]), chunk, preferred_element_type=WIDE)
        total = total + operands[-1][:, columns]
        results[0][:, columns] = total
        results[1][:, columns] = gelu_parts(total)[0].astype(LOW)

    rows, width = sum(left.shape[0] for left in lefts), weight.shape[1]
    results = [jax.ShapeDtypeStruct((rows, width), kind) for kind in (WIDE, LOW)]
    return stream("upward_product", work, weight, width, [*lefts, bias[None]], results)


def dense_kernel(lefts, *refs):
    weight_ref, reward_ref, reward_to_ref = refs[lefts], refs[lefts + 1], refs[-1]
    total = jnp.dot(joined(refs[:lefts]), weight_ref[...], preferred_element_type=WIDE)
    row = 0
    for to_ref in refs[lefts + 2 : -1]:
        to_ref[...] = total[row : row + to_ref.shape[0]].astype(LOW)
        row += to_ref.shape[0]
    scaled = total * reward_ref[...]
    part = scaled[:, :128]
    for start in range(128, scaled.shape[1], 128):
        part = part + scaled[:, start : start + 128]

    @pl.when(pl.program_id(0) == 0)
    def _():
        reward_to_ref[...] = part

    @pl.when(pl.program_id(0) > 0)
    def _():
        reward_to_ref[...] += part


def dense_product(lefts, weight, reward):
    depth, width = weight.shape
    rows = sum(left.shape[0] for left in lefts)
    return pl.pallas_call(
        partial(dense_kernel, len(lefts)),
        out_shape=[jax.ShapeDtypeStruct((left.shape[0], width), LOW) for left in lefts]
        + [jax.ShapeDtypeStruct((rows, 128), WIDE)],
        grid=(width // CHUNK,),
        in_specs=[whole_block(left) for left in lefts]
        + [column_block(depth, CHUNK), column_block(1, CHUNK)],
        out_specs=[column_block(left.shape[0], CHUNK) for left in lefts]
        + [pl.BlockSpec((rows, 128), lambda number: (0, 0))],
        compiler_params=pltpu.CompilerParams(vmem_limit_bytes=16 * 2**20),
        name="dense_product",
    )(*lefts, weight, reward[None])


def against_dot(left, weight):
    return lax.dot_general(left, weight, (((1,), (1,)), ((), ())), preferred_element_type=WIDE)


def against_stream(name, lefts, weight, operands, results, finish):
    rows, depth = sum(left.shape[0] for left in lefts), lefts[0].shape[1]

    def work(number, columns, chunk, operand_refs, result_refs, total):
        left = jnp.concatenate([ref[:, columns] for ref in operand_refs[: len(lefts)]])
        part = against_dot(left, chunk)
        total[...] = part if number == 0 else total[...] + part
        if number == depth // CHUNK - 1:
            finish(total, operand_refs[len(lefts) :], result_refs)

    shape = (rows, weight.shape[0])
    return stream(name, work, weight, depth, [*lefts, *operands], results, shape)


def column_sums(*values):
    sums = [jnp.sum(value, axis=0, keepdims=True) for value in values]
    return jnp.concatenate(sums + [jnp.zeros((8 - len(sums), sums[0].shape[1]), WIDE)])


def by_chunk(width):
    return [slice(start, start + CHUNK) for start in range(0, width, CHUNK)]


def second_kernel(down_ref, up_ref, left_ref, upward_ref, term_ref, low_ref, sums_ref, *scratch):
    down, up, down_sem, up_sem, total = scratch
    width = down.shape[1]
    copies = [
        [
            pltpu.make_async_copy(source.at[:, columns], held.at[:, columns], sem.at[number])
            for number, columns in enumerate(pl.ds(start, CHUNK) for start in range(0, width, CHUNK))
        ]
        for source, held, sem in ((down_ref, down, down_sem), (up_ref, up, up_sem))
    ]
    for copy in copies[0] + copies[1]:
        copy.start()
    for number, columns in enumerate(by_chunk(width)):
        copies[0][number].wait()
        part = against_dot(left_ref[:, columns], down[:, columns])
        total[...] = part if number == 0 else total[...] + part
    for number, columns in enumerate(by_chunk(width)):
        slope = gelu_parts(upward_ref[:, columns])[1]
        low = (total[:, columns] * slope).astype(LOW)
        low_ref[:, columns] = low
        sums_ref[:, columns] = column_sums(low.astype(WIDE))
        copies[1][number].wait()
        part = against_dot(low, up[:, columns])
        term_ref[...] = part if number == 0 else term_ref[...] + part


def second_product(left, weight_down, weight_up, upward):
    rows, width = upward.shape
    chunks = width // CHUNK
    results = [
        jax.ShapeDtypeStruct((rows, width), WIDE),
        jax.ShapeDtypeStruct((rows, width), LOW),
        jax.ShapeDtypeStruct((8, width), WIDE),
    ]
    return pl.pallas_call(
        second_kernel,
        out_shape=results,
        grid=(1,),
        in_specs=[pl.BlockSpec(memory_space=pl.ANY)] * 2
        + [pl.BlockSpec(array.shape, lambda number: (0, 0)) for array in (left, upward)],
        out_specs=[pl.BlockSpec(result.shape, lambda number: (0, 0)) for result in results],
        scratch_shapes=[pltpu.VMEM(weight.shape, LOW) for weight in (weight_down, weight_up)]
        + [pltpu.SemaphoreType.DMA((chunks,))] * 2
        + [pltpu.VMEM((rows, width), WIDE)],
        compiler_params=pltpu.CompilerParams(vmem_limit_bytes=48 * 2**20),
        cost_estimate=pl.CostEstimate(
            flops=4 * rows * width * width, bytes_accessed=4 * width * width, transcendentals=0
        ),
        name="second_product",
    )(
        *(pltpu.with_memory_space_constraint(weight, pltpu.HBM) for weight in (weight_down, weight_up)),
        left,
        upward,
    )


def against(lefts, weight, kind=WIDE):
    def finish(total, operands, results):
        results[0][...] = total[...].astype(kind)

    rows = sum(left.shape[0] for left in lefts)
    result = jax.ShapeDtypeStruct((rows, weight.shape[0]), kind)
    return against_stream("against", lefts, weight, [], [result], finish)[0]


def against_sums(left, weight, normal):
    def finish(total, operands, results):
        for columns in by_chunk(normal.shape[1]):
            value = total[:, columns]
            results[0][:, columns] = value
            results[1][:, columns] = column_sums(value * operands[0][:, columns], value)

    rows, width = normal.shape
    results = [jax.ShapeDtypeStruct((rows, width), WIDE), jax.ShapeDtypeStruct((8, width), WIDE)]
    return against_stream("against_sums", [left], weight, [normal], results, finish)


def masked_scores(query, key, queried_ref, keyed_ref, scale):
    scores = against_dot(query, key) * scale
    segment, place = queried_ref[:, 0:1], queried_ref[:, 1:2]
    other, before = keyed_ref[0:1, :], keyed_ref[1:2, :]
    allowed = ((other == 0) | (other == segment)) & (before <= place)
    return jnp.where(allowed, scores, MASKED)


def attend_kernel(scale, query_ref, key_ref, value_ref, queried_ref, keyed_ref, to_ref, log_ref):
    scores = masked_scores(query_ref[...], key_ref[...], queried_ref, keyed_ref, scale)
    highest = jnp.max(scores, axis=1, keepdims=True)
    exponent = jnp.exp(scores - highest)
    totals = jnp.sum(exponent, axis=1, keepdims=True)
    chances = (exponent / totals).astype(LOW)
    to_ref[...] = jnp.dot(chances, value_ref[...], preferred_element_type=WIDE).astype(LOW)
    log_ref[0] = highest + jnp.log(totals)


def head_blocks(length, wide, count):
    return [
        pl.BlockSpec((length, wide), lambda head, which=which: (0, which * count + head))
        for which in range(3)
    ]


def attend(projected, queried, keyed, wide, scale):
    length, columns = projected.shape
    count = columns // 3 // wide
    return pl.pallas_call(
        partial(attend_kernel, scale),
        out_shape=[
            jax.ShapeDtypeStruct((length, columns // 3), LOW),
            jax.ShapeDtypeStruct((count, length, 1), WIDE),
        ],
        grid=(count,),
        in_specs=head_blocks(length, wide, count)
        + [
            pl.BlockSpec((length, 2), lambda head: (0, 0)),
            pl.BlockSpec((2, length), lambda head: (0, 0)),
        ],
        out_specs=[
            pl.BlockSpec((length, wide), lambda head: (0, head)),
            pl.BlockSpec((1, length, 1), lambda head: (head, 0, 0)),
        ],
        compiler_params=pltpu.CompilerParams(vmem_limit_bytes=24 * 2**20),
        name="attend",
    )(projected, projected, projected, queried, keyed)


def attend_back_kernel(
    scale,
    count,
    query_ref,
    key_ref,
    value_ref,
    queried_ref,
    keyed_ref,
    log_ref,
    grad_ref,
    to_ref,
    sums_ref,
):
    query, key, grad = query_ref[...], key_ref[...], grad_ref[...]
    wide = query.shape[1]
    scores = masked_scores(query, key, queried_ref, keyed_ref, scale)
    chances = jnp.exp(scores - log_ref[0])
    chance_grad = against_dot(grad, value_ref[...])
    weighted = jnp.sum(chances * chance_grad, axis=1, keepdims=True)
    score_grad = (chances * (chance_grad - weighted)).astype(LOW)

    def across(left, right):
        return lax.dot_general(left, right, (((0,), (0,)), ((), ())), preferred_element_type=WIDE)

    grads = (
        jnp.dot(score_grad, key, preferred_element_type=WIDE) * scale,
        across(score_grad, query) * scale,
        across(chances.astype(LOW), grad),
    )
    for which, value in enumerate(grads):
        low = value.astype(LOW)
        start = pl.multiple_of((which * count + pl.program_id(0)) * wide, wide)
        to_ref[:, pl.ds(start, wide)] = low
        sums_ref[:, pl.ds(start, wide)] = column_sums(low.astype(WIDE))


def attend_back(projected, queried, keyed, log_rows, grad, wide, scale):
    length, columns = projected.shape
    count = columns // 3 // wide
    return pl.pallas_call(
        partial(attend_back_kernel, scale, count),
        out_shape=[
            jax.ShapeDtypeStruct((length, columns), LOW),
            jax.ShapeDtypeStruct((8, columns), WIDE),
        ],
        grid=(count,),
        in_specs=head_blocks(length, wide, count)
        + [
            pl.BlockSpec((length, 2), lambda head: (0, 0)),
            pl.BlockSpec((2, length), lambda head: (0, 0)),
            pl.BlockSpec((1, length, 1), lambda head: (head, 0, 0)),
            pl.BlockSpec((length, wide), lambda head: (0, head)),
        ],
        out_specs=[
            pl.BlockSpec((length, columns), lambda head: (0, 0)),
            pl.BlockSpec((8, columns), lambda head: (0, 0)),
        ],
        compiler_params=pltpu.CompilerParams(vmem_limit_bytes=32 * 2**20),
        name="attend_back",
    )(projected, projected, projected, queried, keyed, log_rows, grad)


SMALL = pl.CostEstimate(flops=1 << 30, bytes_accessed=1 << 22, transcendentals=0)


def whole_block(array):
    return pl.BlockSpec(array.shape, lambda *_: (0, 0), pipeline_mode=pl.Buffered(1))


def rows_kernel(lefts, *refs):
    left, right = joined(refs[:lefts]), joined(refs[lefts:-1])
    total = lax.dot_general(left, right, (((0,), (0,)), ((), ())), preferred_element_type=WIDE)
    refs[-1][...] = total.astype(LOW)


def rows_product(lefts, rights):
    rows, width = lefts[0].shape[1], rights[0].shape[1]
    wide = 512
    if rows % wide:
        return inner_rows(jnp.concatenate(lefts), jnp.concatenate(rights)).astype(LOW)
    return pl.pallas_call(
        partial(rows_kernel, len(lefts)),
        out_shape=pltpu.HBM((rows, width), LOW),
        grid=(rows // wide,),
        in_specs=[pl.BlockSpec((left.shape[0], wide), lambda number: (0, number)) for left in lefts]
        + [
            pl.BlockSpec(right.shape, lambda number: (0, 0), pipeline_mode=pl.Buffered(1))
            for right in rights
        ],
        out_specs=pl.BlockSpec((wide, width), lambda number: (number, 0)),
        compiler_params=pltpu.CompilerParams(vmem_limit_bytes=32 * 2**20),
        cost_estimate=pl.CostEstimate(
            flops=4 * rows * width * sum(left.shape[0] for left in lefts),
            bytes_accessed=4 * rows * width,
            transcendentals=0,
        ),
        name="rows_product",
    )(*lefts, *rights)


def scatter_product(lefts, rights):
    return scatter_groups(rows_product(lefts, rights))


def scatter_groups(table):
    return lax.psum_scatter(table, "dp", scatter_dimension=0, tiled=True)


def out_columns(left, rows):
    split, order = out_parts()
    count = left.shape[0]
    back = tuple(1 + order.index(axis) for axis in range(len(order)))
    moved = left.reshape((count,) + tuple(split[axis] for axis in order) + (rows,))
    return moved.transpose((0,) + back + (1 + len(split),)).reshape(count, -1)


def pair_onward(pieces):
    return [swap_bit(pieces[3], "dp", 1), swap_bit(pieces[7], "dp", 2)]


def sums_kernel(counts, *refs):
    at = 0
    for count, to_ref in zip(counts, refs[sum(counts) :]):
        total = refs[at][...].astype(WIDE)
        for ref in refs[at + 1 : at + count]:
            total = total + ref[...].astype(WIDE)
        to_ref[...] = total.astype(LOW)
        at += count


def sums_of(*groups):
    rows, width = groups[0][0].shape
    block = pl.BlockSpec((rows // 2, width), lambda number: (number, 0))
    return pl.pallas_call(
        partial(sums_kernel, [len(group) for group in groups]),
        out_shape=[jax.ShapeDtypeStruct((rows, width), LOW)] * len(groups),
        grid=(2,),
        in_specs=[block] * sum(len(group) for group in groups),
        out_specs=[block] * len(groups),
        cost_estimate=SMALL,
        name="sums_of",
    )(*(array for group in groups for array in group))


def pair_second(pieces, onward):
    return sums_of([pieces[2], onward[0]], [pieces[5], onward[1]])


def pair_last(sent):
    return [swap_bit(sent[0], "dp", 2), swap_bit(sent[1], "dp", 1)]


def pair_staying(pieces):
    return [swap_bit(pieces[1], "dp", 1), swap_bit(pieces[6], "dp", 2)]


def pair_sum(pieces, staying, second):
    groups = zip((pieces[0], pieces[4]), staying, second)
    return jnp.concatenate(sums_of(*(list(group) for group in groups)), axis=1)


def rank_rows(table, rows):
    ranks, me = lax.axis_size("seq"), lax.axis_index("seq")
    return [
        lax.dynamic_slice_in_dim(table, (me + shift) % ranks * rows, rows, 0)
        for shift in range(ranks)
    ]


def swap_rank(block, shift):
    size = lax.axis_size("seq")
    return lax.ppermute(block, "seq", [(place, (place + shift) % size) for place in range(size)])


def swap_ranks(blocks):
    return [blocks[0]] + [swap_rank(blocks[shift], shift) for shift in range(1, len(blocks))]


def rows_by_rank(blocks, beside=None):
    ranks, me = len(blocks), lax.axis_index("seq")
    rows, width = blocks[0].shape
    sources = [(number, 0, rows, 0, width, 0) for number in range(ranks)]
    to_rows = [(me + ranks - number) % ranks * rows for number in range(ranks)]
    arrays, more = list(blocks), 0
    if beside is not None:
        more = beside.shape[1] // ranks
        sources += [(ranks, 0, rows, number * more, more, width) for number in range(ranks)]
        to_rows += [number * rows for number in range(ranks)]
        arrays.append(beside)
    return place(arrays, sources, jnp.stack([jnp.int32(row) for row in to_rows]), (ranks * rows, width + more))


def by_number(blocks):
    return to_ring(jnp.stack(blocks))


def small_order():
    groups, ranks = lax.axis_size("dp"), lax.axis_size("seq")
    number = jnp.arange(groups * ranks)
    place = ((number // ranks) ^ lax.axis_index("dp")) * ranks + (
        (number % ranks) ^ lax.axis_index("seq")
    )
    return (place[:, None] == number[None, :]).astype(WIDE)


def small_groups(table):
    for bit in reversed(bits_of("dp")):
        half = table.shape[0] // 2
        table = table[:half] + swap_bit(table[half:], "dp", bit)
    return table


def small_ranks(table):
    size, me = lax.axis_size("seq"), lax.axis_index("seq")
    total = table[0]
    for shift in range(1, size):
        sent = lax.dynamic_index_in_dim(table, me ^ ((me + shift) % size), 0, keepdims=True)
        perm = [(place, (place + shift) % size) for place in range(size)]
        total = total + lax.ppermute(sent, "seq", perm)[0]
    return total


def small_rows(table):
    return jnp.dot(
        small_order().T, table, precision=lax.Precision.HIGHEST, preferred_element_type=WIDE
    )


def sum_ranks(table):
    size = lax.axis_size("seq")
    total = table
    for shift in range(1, size):
        total = total + lax.ppermute(
            table, "seq", [(place, (place + shift) % size) for place in range(size)]
        )
    return total


def spread_path(
    inputs,
    cotangent,
    segments,
    labels,
    step_ends,
    attend_gain,
    attend_shift,
    project_in,
    project_bias,
    project_out,
    output_bias,
    dense_gain,
    dense_shift,
    up_weight,
    up_bias,
    down_weight,
    down_bias,
    reward_weight,
):
    groups, ranks = lax.axis_size("dp"), lax.axis_size("seq")
    rank = lax.axis_index("seq")
    rows_here, places_here, width = inputs.shape
    all_rows = rows_here * groups
    head_width = width // HEADS
    heads_here = HEADS // ranks
    share = heads_here * head_width
    rows_in = project_in.shape[0]
    hidden_here = down_weight.shape[0]
    length = ranks * places_here
    score_scale = head_width ** (-0.5)

    small = (
        attend_gain,
        attend_shift,
        project_bias,
        output_bias,
        dense_gain,
        dense_shift,
        up_bias,
        down_bias,
        reward_weight,
    )
    sizes = [vector.shape[0] for vector in small]
    riders = [vector.reshape(-(-vector.shape[0] // 128), -1) for vector in small]
    riders += [segments, labels, step_ends]
    dealt_in = deal(project_in, head_pieces, head_width, riders)
    came_in = swap_ranks(dealt_in)
    out_moved = lax.ppermute(after(project_out, dealt_in), EVERY, out_route())
    rows_in_all = rows_by_rank(came_in, out_moved)
    gathered = gather_groups(rows_in_all)
    inputs_ring = ring_gather(
        after(inputs[0], came_in), [idle, idle, idle]
    )
    first_normals = []
    for halves in inputs_ring:
        normal, inverse = normal_parts(jnp.concatenate(halves).astype(WIDE))
        if not first_normals:
            first_inverse = inverse
        first_normals.append(normal)
    dealt_up = deal(after(up_weight, [rows_in_all]), hidden_pieces, hidden_here)
    came_up = swap_ranks(after(dealt_up, inputs_ring[-1]))
    gathered = after(gathered, first_normals)
    rows_up_all = rows_by_rank(came_up)
    weight_up = gather_groups(rows_up_all)
    weight_down = gather_groups(after(down_weight, [rows_up_all]))
    riders = gathered[:, 3 * share : 3 * share + 128]
    lines_all = sum(-(-size // 128) for size in sizes) + 3
    lines_all = -(-lines_all // 8) * 8
    riders = riders.reshape(groups * ranks, rows_in, 128)[:, :lines_all].astype(WIDE)
    vectors = []
    row = 0
    for size in sizes + [places_here] * 3:
        lines = -(-size // 128)
        vectors.append(
            riders[:, row : row + lines].reshape(groups * ranks, -1)[:, :size].reshape(-1)
        )
        row += lines
    gain_one, shift_one, bias_in, bias_out, gain_two, shift_two, bias_up, bias_down, reward_wide = (
        vectors[: len(sizes)]
    )

    held = own_heads()
    bias_heads = exact(held, bias_in.reshape(2, HEADS, head_width).transpose(1, 0, 2).reshape(HEADS, -1))
    bias_heads = bias_heads.reshape(heads_here, 2, head_width)
    bias_full = jnp.concatenate(
        [bias_heads[:, 0].reshape(-1), jnp.zeros((share,), WIDE), bias_heads[:, 1].reshape(-1)]
    )
    bias_up_here = lax.dynamic_index_in_dim(
        bias_up.reshape(groups, ranks, hidden_here), rank, 1, keepdims=False
    ).reshape(-1)
    marks = jnp.stack(
        [
            lax.dynamic_index_in_dim(
                mark.reshape(groups, ranks, places_here), lax.axis_index("dp"), 0, keepdims=False
            )
            for mark in vectors[len(sizes) :]
        ],
        axis=1,
    )
    marks_ring = to_ring(marks)
    segments_ring = marks_ring[:, 0].reshape(-1)
    places_ring = to_ring(jnp.arange(length).reshape(ranks, places_here)).reshape(-1)

    own = inputs[0].astype(WIDE)
    firsts = [(normal * gain_one + shift_one).astype(LOW) for normal in first_normals]
    projected = project(jnp.concatenate(firsts), gathered, bias_full)
    gathered, projected = lax.optimization_barrier((gathered, projected))
    weight_out = out_rows(gathered[:, 3 * share + 128 :], rows_in)
    queried, keyed = (
        jnp.stack([segments_ring.astype(WIDE), places_ring.astype(WIDE)], axis=axis)
        for axis in (1, 0)
    )
    mixture, log_rows = attend(projected, queried, keyed, head_width, score_scale)

    def block_of(array, k):
        return array[k * places_here : (k + 1) * places_here]

    weight_back = None

    def contiguous(gate):
        nonlocal weight_back
        weight_back = after(gathered, gate)[:, : 3 * share]
        return [weight_back]

    mixture_out = None

    def in_blocks(gate):
        nonlocal mixture_out
        mixture_out = out_columns(after(mixture, gate), project_out.shape[0])
        return [mixture_out]

    branch = ring_sum(
        lambda k, gate: product(block_of(mixture, k), weight_out), [contiguous, in_blocks, idle]
    )
    weight_back, mixture_out = lax.optimization_barrier((weight_back, mixture_out))
    hidden = own + branch + bias_out

    second_normal, second_inverse = normal_parts(hidden)
    second_value = second_normal * gain_two + shift_two

    rows_all = ranks * rows_in
    fenced = groups == 8 and rows_all % 128 == 0
    steady = (segments[0, 0] | 1) != 0

    def step(work, *operands):
        return fence(steady, work, *operands) if fenced else work(*operands)

    def upward_of(k, halves):
        return upward_product(halves, weight_up, bias_up_here)

    seconds, found = ring_gather(second_value.astype(LOW), use=upward_of, plan=(1, 1, 1))

    def dense_one(halves, block):
        return upward_of(None, halves), ring_move([block])[0]

    def dense_two(activated, block):
        return dense_product(activated, weight_down, reward_wide), ring_move([block])[0]

    cotangents = [cotangent[0]]
    last, block = step(dense_one, seconds[-1], cotangents[-1])
    cotangents.append(block)
    upwards, activated = map(list, zip(*found, last))
    (*dense_parts, reward_lanes), block = step(dense_two, activated, cotangents[-1])
    cotangents.append(block)
    dense_parts = lax.optimization_barrier(dense_parts)
    reward_parts = list(jnp.sum(reward_lanes, axis=-1).reshape(ranks, places_here))

    reward_parts[0] = reward_parts[0] + jnp.sum((hidden + bias_down) * reward_wide, axis=-1)
    rewards_all = sum_ranks(to_ring(jnp.stack(reward_parts)))
    scored = marks[:, 2] * (marks[:, 0] > 0)
    error_all = scored * (jax.nn.sigmoid(rewards_all) - marks[:, 1]) / all_rows
    error_ring = to_ring(error_all)
    rewards = lax.dynamic_index_in_dim(rewards_all, rank, 0, keepdims=False)

    def dense_grad(block, k):
        return block.astype(WIDE) + error_ring[k][:, None] * reward_wide

    dense_lows = [dense_grad(block, k).astype(LOW) for k, block in enumerate(cotangents)]

    def second_part(k, dense_low):
        term, *low = second_product(dense_low, weight_down, weight_up, upwards[k])
        return term, tuple(low)

    def second_first(block, dense_low):
        term, upward_low = second_part(1, dense_low)
        return term.astype(LOW), upward_low, ring_move([block])[0]

    def second_step(k, sent, dense_low):
        moved = ring_move([sent])[0]
        term, upward_low = second_part(k, dense_low)
        total = moved.astype(WIDE) + term
        return total if k == 0 else total.astype(LOW), upward_low

    upward_lows = [None] * ranks
    sent, upward_lows[1], block = step(second_first, cotangents[-1], dense_lows[1])

    def second_next(sent, block):
        dense_low = dense_grad(block, ranks - 1).astype(LOW)
        table = rows_product(activated, [*dense_lows, dense_low])
        return second_step(2, sent, dense_lows[2]), dense_low, table

    (sent, upward_lows[2]), dense_low, down_table = step(second_next, sent, block)
    dense_lows.append(dense_low)
    down_summed = scatter_groups(down_table)
    for k in list(range(3, ranks)) + [0]:
        sent, upward_lows[k] = step(partial(second_step, k), sent, dense_lows[k])
    second_grad = sent
    result_grad = after(dense_grad(cotangents[0], 0), [sent])
    upward_lows, upward_sums = zip(*upward_lows)
    reward_weight_gradient = jnp.sum(error_ring[0][:, None] * (hidden + bias_down), axis=0)
    for k, part in enumerate(dense_parts):
        reward_weight_gradient += jnp.sum(error_ring[k][:, None] * part.astype(WIDE), axis=0)
    down_bias_gradient = jnp.sum(dense_lows[0].astype(WIDE), axis=0)
    up_bias_gradient = sum(upward_sums)[0]
    dense_gain_gradient = jnp.sum(second_grad * second_normal, axis=0)
    dense_shift_gradient = jnp.sum(second_grad, axis=0)
    hidden_grad = result_grad + normalize_back(second_grad, second_normal, second_inverse, gain_two)

    branch_low = hidden_grad.astype(LOW)
    seconds = sum(seconds, [])
    output_bias_gradient = jnp.sum(branch_low.astype(WIDE), axis=0)

    def by_device(vectors):
        return jnp.concatenate([vector.reshape(groups * ranks, -1) for vector in vectors], axis=1)

    def early_table():
        up_bias_all = lax.dynamic_update_index_in_dim(
            jnp.zeros((groups, ranks, hidden_here), WIDE),
            up_bias_gradient.reshape(groups, hidden_here),
            rank,
            1,
        )
        return by_device(
            (
                output_bias_gradient,
                dense_gain_gradient,
                dense_shift_gradient,
                up_bias_all,
                down_bias_gradient,
                reward_weight_gradient,
            )
        )

    def back(mixture_grad):
        return attend_back(
            projected, queried, keyed, log_rows, mixture_grad, head_width, score_scale
        )

    def first_part(projected_grad, k):
        return against_sums(block_of(projected_grad, k), weight_back, first_normals[k])

    def inputs_back(first_grad):
        return hidden_grad + normalize_back(
            first_grad, first_normals[0], first_inverse, gain_one
        )

    def small_table(bias_sums, first_sums, early):
        bias_heads = jnp.concatenate([bias_sums[0, :share], bias_sums[0, 2 * share :]])
        bias_heads = bias_heads.reshape(2, heads_here, head_width)
        bias_all = jnp.concatenate(
            [exact(held.T, bias_heads[which]).reshape(-1) for which in range(2)]
        )
        gain_sum, shift_sum = sum(first_sums)[:2]
        return jnp.concatenate([by_device((gain_sum, shift_sum, bias_all)), early], axis=1)

    def out_back(out_summed):
        back = [(there, here) for here, there in out_route()]
        return lax.ppermute(out_summed, EVERY, back).astype(WIDE)

    def result_back(dense_sum):
        return (hidden + dense_sum + bias_down).astype(LOW)

    def sent_rows(summed):
        return rank_rows(summed.astype(LOW), rows_in)

    if fenced:

        def gather_one(block):
            return ring_move([block])[0], pair_product(seconds, upward_lows, rows_all)

        def gather_two(block, up_sent):
            return ring_move([block])[0], swap_bit(up_sent, "dp", 0), early_table()

        def gather_three(block, up_got):
            return ring_move([block])[0], pair_product(seconds, upward_lows, rows_all, up_got)

        def attend_one(branch_lows, up_pieces):
            dense_sum = ring_step(dense_parts[1], dense_parts[2])
            up_second = pair_second(up_pieces, pair_onward(up_pieces))
            mixture_grad = against(branch_lows, weight_out, LOW)
            out_table = rows_product([mixture_out], branch_lows)
            return dense_sum, up_second, mixture_grad, out_table

        def attend_two(dense_sum, up_second, mixture_grad):
            dense_sum = ring_step(dense_sum, dense_parts[3])
            return dense_sum, pair_last(up_second), back(mixture_grad)

        def attend_three(dense_sum, up_pieces, projected_grad):
            dense_sum = ring_step(dense_sum, dense_parts[0], WIDE)
            up_staying = pair_staying(up_pieces)
            in_sent = pair_product(firsts, [projected_grad], rows_all)
            term, sums = first_part(projected_grad, 1)
            return result_back(dense_sum), up_staying, in_sent, term.astype(LOW), sums

        def first_one(sent, in_sent, projected_grad, up_pieces, up_staying, up_second):
            moved = ring_move([sent])[0]
            in_got = swap_bit(in_sent, "dp", 0)
            term, sums = first_part(projected_grad, 2)
            up_sent = sent_rows(pair_sum(up_pieces, up_staying, up_second))
            in_pieces = list(pair_product(firsts, [projected_grad], rows_all, in_got))
            moved = after(moved, in_pieces)
            return (moved.astype(WIDE) + term).astype(LOW), in_pieces, up_sent, sums

        def first_two(sent, in_pieces, projected_grad, bias_sums, first_sums, early, up_near):
            moved = ring_move([sent])[0]
            in_staying, in_onward = pair_staying(in_pieces), pair_onward(in_pieces)
            in_second = pair_second(in_pieces, in_onward)
            up_near = swap_rank(after(up_near, in_onward[:1]), near[0])
            term, sums = first_part(projected_grad, 3)
            last_term, last_sums = first_part(projected_grad, 0)
            table = small_rows(small_table(bias_sums, [sums, last_sums, *first_sums], early))
            sent = (moved.astype(WIDE) + term).astype(LOW)
            return sent, in_staying, in_second, up_near, last_term, table

        def first_three(sent, in_pieces, in_staying, in_second, term, table, up_far):
            moved = ring_move([sent])[0]
            up_far = swap_rank(up_far, far)
            in_second = pair_last(in_second)
            summed = small_ranks(small_groups(after(table, in_second[:1])))
            in_sent = sent_rows(pair_sum(in_pieces, in_staying, in_second))
            moved, up_far = after((moved, up_far), [up_far])
            return moved.astype(WIDE) + term, in_sent, summed, up_far

        def last(in_sent, came_up, up_near, first_grad):
            for shift, block in zip(near[1:], up_near):
                came_up[shift] = swap_rank(block, shift)
            came_up = [came_up[shift] for shift in range(ranks)]
            came_in = swap_ranks(in_sent)
            first_grad, down_late = after((first_grad, down_early), [came_in[1]])
            done = inputs_back(first_grad), down_late.astype(WIDE), out_back(out_early)
            came_in, came_up, done = lax.optimization_barrier((came_in, came_up, done))
            return (
                collect(came_in, head_pieces, head_width),
                collect(came_up, hidden_pieces, hidden_here),
                *done,
            )

        branch_lows = [branch_low]
        moved, up_sent = step(gather_one, branch_low)
        branch_lows.append(moved)
        moved, up_got, early = step(gather_two, moved, up_sent)
        branch_lows.append(moved)
        moved, up_pieces = step(gather_three, moved, up_got)
        branch_lows.append(moved)
        dense_sum, up_second, mixture_grad, out_table = step(attend_one, branch_lows, up_pieces)
        out_summed = scatter_groups(out_table)
        dense_sum, up_second, (projected_grad, bias_sums) = step(
            attend_two, dense_sum, up_second, mixture_grad
        )
        result_low, up_staying, in_sent, sent, sums_one = step(
            attend_three, dense_sum, up_pieces, projected_grad
        )
        sent, down_early = after((sent, down_summed), [down_summed])
        sent, in_pieces, up_sent, sums_two = step(
            first_one, sent, in_sent, projected_grad, up_pieces, up_staying, up_second
        )
        far = ranks // 2
        near = [shift for shift in range(1, ranks) if shift != far]
        sent, in_staying, in_second, up_near, last_term, table = step(
            first_two,
            sent,
            in_pieces,
            projected_grad,
            bias_sums,
            [sums_one, sums_two],
            early,
            up_sent[near[0]],
        )
        sent, out_early = after((sent, out_summed), [out_summed])
        first_grad, in_sent, summed, up_far = step(
            first_three, sent, in_pieces, in_staying, in_second, last_term, table, up_sent[far]
        )
        came_up = {0: up_sent[0], far: up_far, near[0]: up_near}
        up_near = [up_sent[shift] for shift in near[1:]]
        (
            project_in_gradient,
            up_weight_gradient,
            inputs_gradient,
            down_weight_gradient,
            project_out_gradient,
        ) = step(last, in_sent, came_up, up_near, first_grad)
    else:
        branch_lows = sum(ring_gather(branch_low, cut=1), [])
        projected_grad, bias_sums = back(against(branch_lows, weight_out, LOW))
        out_summed = scatter_groups(rows_product([mixture_out], branch_lows))
        first_sums = [None] * ranks

        def first_term(k, gate):
            term, first_sums[k] = first_part(projected_grad, k)
            return term

        first_grad = ring_sum(first_term, cut=1)
        dense_sum = dense_parts[1]
        for part in dense_parts[2:] + dense_parts[:1]:
            dense_sum = ring_step(dense_sum, part, WIDE)
        up_summed = scatter_product(seconds, upward_lows)
        in_summed = scatter_product(firsts, [projected_grad])
        inputs_gradient, result_low = inputs_back(first_grad), result_back(dense_sum)
        table = small_rows(small_table(bias_sums, first_sums, early_table()))
        summed = small_ranks(small_groups(table))
        up_weight_gradient = collect(swap_ranks(sent_rows(up_summed)), hidden_pieces, hidden_here)
        project_in_gradient = collect(swap_ranks(sent_rows(in_summed)), head_pieces, head_width)
        project_out_gradient = out_back(out_summed)
        down_weight_gradient = down_summed.astype(WIDE)
    parts = []
    start = 0
    for size in sizes:
        parts.append(summed[start : start + size])
        start += size
    return (
        result_low[None],
        rewards[None],
        inputs_gradient[None],
        parts[0],
        parts[1],
        project_in_gradient,
        parts[2],
        project_out_gradient,
        parts[3],
        parts[4],
        parts[5],
        up_weight_gradient,
        parts[6],
        down_weight_gradient,
        parts[7],
        parts[8],
    )


def solution(mesh):
    row = P("dp", "seq")
    wide_row = P("dp", "seq", None)
    vector = P(("dp", "seq"))
    matrix = P(("dp", "seq"), None)
    in_specs = (
        wide_row,
        wide_row,
        row,
        row,
        row,
        vector,
        vector,
        matrix,
        vector,
        matrix,
        vector,
        vector,
        vector,
        matrix,
        vector,
        matrix,
        vector,
        vector,
    )
    out_specs = (
        wide_row,
        row,
        wide_row,
        vector,
        vector,
        matrix,
        vector,
        matrix,
        vector,
        vector,
        vector,
        matrix,
        vector,
        matrix,
        vector,
        vector,
    )
    return jax.shard_map(
        spread_path, mesh=mesh, in_specs=in_specs, out_specs=out_specs, check_vma=False
    )
```

profile of v0, /device:TPU:0, one launch (start us, length us, event | category | flops | bytes accessed | tf_op | source)
XLA Modules:
  0.0 539.2 jit_solution(10258836310359729934)
XLA Ops:
  11.2 4.8 collective-permute-start.42
  18.6 11.3 %collective-permute-done.42.refs_1_ = bf16[64,1664]{1,0:T(8,128)(2,1)S(1)} collective-permute-done((bf16[64,1664]{1,0:T(8,128)(2,1)}, bf16[64,1664]{1,0:T(8,128)(2,1)S(1)}, u32[]{:S(2)}, u32[]{:S(2)}) %collective-permute-start.42) | collective-permute-done | bytes 213024 | tf_op jit(solution)/shard_map/ppermute | solution.py:844
  29.9 4.4 collective-permute-done.43.refs_2_
  42.9 7.8 %collective-permute-done.46 = bf16[64,2048]{1,0:T(8,128)(2,1)S(1)} collective-permute-done((bf16[64,2048]{1,0:T(8,128)(2,1)S(1)}, bf16[64,2048]{1,0:T(8,128)(2,1)S(1)}, u32[]{:S(2)}, u32[]{:S(2)}) %collective-permute-start.46) | collective-permute-done | bytes 262176 | tf_op jit(solution)/shard_map/ppermute | solution.py:73
  51.0 5.4 %collective-permute-done.47 = bf16[64,2048]{1,0:T(8,128)(2,1)S(1)} collective-permute-done((bf16[64,2048]{1,0:T(8,128)(2,1)S(1)}, bf16[64,2048]{1,0:T(8,128)(2,1)S(1)}, u32[]{:S(2)}, u32[]{:S(2)}) %collective-permute-start.47) | collective-permute-done | bytes 262176 | tf_op jit(solution)/shard_map/ppermute | solution.py:73
  56.6 5.4 %collective-permute-done.48 = bf16[64,2048]{1,0:T(8,128)(2,1)S(1)} collective-permute-done((bf16[64,2048]{1,0:T(8,128)(2,1)S(1)}, bf16[64,2048]{1,0:T(8,128)(2,1)S(1)}, u32[]{:S(2)}, u32[]{:S(2)}) %collective-permute-start.48) | collective-permute-done | bytes 262176 | tf_op jit(solution)/shard_map/ppermute | solution.py:73
  62.2 5.4 %collective-permute-done.49 = bf16[64,2048]{1,0:T(8,128)(2,1)S(1)} collective-permute-done((bf16[64,2048]{1,0:T(8,128)(2,1)S(1)}, bf16[64,2048]{1,0:T(8,128)(2,1)S(1)}, u32[]{:S(2)}, u32[]{:S(2)}) %collective-permute-start.49) | collective-permute-done | bytes 262176 | tf_op jit(solution)/shard_map/ppermute | solution.py:73
  73.2 3.5 collective-permute-done.51
  80.7 7.4 %collective-permute-done.52.refs_1_ = bf16[64,2048]{1,0:T(8,128)(2,1)S(1)} collective-permute-done((bf16[64,2048]{1,0:T(8,128)(2,1)}, bf16[64,2048]{1,0:T(8,128)(2,1)S(1)}, u32[]{:S(2)}, u32[]{:S(2)}) %collective-permute-start.52) | collective-permute-done | bytes 262176 | tf_op jit(solution)/shard_map/ppermute | solution.py:844
  88.1 8.4 %collective-permute-done.53.refs_2_ = bf16[64,2048]{1,0:T(8,128)(2,1)S(1)} collective-permute-done((bf16[64,2048]{1,0:T(8,128)(2,1)}, bf16[64,2048]{1,0:T(8,128)(2,1)S(1)}, u32[]{:S(2)}, u32[]{:S(2)}) %collective-permute-start.53) | collective-permute-done | bytes 262176 | tf_op jit(solution)/shard_map/ppermute | solution.py:844
  112.7 6.8 %project.1.query_ref.key_ref.value_ref = bf16[512,1536]{1,0:T(8,128)(2,1)S(1)} custom-call(bf16[512,2048]{1,0:T(8,128)(2,1)S(1)} %pad_maximum_fusion.left_ref, bf16[2048,2176]{1,0:T(8,128)(2,1)} %all-gather.4.cloned.1.call-done.weight_ref, f32[1,1536]{1,0:T(1,128)S(1)} %broadcast_in_dim.65.bias_ref), custom_call_target="tpu_custom_call" | custom-call | tf_op jit(solution)/shard_map/project/pallas_call | solution.py:459
  123.3 5.8 %attend.1 = (bf16[512,512]{1,0:T(8,128)(2,1)S(1)}, f32[4,512,1]{2,1,0:T(8,128)}) custom-call(bf16[512,1536]{1,0:T(8,128)(2,1)S(1)} %project.1.query_ref.key_ref.value_ref, bf16[512,1536]{1,0:T(8,128)(2,1)S(1)} %project.1.query_ref.key_ref.value_ref, bf16[512,1536]{1,0:T(8,128)(2,1)S(1)} %project.1.query_ref.key_ref.value_ref, ...), custom_call_target="tpu_custom_call" | custom-call | tf_op jit(solution)/shard_map/attend/pallas_call | solution.py:652
  130.3 5.1 collective-permute-start.55
  157.6 4.1 collective-permute-done.59
  162.9 5.6 %collective-permute-done.57 = bf16[64,2048]{1,0:T(8,128)(2,1)S(1)} collective-permute-done((bf16[64,2048]{1,0:T(8,128)(2,1)S(1)}, bf16[64,2048]{1,0:T(8,128)(2,1)S(1)}, u32[]{:S(2)}, u32[]{:S(2)}) %collective-permute-start.57) | collective-permute-done | bytes 262176 | tf_op jit(solution)/shard_map/ppermute | solution.py:73
  174.6 6.0 %upward_product.5 = (f32[128,2048]{1,0:T(8,128)}, bf16[128,2048]{1,0:T(8,128)(2,1)}) custom-call(bf16[2048,2048]{1,0:T(8,128)(2,1)} %all-gather.6.cloned.1.call-done.refs_0_, bf16[64,2048]{1,0:T(8,128)(2,1)S(1)} %get-tuple-element.1066.refs_1_, bf16[64,2048]{1,0:T(8,128)(2,1)S(1)} %get-tuple-element.1065.refs_2_, f32[1,2048]{1,0:T(1,128)S(1)} %bitcast.178), custom_call_target="tpu_custom_call" | custom-call | flops 536870912 | bytes 8388608 | tf_op jit(solution)/shard_map/upward_product/pallas_call | solution.py:430
  180.6 4.8 collective-permute-done.62.refs_2_
  185.5 5.7 %collective-permute-done.61.refs_1_ = bf16[64,2048]{1,0:T(8,128)(2,1)} collective-permute-done((bf16[64,2048]{1,0:T(8,128)(2,1)S(1)}, bf16[64,2048]{1,0:T(8,128)(2,1)}, u32[]{:S(2)}, u32[]{:S(2)}) %collective-permute-start.61) | collective-permute-done | bytes 262176 | tf_op jit(solution)/shard_map/ppermute | solution.py:73
  191.2 7.0 %upward_product.6 = (f32[128,2048]{1,0:T(8,128)}, bf16[128,2048]{1,0:T(8,128)(2,1)}) custom-call(bf16[2048,2048]{1,0:T(8,128)(2,1)} %all-gather.6.cloned.1.call-done.refs_0_, bf16[64,2048]{1,0:T(8,128)(2,1)} %collective-permute-done.61.refs_1_, bf16[64,2048]{1,0:T(8,128)(2,1)S(1)} %collective-permute-done.62.refs_2_, f32[1,2048]{1,0:T(1,128)S(1)} %bitcast.179), custom_call_target="tpu_custom_call" | custom-call | flops 536870912 | bytes 8388608 | tf_op jit(solution)/shard_map/upward_product/pallas_call | solution.py:430
  198.2 4.1 collective-permute-done.63.refs_1_
  202.8 6.1 %upward_product.7 = (f32[128,2048]{1,0:T(8,128)}, bf16[128,2048]{1,0:T(8,128)(2,1)}) custom-call(bf16[2048,2048]{1,0:T(8,128)(2,1)} %all-gather.6.cloned.1.call-done.refs_0_, bf16[64,2048]{1,0:T(8,128)(2,1)S(1)} %collective-permute-done.63.refs_1_, bf16[64,2048]{1,0:T(8,128)(2,1)S(1)} %collective-permute-done.64.refs_2_, f32[1,2048]{1,0:T(1,128)S(1)} %bitcast.180), custom_call_target="tpu_custom_call" | custom-call | flops 536870912 | bytes 8388608 | tf_op jit(solution)/shard_map/upward_product/pallas_call | solution.py:430
  211.7 12.7 %conditional.16 = (f32[128,2048]{1,0:T(8,128)}, bf16[128,2048]{1,0:T(8,128)(2,1)}, bf16[128,2048]{1,0:T(8,128)(2,1)}) conditional(s32[]{:T(128)} %bitcast.20, () %tuple.191, (f32[8,1,256]{2,1,0:T(1,128)S(1)}, bf16[2048,2048]{1,0:T(8,128)(2,1)}, bf16[64,2048]{1,0:T(8,128)(2,1)}, bf16[64,2048]{1,0:T(8,128)(2,1)}, ...), branch_computations={%region_10.11_spmd, %region_11.12_spmd} | conditional | flops 536870912 | bytes 10485824 | solution.py:55
  211.7 7.0 %upward_product.4 = (f32[128,2048]{1,0:T(8,128)}, bf16[128,2048]{1,0:T(8,128)(2,1)}) custom-call(bf16[2048,2048]{1,0:T(8,128)(2,1)} %get-tuple-element.417.refs_0_, bf16[64,2048]{1,0:T(8,128)(2,1)} %get-tuple-element.418.refs_1_, bf16[64,2048]{1,0:T(8,128)(2,1)} %get-tuple-element.419.refs_2_, f32[1,2048]{1,0:T(1,128)S(1)} %bitcast.181), custom_call_target="tpu_custom_call" | custom-call | flops 536870912 | bytes 8388608 | tf_op jit(solution)/shard_map/cond/branch_1_fun/upward_product/pallas_call | solution.py:430
  218.7 5.6 %collective-permute-done = bf16[128,2048]{1,0:T(8,128)(2,1)} collective-permute-done((bf16[128,2048]{1,0:T(8,128)(2,1)S(1)}, bf16[128,2048]{1,0:T(8,128)(2,1)}, u32[]{:S(2)}, u32[]{:S(2)}) %collective-permute-start) | collective-permute-done | bytes 524320 | tf_op jit(solution)/shard_map/cond/branch_1_fun/ppermute | solution.py:73
  224.4 11.4 %conditional.17 = (bf16[128,2048]{1,0:T(8,128)(2,1)}, bf16[128,2048]{1,0:T(8,128)(2,1)}, bf16[128,2048]{1,0:T(8,128)(2,1)}, bf16[128,2048]{1,0:T(8,128)(2,1)}, f...) conditional(s32[]{:T(128)} %bitcast.20, () %tuple.180, (f32[32,64]{1,0:T(8,128)S(1)}, ...), branch_computations={%region_12.13_spmd, %region_13.14_spmd} | conditional | bytes 2883646 | solution.py:55
  224.4 10.6 %dense_product.1 = (bf16[128,2048]{1,0:T(8,128)(2,1)}, bf16[128,2048]{1,0:T(8,128)(2,1)}, bf16[128,2048]{1,0:T(8,128)(2,1)}, bf16[128,2048]{1,0:T(8,128)(2,1)}, f32[512,128]{1,0:T(8,128)S(1)}) custom-call(bf16[128,2048]{1,0:T(8,128)(2,1)} %get-tuple-element.424.refs_0_, bf16[128,2048]{1,0:T(8,128)(2,1)} %get-tuple-element.425.refs_1_, ...), custom_call_target="tpu_custom_call" | custom-call | tf_op jit(solution)/shard_map/cond/branch_1_fun/dense_product/pallas_call | solution.py:506
  248.6 16.7 %conditional.18 = (bf16[128,2048]{1,0:T(8,128)(2,1)}, bf16[128,2048]{1,0:T(8,128)(2,1)}, f32[8,2048]{1,0:T(8,128)}, bf16[128,2048]{1,0:T(8,128)(2,1)}) conditional(s32[]{:T(128)} %bitcast.20, () %tuple.199, (bf16[2048,2048]{1,0:T(8,128)(2,1)}, bf16[2048,2048]{1,0:T(8,128)(2,1)}, bf16[128,2048]{1,0:T(8,128)(2,1)S(1)}, f32[128,2048]{1,0:T(8,128)S(1)}, ...), branch_computations={%region_16.17_spmd, %region_17.18_spmd} | conditional | flops 2147745792 | bytes 20447304 | solution.py:55
  249.5 10.3 %second_product.4 = (f32[128,2048]{1,0:T(8,128)S(1)}, bf16[128,2048]{1,0:T(8,128)(2,1)}, f32[8,2048]{1,0:T(8,128)}) custom-call(bf16[2048,2048]{1,0:T(8,128)(2,1)} %get-tuple-element.436.down_ref, bf16[2048,2048]{1,0:T(8,128)(2,1)} %get-tuple-element.437.up_ref, bf16[128,2048]{1,0:T(8,128)(2,1)S(1)} %get-tuple-element.438.left_ref, ...), custom_call_target="tpu_custom_call" | custom-call | flops 2147483648 | bytes 16777216 | tf_op jit(solution)/shard_map/cond/branch_1_fun/second_product/pallas_call | solution.py:581
  260.6 4.5 collective-permute-done.2
  265.3 23.6 %conditional.19 = (bf16[128,2048]{1,0:T(8,128)(2,1)}, bf16[128,2048]{1,0:T(8,128)(2,1)S(1)}, f32[8,2048]{1,0:T(8,128)S(1)}, bf16[128,2048]{1,0:T(8,128)(2,1)}, bf16[2048,2048]{1,0:T(8,128)(2,1)}) conditional(s32[]{:T(128)} %bitcast.20, () %tuple.198, (bf16[128,2048]{1,0:T(8,128)(2,1)}, bf16[2048,2048]{1,0:T(8,128)(2,1)}, ...), branch_computations={%region_18.19_spmd, %region_19.20_spmd} | conditional | flops 10739253248 | bytes 53502740 | solution.py:55
  267.6 11.5 %second_product.5 = (f32[128,2048]{1,0:T(8,128)S(1)}, bf16[128,2048]{1,0:T(8,128)(2,1)S(1)}, f32[8,2048]{1,0:T(8,128)S(1)}) custom-call(bf16[2048,2048]{1,0:T(8,128)(2,1)} %get-tuple-element.445.down_ref, bf16[2048,2048]{1,0:T(8,128)(2,1)} %get-tuple-element.446.up_ref, bf16[128,2048]{1,0:T(8,128)(2,1)} %get-tuple-element.447.left_ref.refs_6_, ...), custom_call_target="tpu_custom_call" | custom-call | flops 2147483648 | bytes 16777216 | tf_op jit(solution)/shard_map/cond/branch_1_fun/second_product/pallas_call | solution.py:581
  279.1 7.8 %rows_product.2 = bf16[2048,2048]{1,0:T(8,128)(2,1)} custom-call(bf16[128,2048]{1,0:T(8,128)(2,1)S(1)} %copy-done.38, bf16[128,2048]{1,0:T(8,128)(2,1)S(1)} %copy-done.39, bf16[128,2048]{1,0:T(8,128)(2,1)S(1)} %copy-done.40, bf16[128,2048]{1,0:T(8,128)(2,1)} %get-tuple-element.458.refs_3_, bf16[128,2048]{1,0:T(8,128)(2,1)S(1)} %copy-done.29, ...), custom_call_target="tpu_custom_call" | custom-call | flops 8589934592 | bytes 16777216 | tf_op jit(solution)/shard_map/cond/branch_1_fun/rows_product/pallas_call | solution.py:753
  289.0 15.2 %conditional.20 = (bf16[128,2048]{1,0:T(8,128)(2,1)S(1)}, bf16[128,2048]{1,0:T(8,128)(2,1)}, f32[8,2048]{1,0:T(8,128)}) conditional(s32[]{:T(128)} %bitcast.20, () %tuple.197, (bf16[128,2048]{1,0:T(8,128)(2,1)}, bf16[2048,2048]{1,0:T(8,128)(2,1)}, bf16[2048,2048]{1,0:T(8,128)(2,1)}, bf16[128,2048]{1,0:T(8,128)(2,1)}, f32[128,2048]{1,0:T(8,128)}) %tuple.202), branch_computations={%region_20.21_spmd, %region_21.22_spmd} | conditional | flops 2148270080 | bytes 20971584 | solution.py:55
  290.2 12.9 %second_product.6 = (f32[128,2048]{1,0:T(8,128)S(1)}, bf16[128,2048]{1,0:T(8,128)(2,1)}, f32[8,2048]{1,0:T(8,128)}) custom-call(bf16[2048,2048]{1,0:T(8,128)(2,1)} %get-tuple-element.462.down_ref, bf16[2048,2048]{1,0:T(8,128)(2,1)} %get-tuple-element.463.up_ref, bf16[128,2048]{1,0:T(8,128)(2,1)} %get-tuple-element.464.left_ref, ...), custom_call_target="tpu_custom_call" | custom-call | flops 2147483648 | bytes 16777216 | tf_op jit(solution)/shard_map/cond/branch_1_fun/second_product/pallas_call | solution.py:581
  304.2 15.1 %conditional.21 = (f32[128,2048]{1,0:T(8,128)S(1)}, bf16[128,2048]{1,0:T(8,128)(2,1)}, f32[8,2048]{1,0:T(8,128)}, f32[2048]{0:T(1024)S(1)}) conditional(s32[]{:T(128)} %bitcast.20, () %tuple.196, (bf16[128,2048]{1,0:T(8,128)(2,1)S(1)}, bf16[2048,2048]{1,0:T(8,128)(2,1)}, bf16[2048,2048]{1,0:T(8,128)(2,1)}, bf16[128,2048]{1,0:T(8,128)(2,1)}, ...), branch_computations={%region_22.23_spmd, %region_23.25_spmd} | conditional | flops 2148268032 | bytes 21504072 | solution.py:55
  306.6 11.7 %second_product.7 = (f32[128,2048]{1,0:T(8,128)S(1)}, bf16[128,2048]{1,0:T(8,128)(2,1)}, f32[8,2048]{1,0:T(8,128)}) custom-call(bf16[2048,2048]{1,0:T(8,128)(2,1)} %get-tuple-element.470.down_ref, bf16[2048,2048]{1,0:T(8,128)(2,1)} %get-tuple-element.471.up_ref, bf16[128,2048]{1,0:T(8,128)(2,1)} %get-tuple-element.472.left_ref, ...), custom_call_target="tpu_custom_call" | custom-call | flops 2147483648 | bytes 16777216 | tf_op jit(solution)/shard_map/cond/branch_1_fun/second_product/pallas_call | solution.py:581
  323.4 11.3 %conditional.22 = (bf16[128,2048]{1,0:T(8,128)(2,1)}, bf16[1024,2048]{1,0:T(8,128)(2,1)}) conditional(s32[]{:T(128)} %bitcast.20, () %tuple.176, (bf16[128,2048]{1,0:T(8,128)(2,1)}, bf16[64,2048]{1,0:T(8,128)(2,1)}, bf16[64,2048]{1,0:T(8,128)(2,1)S(1)}, bf16[64,2048]{1,0:T(8,128)(2,1)}, bf16[64,2048]{1,0:T(8,128)(2,1)}, ...), branch_computations={%region_27.28_spmd, %region_28.29_spmd} | conditional | flops 1073741824 | bytes 6291544 | solution.py:55
  325.6 6.6 %pair_product.4 = bf16[1024,2048]{1,0:T(8,128)(2,1)} custom-call(s32[1]{0:T(128)} %bitcast.1.me_ref, bf16[64,2048]{1,0:T(8,128)(2,1)} %get-tuple-element.478.refs_0_, bf16[64,2048]{1,0:T(8,128)(2,1)S(1)} %get-tuple-element.479.refs_1_, bf16[64,2048]{1,0:T(8,128)(2,1)} %get-tuple-element.480.refs_2_, bf16[64,2048]{1,0:T(8,128)(2,1)} %get-tuple-element.481.refs_3_, ...), custom_call_target="tpu_custom_call" | custom-call | flops 1073741824 | bytes 4194304 | tf_op jit(solution)/shard_map/cond/branch_1_fun/pair_product/pallas_call | solution.py:372
  336.0 16.5 %conditional.23 = (bf16[128,2048]{1,0:T(8,128)(2,1)}, bf16[1024,2048]{1,0:T(8,128)(2,1)}, f32[32,576]{1,0:T(8,128)S(1)}) conditional(s32[]{:T(128)} %bitcast.20, () %tuple.175, (bf16[128,2048]{1,0:T(8,128)(2,1)}, bf16[1024,2048]{1,0:T(8,128)(2,1)}, f32[128,2048]{1,0:T(8,128)}, f32[128,2048]{1,0:T(8,128)}, f32[128,2048]{1,0:T(8,128)}, ...), branch_computations={%region_29.30_spmd, %region_30.0_spmd} | conditional | flops 4716547 | bytes 30057196 | solution.py:55
  353.1 15.7 %conditional.24 = (bf16[128,2048]{1,0:T(8,128)(2,1)}, bf16[256,1024]{1,0:T(8,128)(2,1)}, bf16[256,1024]{1,0:T(8,128)(2,1)}, bf16[256,1024]{1,0:T(8,128)(2,1)}, b...) conditional(s32[]{:T(128)} %bitcast.20, () %tuple.174, ...), branch_computations={%region_39.40_spmd, %region_40.41_spmd} | conditional | flops 1073741824 | bytes 6291600 | solution.py:55
  353.1 7.0 %pair_product.5 = (bf16[256,1024]{1,0:T(8,128)(2,1)}, bf16[256,1024]{1,0:T(8,128)(2,1)}, bf16[256,1024]{1,0:T(8,128)(2,1)}, bf16[256,1024]{1,0:T(8,128)(2,1)}, b...) custom-call(s32[1]{0:T(128)} %bitcast.3.me_ref, ...), custom_call_target="tpu_custom_call" | custom-call | flops 1073741824 | bytes 4194304 | tf_op jit(solution)/shard_map/cond/branch_1_fun/pair_product/pallas_call | solution.py:372
  360.1 8.6 %collective-permute-done.4 = bf16[128,2048]{1,0:T(8,128)(2,1)} collective-permute-done((bf16[128,2048]{1,0:T(8,128)(2,1)}, bf16[128,2048]{1,0:T(8,128)(2,1)}, u32[]{:S(2)}, u32[]{:S(2)}) %collective-permute-start.4) | collective-permute-done | bytes 524320 | tf_op jit(solution)/shard_map/cond/branch_1_fun/ppermute | solution.py:73
  368.8 19.3 %conditional.25 = (bf16[128,2048]{1,0:T(8,128)(2,1)}, bf16[256,1024]{1,0:T(8,128)(2,1)}, bf16[256,1024]{1,0:T(8,128)(2,1)}, bf16[512,512]{1,0:T(8,128)(2,1)S(1)}, bf16[512,2048]{1,0:T(8,128)(2,1)}) conditional(s32[]{:T(128)} %bitcast.20, () %tuple.210, (bf16[128,2048]{1,0:T(8,128)(2,1)}, bf16[128,2048]{1,0:T(8,128)(2,1)}, ...), branch_computations={%region_41.42_spmd, %region_42.43_spmd} | conditional | flops 3490709504 | bytes 19398816 | solution.py:55
  371.6 4.1 rows_product.3
  375.8 4.4 against.1
  389.4 16.2 %conditional.26 = (bf16[128,2048]{1,0:T(8,128)(2,1)}, bf16[256,1024]{1,0:T(8,128)(2,1)}, bf16[256,1024]{1,0:T(8,128)(2,1)}, bf16[512,1536]{1,0:T(8,128)(2,1)}, f32[8,1536]{1,0:T(8,128)}) conditional(s32[]{:T(128)} %bitcast.20, () %tuple.209, (bf16[128,2048]{1,0:T(8,128)(2,1)}, bf16[128,2048]{1,0:T(8,128)(2,1)}, bf16[256,1024]{1,0:T(8,128)(2,1)}, ...), branch_computations={%region_43.44_spmd, %region_44.45_spmd} | conditional | flops 1048576 | bytes 9969852 | solution.py:55
  391.4 8.4 %attend_back.1 = (bf16[512,1536]{1,0:T(8,128)(2,1)}, f32[8,1536]{1,0:T(8,128)}) custom-call(bf16[512,1536]{1,0:T(8,128)(2,1)S(1)} %get-tuple-element.551.query_ref.key_ref.value_ref, bf16[512,1536]{1,0:T(8,128)(2,1)S(1)} %get-tuple-element.551.query_ref.key_ref.value_ref, bf16[512,1536]{1,0:T(8,128)(2,1)S(1)} %get-tuple-element.551.query_ref.key_ref.value_ref, ...), custom_call_target="tpu_custom_call" | custom-call | tf_op jit(solution)/shard_map/cond/branch_1_fun/attend_back/pallas_call | solution.py:712
  399.7 3.5 collective-permute-done.12
  405.6 18.2 %conditional.27 = (bf16[256,1024]{1,0:T(8,128)(2,1)}, bf16[256,1024]{1,0:T(8,128)(2,1)}, bf16[1024,1536]{1,0:T(8,128)(2,1)}, bf16[128,2048]{1,0:T(8,128)(2,1)}, ...) conditional(s32[]{:T(128)} %bitcast.20, () %tuple.173, (bf16[256,1024]{1,0:T(8,128)(2,1)}, ...), branch_computations={%region_45.46_spmd, %region_46.47_spmd} | conditional | flops 1880883200 | bytes 25977060 | solution.py:55
  408.4 5.7 %pair_product.6 = bf16[1024,1536]{1,0:T(8,128)(2,1)} custom-call(s32[1]{0:T(128)} %bitcast.4.me_ref, bf16[128,2048]{1,0:T(8,128)(2,1)} %get-tuple-element.560.refs_0_, bf16[128,2048]{1,0:T(8,128)(2,1)} %get-tuple-element.561.refs_1_, bf16[128,2048]{1,0:T(8,128)(2,1)} %get-tuple-element.562.refs_2_, bf16[128,2048]{1,0:T(8,128)(2,1)} %get-tuple-element.563.refs_3_, ...), custom_call_target="tpu_custom_call" | custom-call | flops 1073741824 | bytes 4194304 | tf_op jit(solution)/shard_map/cond/branch_1_fun/pair_product/pallas_call | solution.py:372
  414.1 4.2 against_sums.4
  425.0 18.6 %conditional.28 = (bf16[128,2048]{1,0:T(8,128)(2,1)}, bf16[256,768]{1,0:T(8,128)(2,1)}, bf16[256,768]{1,0:T(8,128)(2,1)}, bf16[256,768]{1,0:T(8,128)(2,1)}, bf16...) conditional(s32[]{:T(128)} %bitcast.20, () %tuple.218, ...), branch_computations={%region_48.49_spmd, %region_49.50_spmd} | conditional | flops 2953576448 | bytes 46924804 | solution.py:55
  430.0 5.5 %against_sums.5 = (f32[128,2048]{1,0:T(8,128)S(1)}, f32[8,2048]{1,0:T(8,128)}) custom-call(bf16[2048,1536]{1,0:T(8,128)(2,1)} %get-tuple-element.589.refs_0_, bf16[128,1536]{1,0:T(8,128)(2,1)S(1)} %slice.189.refs_1_, f32[128,2048]{1,0:T(8,128)} %get-tuple-element.590.refs_2_), custom_call_target="tpu_custom_call" | custom-call | flops 805306368 | bytes 6291456 | tf_op jit(solution)/shard_map/cond/branch_1_fun/against_sums/pallas_call | solution.py:430
  437.4 4.3 pair_product.7
  443.7 27.2 %conditional.29 = (bf16[128,2048]{1,0:T(8,128)(2,1)}, bf16[256,768]{1,0:T(8,128)(2,1)}, bf16[256,768]{1,0:T(8,128)(2,1)}, bf16[256,768]{1,0:T(8,128)(2,1)}, bf16...) conditional(s32[]{:T(128)} %bitcast.20, () %tuple.217, ...), branch_computations={%region_50.51_spmd, %region_51.52_spmd} | conditional | flops 2695718400 | bytes 39466204 | solution.py:55
  451.8 3.7 against_sums.6
  455.6 4.6 against_sums.7
  461.6 4.1 collective-permute-start.41
  470.9 28.2 %conditional.30 = (f32[128,2048]{1,0:T(8,128)S(1)}, bf16[64,1536]{1,0:T(8,128)(2,1)S(1)}, bf16[64,1536]{1,0:T(8,128)(2,1)}, bf16[64,1536]{1,0:T(8,128)(2,1)}, bf...) conditional(s32[]{:T(128)} %bitcast.20, () %tuple.216, ...), branch_computations={%region_53.54_spmd, %region_54.55_spmd} | conditional | flops 1074291968 | bytes 24517900 | solution.py:55
  474.1 6.3 %collective-permute-done.28.refs_2_ = bf16[256,768]{1,0:T(8,128)(2,1)S(1)} collective-permute-done((bf16[256,768]{1,0:T(8,128)(2,1)}, bf16[256,768]{1,0:T(8,128)(2,1)S(1)}, u32[]{:S(2)}, u32[]{:S(2)}) %collective-permute-start.28) | collective-permute-done | bytes 393248 | tf_op jit(solution)/shard_map/cond/branch_1_fun/ppermute | solution.py:333
  499.7 32.8 %conditional.31 = (f32[64,6144]{1,0:T(8,128)}, f32[64,8192]{1,0:T(8,128)}, f32[256,2048]{1,0:T(8,128)}, f32[64,2048]{1,0:T(8,128)}, f32[1,128,2048]{2,1,0:T(8,128)}) conditional(s32[]{:T(128)} %bitcast.20, () %tuple.215, (bf16[64,1536]{1,0:T(8,128)(2,1)}, bf16[64,1536]{1,0:T(8,128)(2,1)}, bf16[64,1536]{1,0:T(8,128)(2,1)}, ...), branch_computations={%region_55.56_spmd, %region_56.59_spmd} | conditional | flops 3277058 | bytes 19732312 | solution.py:55
  500.4 3.6 collective-permute-start.24
  515.3 5.4 collective-permute-done.21.refs_2_
  520.7 6.7 %collective-permute-done.22.refs_3_ = bf16[64,1536]{1,0:T(8,128)(2,1)} collective-permute-done((bf16[64,1536]{1,0:T(8,128)(2,1)}, bf16[64,1536]{1,0:T(8,128)(2,1)}, u32[]{:S(2)}, u32[]{:S(2)}) %collective-permute-start.22) | collective-permute-done | bytes 196640 | tf_op jit(solution)/shard_map/cond/branch_1_fun/ppermute | solution.py:844
  (470 shorter events, 219.2 us)
Async XLA Ops:
  7.2 100.5 %all-gather.4.cloned.1.call-start = ((), (), s32[]{:S(2)}) async-start(), calls=%async_computation.2 | async-start | bytes 10027008 | tf_op jit(solution)/shard_map/all_gather | solution.py:329
  9.6 26.2 %collective-permute-start.45 = (bf16[64,2048]{1,0:T(8,128)(2,1)}, bf16[64,2048]{1,0:T(8,128)(2,1)S(1)}, u32[]{:S(2)}, u32[]{:S(2)}) collective-permute-start(bf16[64,2048]{1,0:T(8,128)(2,1)} %param.60), channel_id=1, source_target_pairs={{0,0},{1,16},{2,2},{3,18},{4,4},{5,20},{6,6},{7,22},{8,8},{9,24},{... | collective-permute-start | bytes 786440 | tf_op jit(solution)/shard_map/ppermute | solution.py:959
  11.2 18.8 %collective-permute-start.42 = (bf16[64,1664]{1,0:T(8,128)(2,1)}, bf16[64,1664]{1,0:T(8,128)(2,1)S(1)}, u32[]{:S(2)}, u32[]{:S(2)}) collective-permute-start(bf16[64,1664]{1,0:T(8,128)(2,1)} %get-tuple-element.828), channel_id=1, source_target_pairs={{0,1},{1,2},{2,3},{3,0},{4,5},{5,6},{6,7},{7,4},{8,9},{9,10},{10,1... | collective-permute-start | bytes 638984 | tf_op jit(solution)/shard_map/ppermute | solution.py:844
  16.0 18.4 %collective-permute-start.43 = (bf16[64,1664]{1,0:T(8,128)(2,1)}, bf16[64,1664]{1,0:T(8,128)(2,1)S(1)}, u32[]{:S(2)}, u32[]{:S(2)}) collective-permute-start(bf16[64,1664]{1,0:T(8,128)(2,1)} %get-tuple-element.829), channel_id=1, source_target_pairs={{0,2},{1,3},{2,0},{3,1},{4,6},{5,7},{6,4},{7,5},{8,10},{9,11},{10,... | collective-permute-start | bytes 638984 | tf_op jit(solution)/shard_map/ppermute | solution.py:844
  18.5 17.3 %collective-permute-start.44 = (bf16[64,1664]{1,0:T(8,128)(2,1)}, bf16[64,1664]{1,0:T(8,128)(2,1)S(1)}, u32[]{:S(2)}, u32[]{:S(2)}) collective-permute-start(bf16[64,1664]{1,0:T(8,128)(2,1)} %get-tuple-element.830), channel_id=1, source_target_pairs={{0,3},{1,0},{2,1},{3,2},{4,7},{5,4},{6,5},{7,6},{8,11},{9,8},{10,9... | collective-permute-start | bytes 638984 | tf_op jit(solution)/shard_map/ppermute | solution.py:844
  39.6 135.1 %all-gather.6.cloned.1.call-start = ((), (), s32[]{:S(2)}) async-start(), calls=%async_computation.3 | async-start | bytes 9437184 | tf_op jit(solution)/shard_map/all_gather | solution.py:329
  39.7 11.1 %collective-permute-start.46 = (bf16[64,2048]{1,0:T(8,128)(2,1)S(1)}, bf16[64,2048]{1,0:T(8,128)(2,1)S(1)}, u32[]{:S(2)}, u32[]{:S(2)}) collective-permute-start(bf16[64,2048]{1,0:T(8,128)(2,1)S(1)} %get-tuple-element.1069), channel_id=1, source_target_pairs={{0,1},{1,2},{2,3},{3,0},{4,5},{5,6},{6,7},{7,4},{8,9},{9,10},{10,1... | collective-permute-start | bytes 786440 | tf_op jit(solution)/shard_map/ppermute | solution.py:73
  41.7 14.7 %collective-permute-start.47 = (bf16[64,2048]{1,0:T(8,128)(2,1)S(1)}, bf16[64,2048]{1,0:T(8,128)(2,1)S(1)}, u32[]{:S(2)}, u32[]{:S(2)}) collective-permute-start(bf16[64,2048]{1,0:T(8,128)(2,1)S(1)} %get-tuple-element.1070), channel_id=1, source_target_pairs={{0,1},{1,2},{2,3},{3,0},{4,5},{5,6},{6,7},{7,4},{8,9},{9,10},{10,1... | collective-permute-start | bytes 786440 | tf_op jit(solution)/shard_map/ppermute | solution.py:73
  50.8 11.2 %collective-permute-start.48 = (bf16[64,2048]{1,0:T(8,128)(2,1)S(1)}, bf16[64,2048]{1,0:T(8,128)(2,1)S(1)}, u32[]{:S(2)}, u32[]{:S(2)}) collective-permute-start(bf16[64,2048]{1,0:T(8,128)(2,1)S(1)} %collective-permute-done.46), channel_id=1, source_target_pairs={{0,1},{1,2},{2,3},{3,0},{4,5},{5,6},{6,7},{7,4},{8,9},{9,10},{10,1... | collective-permute-start | bytes 786440 | tf_op jit(solution)/shard_map/ppermute | solution.py:73
  56.4 11.2 %collective-permute-start.49 = (bf16[64,2048]{1,0:T(8,128)(2,1)S(1)}, bf16[64,2048]{1,0:T(8,128)(2,1)S(1)}, u32[]{:S(2)}, u32[]{:S(2)}) collective-permute-start(bf16[64,2048]{1,0:T(8,128)(2,1)S(1)} %collective-permute-done.47), channel_id=1, source_target_pairs={{0,1},{1,2},{2,3},{3,0},{4,5},{5,6},{6,7},{7,4},{8,9},{9,10},{10,1... | collective-permute-start | bytes 786440 | tf_op jit(solution)/shard_map/ppermute | solution.py:73
  62.0 11.2 %collective-permute-start.50 = (bf16[64,2048]{1,0:T(8,128)(2,1)S(1)}, bf16[64,2048]{1,0:T(8,128)(2,1)S(1)}, u32[]{:S(2)}, u32[]{:S(2)}) collective-permute-start(bf16[64,2048]{1,0:T(8,128)(2,1)S(1)} %collective-permute-done.48), channel_id=1, source_target_pairs={{0,1},{1,2},{2,3},{3,0},{4,5},{5,6},{6,7},{7,4},{8,9},{9,10},{10,1... | collective-permute-start | bytes 786440 | tf_op jit(solution)/shard_map/ppermute | solution.py:73
  76.8 11.3 %collective-permute-start.52 = (bf16[64,2048]{1,0:T(8,128)(2,1)}, bf16[64,2048]{1,0:T(8,128)(2,1)S(1)}, u32[]{:S(2)}, u32[]{:S(2)}) collective-permute-start(bf16[64,2048]{1,0:T(8,128)(2,1)} %get-tuple-element.840), channel_id=1, source_target_pairs={{0,1},{1,2},{2,3},{3,0},{4,5},{5,6},{6,7},{7,4},{8,9},{9,10},{10,1... | collective-permute-start | bytes 786440 | tf_op jit(solution)/shard_map/ppermute | solution.py:844
  76.8 19.7 %collective-permute-start.53 = (bf16[64,2048]{1,0:T(8,128)(2,1)}, bf16[64,2048]{1,0:T(8,128)(2,1)S(1)}, u32[]{:S(2)}, u32[]{:S(2)}) collective-permute-start(bf16[64,2048]{1,0:T(8,128)(2,1)} %get-tuple-element.841), channel_id=1, source_target_pairs={{0,2},{1,3},{2,0},{3,1},{4,6},{5,7},{6,4},{7,5},{8,10},{9,11},{10,... | collective-permute-start | bytes 786440 | tf_op jit(solution)/shard_map/ppermute | solution.py:844
  77.9 18.6 %collective-permute-start.54 = (bf16[64,2048]{1,0:T(8,128)(2,1)}, bf16[64,2048]{1,0:T(8,128)(2,1)S(1)}, u32[]{:S(2)}, u32[]{:S(2)}) collective-permute-start(bf16[64,2048]{1,0:T(8,128)(2,1)} %get-tuple-element.842), channel_id=1, source_target_pairs={{0,3},{1,0},{2,1},{3,2},{4,7},{5,4},{6,5},{7,6},{8,11},{9,8},{10,9... | collective-permute-start | bytes 786440 | tf_op jit(solution)/shard_map/ppermute | solution.py:844
  99.1 125.2 %all-gather.8.cloned.1.call-start = ((), (), s32[]{:S(2)}) async-start(), calls=%async_computation.4 | async-start | bytes 9437184 | tf_op jit(solution)/shard_map/all_gather | solution.py:329
  99.9 325.1 %reduce-scatter.3.cloned.1.call-start = ((), (), s32[]{:S(2)}) async-start(), calls=%async_computation.5 | async-start | bytes 9437184 | tf_op jit(solution)/shard_map/reduce_scatter | solution.py:778
  130.3 12.9 %collective-permute-start.55 = (bf16[64,2048]{1,0:T(8,128)(2,1)}, bf16[64,2048]{1,0:T(8,128)(2,1)}, u32[]{:S(2)}, u32[]{:S(2)}) collective-permute-start(bf16[64,2048]{1,0:T(8,128)(2,1)} %get-tuple-element.1067), channel_id=1, source_target_pairs={{0,1},{1,2},{2,3},{3,0},{4,5},{5,6},{6,7},{7,4},{8,9},{9,10},{10,1... | collective-permute-start | bytes 786440 | tf_op jit(solution)/shard_map/ppermute | solution.py:73
  135.3 12.1 %collective-permute-start.58 = (bf16[64,2048]{1,0:T(8,128)(2,1)S(1)}, bf16[64,2048]{1,0:T(8,128)(2,1)}, u32[]{:S(2)}, u32[]{:S(2)}) collective-permute-start(bf16[64,2048]{1,0:T(8,128)(2,1)S(1)} %get-tuple-element.1068), channel_id=1, source_target_pairs={{0,1},{1,2},{2,3},{3,0},{4,5},{5,6},{6,7},{7,4},{8,9},{9,10},{10,1... | collective-permute-start | bytes 786440 | tf_op jit(solution)/shard_map/ppermute | solution.py:73
  145.0 11.4 %collective-permute-start.56 = (bf16[64,2048]{1,0:T(8,128)(2,1)}, bf16[64,2048]{1,0:T(8,128)(2,1)}, u32[]{:S(2)}, u32[]{:S(2)}) collective-permute-start(bf16[64,2048]{1,0:T(8,128)(2,1)} %fusion.35), channel_id=1, source_target_pairs={{0,1},{1,2},{2,3},{3,0},{4,5},{5,6},{6,7},{7,4},{8,9},{9,10},{10,1... | collective-permute-start | bytes 786440 | tf_op jit(solution)/shard_map/ppermute | solution.py:73
  148.5 13.2 %collective-permute-start.59 = (bf16[64,2048]{1,0:T(8,128)(2,1)S(1)}, bf16[64,2048]{1,0:T(8,128)(2,1)}, u32[]{:S(2)}, u32[]{:S(2)}) collective-permute-start(bf16[64,2048]{1,0:T(8,128)(2,1)S(1)} %fusion.33), channel_id=1, source_target_pairs={{0,1},{1,2},{2,3},{3,0},{4,5},{5,6},{6,7},{7,4},{8,9},{9,10},{10,1... | collective-permute-start | bytes 786440 | tf_op jit(solution)/shard_map/ppermute | solution.py:73
  157.5 11.0 %collective-permute-start.57 = (bf16[64,2048]{1,0:T(8,128)(2,1)S(1)}, bf16[64,2048]{1,0:T(8,128)(2,1)S(1)}, u32[]{:S(2)}, u32[]{:S(2)}) collective-permute-start(bf16[64,2048]{1,0:T(8,128)(2,1)S(1)} %fusion.34), channel_id=1, source_target_pairs={{0,1},{1,2},{2,3},{3,0},{4,5},{5,6},{6,7},{7,4},{8,9},{9,10},{10,1... | collective-permute-start | bytes 786440 | tf_op jit(solution)/shard_map/ppermute | solution.py:73
  174.4 11.1 %collective-permute-start.62 = (bf16[64,2048]{1,0:T(8,128)(2,1)S(1)}, bf16[64,2048]{1,0:T(8,128)(2,1)S(1)}, u32[]{:S(2)}, u32[]{:S(2)}) collective-permute-start(bf16[64,2048]{1,0:T(8,128)(2,1)S(1)} %get-tuple-element.1065.refs_2_), channel_id=1, source_target_pairs={{0,1},{1,2},{2,3},{3,0},{4,5},{5,6},{6,7},{7,4},{8,9},{9,10},{10,1... | collective-permute-start | bytes 786440 | tf_op jit(solution)/shard_map/ppermute | solution.py:73
  174.4 16.7 %collective-permute-start.61 = (bf16[64,2048]{1,0:T(8,128)(2,1)S(1)}, bf16[64,2048]{1,0:T(8,128)(2,1)}, u32[]{:S(2)}, u32[]{:S(2)}) collective-permute-start(bf16[64,2048]{1,0:T(8,128)(2,1)S(1)} %get-tuple-element.1066.refs_1_), channel_id=1, source_target_pairs={{0,1},{1,2},{2,3},{3,0},{4,5},{5,6},{6,7},{7,4},{8,9},{9,10},{10,1... | collective-permute-start | bytes 786440 | tf_op jit(solution)/shard_map/ppermute | solution.py:73
  185.5 12.7 %collective-permute-start.64 = (bf16[64,2048]{1,0:T(8,128)(2,1)S(1)}, bf16[64,2048]{1,0:T(8,128)(2,1)S(1)}, u32[]{:S(2)}, u32[]{:S(2)}) collective-permute-start(bf16[64,2048]{1,0:T(8,128)(2,1)S(1)} %collective-permute-done.62.refs_2_), channel_id=1, source_target_pairs={{0,1},{1,2},{2,3},{3,0},{4,5},{5,6},{6,7},{7,4},{8,9},{9,10},{10,1... | collective-permute-start | bytes 786440 | tf_op jit(solution)/shard_map/ppermute | solution.py:73
  191.2 11.1 %collective-permute-start.63 = (bf16[64,2048]{1,0:T(8,128)(2,1)}, bf16[64,2048]{1,0:T(8,128)(2,1)S(1)}, u32[]{:S(2)}, u32[]{:S(2)}) collective-permute-start(bf16[64,2048]{1,0:T(8,128)(2,1)} %collective-permute-done.61.refs_1_), channel_id=1, source_target_pairs={{0,1},{1,2},{2,3},{3,0},{4,5},{5,6},{6,7},{7,4},{8,9},{9,10},{10,1... | collective-permute-start | bytes 786440 | tf_op jit(solution)/shard_map/ppermute | solution.py:73
  198.2 10.7 %collective-permute-start.66 = (bf16[64,2048]{1,0:T(8,128)(2,1)S(1)}, bf16[64,2048]{1,0:T(8,128)(2,1)}, u32[]{:S(2)}, u32[]{:S(2)}) collective-permute-start(bf16[64,2048]{1,0:T(8,128)(2,1)S(1)} %collective-permute-done.64.refs_2_), channel_id=1, source_target_pairs={{0,1},{1,2},{2,3},{3,0},{4,5},{5,6},{6,7},{7,4},{8,9},{9,10},{10,1... | collective-permute-start | bytes 786440 | tf_op jit(solution)/shard_map/ppermute | solution.py:73
  202.3 9.4 %collective-permute-start.65 = (bf16[64,2048]{1,0:T(8,128)(2,1)S(1)}, bf16[64,2048]{1,0:T(8,128)(2,1)}, u32[]{:S(2)}, u32[]{:S(2)}) collective-permute-start(bf16[64,2048]{1,0:T(8,128)(2,1)S(1)} %collective-permute-done.63.refs_1_), channel_id=1, source_target_pairs={{0,1},{1,2},{2,3},{3,0},{4,5},{5,6},{6,7},{7,4},{8,9},{9,10},{10,1... | collective-permute-start | bytes 786440 | tf_op jit(solution)/shard_map/ppermute | solution.py:73
  211.7 12.7 %collective-permute-start = (bf16[128,2048]{1,0:T(8,128)(2,1)S(1)}, bf16[128,2048]{1,0:T(8,128)(2,1)}, u32[]{:S(2)}, u32[]{:S(2)}) collective-permute-start(bf16[128,2048]{1,0:T(8,128)(2,1)S(1)} %get-tuple-element.423), channel_id=1, source_target_pairs={{0,1},{1,2},{2,3},{3,0},{4,5},{5,6},{6,7},{7,4},{8,9},{9,10},{10,1... | collective-permute-start | bytes 1572872 | tf_op jit(solution)/shard_map/cond/branch_1_fun/ppermute | solution.py:73
  224.4 11.4 %collective-permute-start.1 = (bf16[128,2048]{1,0:T(8,128)(2,1)}, bf16[128,2048]{1,0:T(8,128)(2,1)}, u32[]{:S(2)}, u32[]{:S(2)}) collective-permute-start(bf16[128,2048]{1,0:T(8,128)(2,1)} %get-tuple-element.435), channel_id=1, source_target_pairs={{0,1},{1,2},{2,3},{3,0},{4,5},{5,6},{6,7},{7,4},{8,9},{9,10},{10,1... | collective-permute-start | bytes 1572872 | tf_op jit(solution)/shard_map/cond/branch_1_fun/ppermute | solution.py:73
  248.6 16.6 %collective-permute-start.2 = (bf16[128,2048]{1,0:T(8,128)(2,1)}, bf16[128,2048]{1,0:T(8,128)(2,1)}, u32[]{:S(2)}, u32[]{:S(2)}) collective-permute-start(bf16[128,2048]{1,0:T(8,128)(2,1)} %get-tuple-element.443), channel_id=1, source_target_pairs={{0,1},{1,2},{2,3},{3,0},{4,5},{5,6},{6,7},{7,4},{8,9},{9,10},{10,1... | collective-permute-start | bytes 1572872 | tf_op jit(solution)/shard_map/cond/branch_1_fun/ppermute | solution.py:73
  265.3 21.6 %collective-permute-start.5 = (bf16[128,2048]{1,0:T(8,128)(2,1)}, bf16[128,2048]{1,0:T(8,128)(2,1)}, u32[]{:S(2)}, u32[]{:S(2)}) collective-permute-start(bf16[128,2048]{1,0:T(8,128)(2,1)} %get-tuple-element.444), channel_id=1, source_target_pairs={{0,1},{1,2},{2,3},{3,0},{4,5},{5,6},{6,7},{7,4},{8,9},{9,10},{10,1... | collective-permute-start | bytes 1572872 | tf_op jit(solution)/shard_map/cond/branch_1_fun/ppermute | solution.py:73
  288.9 181.9 %reduce-scatter.5.cloned.1.call-start = ((), (), s32[]{:S(2)}) async-start(), calls=%async_computation.6 | async-start | bytes 2359296 | tf_op jit(solution)/shard_map/reduce_scatter | solution.py:778
  289.0 15.1 %collective-permute-start.6 = (bf16[128,2048]{1,0:T(8,128)(2,1)}, bf16[128,2048]{1,0:T(8,128)(2,1)S(1)}, u32[]{:S(2)}, u32[]{:S(2)}) collective-permute-start(bf16[128,2048]{1,0:T(8,128)(2,1)} %get-tuple-element.461), channel_id=1, source_target_pairs={{0,1},{1,2},{2,3},{3,0},{4,5},{5,6},{6,7},{7,4},{8,9},{9,10},{10,1... | collective-permute-start | bytes 1572872 | tf_op jit(solution)/shard_map/cond/branch_1_fun/ppermute | solution.py:73
  304.2 14.5 %collective-permute-start.25 = (bf16[128,2048]{1,0:T(8,128)(2,1)S(1)}, bf16[128,2048]{1,0:T(8,128)(2,1)S(1)}, u32[]{:S(2)}, u32[]{:S(2)}) collective-permute-start(bf16[128,2048]{1,0:T(8,128)(2,1)S(1)} %get-tuple-element.469), channel_id=1, source_target_pairs={{0,1},{1,2},{2,3},{3,0},{4,5},{5,6},{6,7},{7,4},{8,9},{9,10},{10,1... | collective-permute-start | bytes 1572872 | tf_op jit(solution)/shard_map/cond/branch_1_fun/ppermute | solution.py:73
  323.4 11.3 %collective-permute-start.3 = (bf16[128,2048]{1,0:T(8,128)(2,1)}, bf16[128,2048]{1,0:T(8,128)(2,1)}, u32[]{:S(2)}, u32[]{:S(2)}) collective-permute-start(bf16[128,2048]{1,0:T(8,128)(2,1)} %get-tuple-element.477), channel_id=1, source_target_pairs={{0,1},{1,2},{2,3},{3,0},{4,5},{5,6},{6,7},{7,4},{8,9},{9,10},{10,1... | collective-permute-start | bytes 1572872 | tf_op jit(solution)/shard_map/cond/branch_1_fun/ppermute | solution.py:73
  336.0 16.5 %collective-permute-start.8 = (bf16[1024,2048]{1,0:T(8,128)(2,1)}, bf16[1024,2048]{1,0:T(8,128)(2,1)}, u32[]{:S(2)}, u32[]{:S(2)}) collective-permute-start(bf16[1024,2048]{1,0:T(8,128)(2,1)} %get-tuple-element.491), channel_id=1, source_target_pairs={{0,4},{4,0},{8,12},{12,8},{16,20},{20,16},{24,28},{28,24},{1,5},{5... | collective-permute-start | bytes 12582920 | tf_op jit(solution)/shard_map/cond/branch_1_fun/ppermute | solution.py:333
  336.0 16.4 %collective-permute-start.7 = (bf16[128,2048]{1,0:T(8,128)(2,1)}, bf16[128,2048]{1,0:T(8,128)(2,1)}, u32[]{:S(2)}, u32[]{:S(2)}) collective-permute-start(bf16[128,2048]{1,0:T(8,128)(2,1)} %get-tuple-element.490), channel_id=1, source_target_pairs={{0,1},{1,2},{2,3},{3,0},{4,5},{5,6},{6,7},{7,4},{8,9},{9,10},{10,1... | collective-permute-start | bytes 1572872 | tf_op jit(solution)/shard_map/cond/branch_1_fun/ppermute | solution.py:73
  353.1 15.7 %collective-permute-start.4 = (bf16[128,2048]{1,0:T(8,128)(2,1)}, bf16[128,2048]{1,0:T(8,128)(2,1)}, u32[]{:S(2)}, u32[]{:S(2)}) collective-permute-start(bf16[128,2048]{1,0:T(8,128)(2,1)} %get-tuple-element.511), channel_id=1, source_target_pairs={{0,1},{1,2},{2,3},{3,0},{4,5},{5,6},{6,7},{7,4},{8,9},{9,10},{10,1... | collective-permute-start | bytes 1572872 | tf_op jit(solution)/shard_map/cond/branch_1_fun/ppermute | solution.py:73
  368.8 14.8 %collective-permute-start.9 = (bf16[128,2048]{1,0:T(8,128)(2,1)}, bf16[128,2048]{1,0:T(8,128)(2,1)}, u32[]{:S(2)}, u32[]{:S(2)}) collective-permute-start(bf16[128,2048]{1,0:T(8,128)(2,1)} %get-tuple-element.533), channel_id=1, source_target_pairs={{0,1},{1,2},{2,3},{3,0},{4,5},{5,6},{6,7},{7,4},{8,9},{9,10},{10,1... | collective-permute-start | bytes 1572872 | tf_op jit(solution)/shard_map/cond/branch_1_fun/ppermute | solution.py:109
  368.8 16.9 %collective-permute-start.10 = (bf16[256,1024]{1,0:T(8,128)(2,1)}, bf16[256,1024]{1,0:T(8,128)(2,1)}, u32[]{:S(2)}, u32[]{:S(2)}) collective-permute-start(bf16[256,1024]{1,0:T(8,128)(2,1)} %get-tuple-element.536), channel_id=1, source_target_pairs={{0,8},{4,12},{8,0},{12,4},{16,24},{20,28},{24,16},{28,20},{1,9},{5... | collective-permute-start | bytes 1572872 | tf_op jit(solution)/shard_map/cond/branch_1_fun/ppermute | solution.py:333
  370.4 15.3 %collective-permute-start.11 = (bf16[256,1024]{1,0:T(8,128)(2,1)}, bf16[256,1024]{1,0:T(8,128)(2,1)}, u32[]{:S(2)}, u32[]{:S(2)}) collective-permute-start(bf16[256,1024]{1,0:T(8,128)(2,1)} %get-tuple-element.538), channel_id=1, source_target_pairs={{0,16},{4,20},{8,24},{12,28},{16,0},{20,4},{24,8},{28,12},{1,17},{... | collective-permute-start | bytes 1572872 | tf_op jit(solution)/shard_map/cond/branch_1_fun/ppermute | solution.py:333
  389.4 13.9 %collective-permute-start.12 = (bf16[128,2048]{1,0:T(8,128)(2,1)}, bf16[128,2048]{1,0:T(8,128)(2,1)}, u32[]{:S(2)}, u32[]{:S(2)}) collective-permute-start(bf16[128,2048]{1,0:T(8,128)(2,1)} %get-tuple-element.547), channel_id=1, source_target_pairs={{0,1},{1,2},{2,3},{3,0},{4,5},{5,6},{6,7},{7,4},{8,9},{9,10},{10,1... | collective-permute-start | bytes 1572872 | tf_op jit(solution)/shard_map/cond/branch_1_fun/ppermute | solution.py:109
  389.4 16.0 %collective-permute-start.13 = (bf16[256,1024]{1,0:T(8,128)(2,1)}, bf16[256,1024]{1,0:T(8,128)(2,1)}, u32[]{:S(2)}, u32[]{:S(2)}) collective-permute-start(bf16[256,1024]{1,0:T(8,128)(2,1)} %get-tuple-element.549), channel_id=1, source_target_pairs={{0,16},{4,20},{8,24},{12,28},{16,0},{20,4},{24,8},{28,12},{1,17},{... | collective-permute-start | bytes 1572872 | tf_op jit(solution)/shard_map/cond/branch_1_fun/ppermute | solution.py:333
  389.5 15.9 %collective-permute-start.14 = (bf16[256,1024]{1,0:T(8,128)(2,1)}, bf16[256,1024]{1,0:T(8,128)(2,1)}, u32[]{:S(2)}, u32[]{:S(2)}) collective-permute-start(bf16[256,1024]{1,0:T(8,128)(2,1)} %get-tuple-element.550), channel_id=1, source_target_pairs={{0,8},{4,12},{8,0},{12,4},{16,24},{20,28},{24,16},{28,20},{1,9},{5... | collective-permute-start | bytes 1572872 | tf_op jit(solution)/shard_map/cond/branch_1_fun/ppermute | solution.py:333
  405.6 13.7 %collective-permute-start.17 = (bf16[128,2048]{1,0:T(8,128)(2,1)}, bf16[128,2048]{1,0:T(8,128)(2,1)S(1)}, u32[]{:S(2)}, u32[]{:S(2)}) collective-permute-start(bf16[128,2048]{1,0:T(8,128)(2,1)} %get-tuple-element.570), channel_id=1, source_target_pairs={{0,1},{1,2},{2,3},{3,0},{4,5},{5,6},{6,7},{7,4},{8,9},{9,10},{10,1... | collective-permute-start | bytes 1572872 | tf_op jit(solution)/shard_map/cond/branch_1_fun/ppermute | solution.py:109
  405.7 16.8 %collective-permute-start.15 = (bf16[256,1024]{1,0:T(8,128)(2,1)}, bf16[256,1024]{1,0:T(8,128)(2,1)}, u32[]{:S(2)}, u32[]{:S(2)}) collective-permute-start(bf16[256,1024]{1,0:T(8,128)(2,1)} %get-tuple-element.558), channel_id=1, source_target_pairs={{0,8},{4,12},{8,0},{12,4},{16,24},{20,28},{24,16},{28,20},{1,9},{5... | collective-permute-start | bytes 1572872 | tf_op jit(solution)/shard_map/cond/branch_1_fun/ppermute | solution.py:333
  407.3 16.5 %collective-permute-start.16 = (bf16[256,1024]{1,0:T(8,128)(2,1)}, bf16[256,1024]{1,0:T(8,128)(2,1)}, u32[]{:S(2)}, u32[]{:S(2)}) collective-permute-start(bf16[256,1024]{1,0:T(8,128)(2,1)} %get-tuple-element.559), channel_id=1, source_target_pairs={{0,16},{4,20},{8,24},{12,28},{16,0},{20,4},{24,8},{28,12},{1,17},{... | collective-permute-start | bytes 1572872 | tf_op jit(solution)/shard_map/cond/branch_1_fun/ppermute | solution.py:333
  425.0 11.6 %collective-permute-start.19 = (bf16[1024,1536]{1,0:T(8,128)(2,1)}, bf16[1024,1536]{1,0:T(8,128)(2,1)S(1)}, u32[]{:S(2)}, u32[]{:S(2)}) collective-permute-start(bf16[1024,1536]{1,0:T(8,128)(2,1)} %get-tuple-element.579), channel_id=1, source_target_pairs={{0,4},{4,0},{8,12},{12,8},{16,20},{20,16},{24,28},{28,24},{1,5},{5... | collective-permute-start | bytes 9437192 | tf_op jit(solution)/shard_map/cond/branch_1_fun/ppermute | solution.py:333
  425.0 16.7 %collective-permute-start.18 = (bf16[128,2048]{1,0:T(8,128)(2,1)}, bf16[128,2048]{1,0:T(8,128)(2,1)}, u32[]{:S(2)}, u32[]{:S(2)}) collective-permute-start(bf16[128,2048]{1,0:T(8,128)(2,1)} %get-tuple-element.573), channel_id=1, source_target_pairs={{0,1},{1,2},{2,3},{3,0},{4,5},{5,6},{6,7},{7,4},{8,9},{9,10},{10,1... | collective-permute-start | bytes 1572872 | tf_op jit(solution)/shard_map/cond/branch_1_fun/ppermute | solution.py:73
  443.7 24.3 %collective-permute-start.36 = (bf16[128,2048]{1,0:T(8,128)(2,1)}, bf16[128,2048]{1,0:T(8,128)(2,1)}, u32[]{:S(2)}, u32[]{:S(2)}) collective-permute-start(bf16[128,2048]{1,0:T(8,128)(2,1)} %get-tuple-element.601), channel_id=1, source_target_pairs={{0,1},{1,2},{2,3},{3,0},{4,5},{5,6},{6,7},{7,4},{8,9},{9,10},{10,1... | collective-permute-start | bytes 1572872 | tf_op jit(solution)/shard_map/cond/branch_1_fun/ppermute | solution.py:73
  444.1 17.5 %collective-permute-start.39 = (bf16[256,768]{1,0:T(8,128)(2,1)}, bf16[256,768]{1,0:T(8,128)(2,1)}, u32[]{:S(2)}, u32[]{:S(2)}) collective-permute-start(bf16[256,768]{1,0:T(8,128)(2,1)} %get-tuple-element.609), channel_id=1, source_target_pairs={{0,8},{4,12},{8,0},{12,4},{16,24},{20,28},{24,16},{28,20},{1,9},{5... | collective-permute-start | bytes 1179656 | tf_op jit(solution)/shard_map/cond/branch_1_fun/ppermute | solution.py:333
  445.4 20.3 %collective-permute-start.40 = (bf16[256,768]{1,0:T(8,128)(2,1)}, bf16[256,768]{1,0:T(8,128)(2,1)}, u32[]{:S(2)}, u32[]{:S(2)}) collective-permute-start(bf16[256,768]{1,0:T(8,128)(2,1)} %get-tuple-element.611), channel_id=1, source_target_pairs={{0,16},{4,20},{8,24},{12,28},{16,0},{20,4},{24,8},{28,12},{1,17},{... | collective-permute-start | bytes 1179656 | tf_op jit(solution)/shard_map/cond/branch_1_fun/ppermute | solution.py:333
  447.2 22.7 %collective-permute-start.37 = (bf16[256,768]{1,0:T(8,128)(2,1)}, bf16[256,768]{1,0:T(8,128)(2,1)}, u32[]{:S(2)}, u32[]{:S(2)}) collective-permute-start(bf16[256,768]{1,0:T(8,128)(2,1)} %get-tuple-element.606), channel_id=1, source_target_pairs={{0,8},{4,12},{8,0},{12,4},{16,24},{20,28},{24,16},{28,20},{1,9},{5... | collective-permute-start | bytes 1179656 | tf_op jit(solution)/shard_map/cond/branch_1_fun/ppermute | solution.py:333
  447.6 22.4 %collective-permute-start.38 = (bf16[256,768]{1,0:T(8,128)(2,1)}, bf16[256,768]{1,0:T(8,128)(2,1)}, u32[]{:S(2)}, u32[]{:S(2)}) collective-permute-start(bf16[256,768]{1,0:T(8,128)(2,1)} %get-tuple-element.607), channel_id=1, source_target_pairs={{0,16},{4,20},{8,24},{12,28},{16,0},{20,4},{24,8},{28,12},{1,17},{... | collective-permute-start | bytes 1179656 | tf_op jit(solution)/shard_map/cond/branch_1_fun/ppermute | solution.py:333
  461.6 9.3 %collective-permute-start.41 = (bf16[64,2048]{1,0:T(8,128)(2,1)}, bf16[64,2048]{1,0:T(8,128)(2,1)}, u32[]{:S(2)}, u32[]{:S(2)}) collective-permute-start(bf16[64,2048]{1,0:T(8,128)(2,1)} %get-tuple-element.615), channel_id=1, source_target_pairs={{0,1},{1,2},{2,3},{3,0},{4,5},{5,6},{6,7},{7,4},{8,9},{9,10},{10,1... | collective-permute-start | bytes 786440 | tf_op jit(solution)/shard_map/cond/branch_1_fun/ppermute | solution.py:844
  470.9 9.5 %collective-permute-start.28 = (bf16[256,768]{1,0:T(8,128)(2,1)}, bf16[256,768]{1,0:T(8,128)(2,1)S(1)}, u32[]{:S(2)}, u32[]{:S(2)}) collective-permute-start(bf16[256,768]{1,0:T(8,128)(2,1)} %get-tuple-element.631), channel_id=1, source_target_pairs={{0,16},{4,20},{8,24},{12,28},{16,0},{20,4},{24,8},{28,12},{1,17},{... | collective-permute-start | bytes 1179656 | tf_op jit(solution)/shard_map/cond/branch_1_fun/ppermute | solution.py:333
  472.3 9.5 %collective-permute-start.29 = (bf16[256,768]{1,0:T(8,128)(2,1)}, bf16[256,768]{1,0:T(8,128)(2,1)S(1)}, u32[]{:S(2)}, u32[]{:S(2)}) collective-permute-start(bf16[256,768]{1,0:T(8,128)(2,1)} %get-tuple-element.634), channel_id=1, source_target_pairs={{0,8},{4,12},{8,0},{12,4},{16,24},{20,28},{24,16},{28,20},{1,9},{5... | collective-permute-start | bytes 1179656 | tf_op jit(solution)/shard_map/cond/branch_1_fun/ppermute | solution.py:333
  473.9 24.0 %collective-permute-start.26 = (bf16[128,2048]{1,0:T(8,128)(2,1)}, bf16[128,2048]{1,0:T(8,128)(2,1)}, u32[]{:S(2)}, u32[]{:S(2)}) collective-permute-start(bf16[128,2048]{1,0:T(8,128)(2,1)} %get-tuple-element.625), channel_id=1, source_target_pairs={{0,1},{1,2},{2,3},{3,0},{4,5},{5,6},{6,7},{7,4},{8,9},{9,10},{10,1... | collective-permute-start | bytes 1572872 | tf_op jit(solution)/shard_map/cond/branch_1_fun/ppermute | solution.py:73
  474.0 23.9 %collective-permute-start.27 = (bf16[64,2048]{1,0:T(8,128)(2,1)}, bf16[64,2048]{1,0:T(8,128)(2,1)}, u32[]{:S(2)}, u32[]{:S(2)}) collective-permute-start(bf16[64,2048]{1,0:T(8,128)(2,1)} %get-tuple-element.626), channel_id=1, source_target_pairs={{0,2},{1,3},{2,0},{3,1},{4,6},{5,7},{6,4},{7,5},{8,10},{9,11},{10,... | collective-permute-start | bytes 786440 | tf_op jit(solution)/shard_map/cond/branch_1_fun/ppermute | solution.py:844
  499.7 10.0 %collective-permute-start.20 = (bf16[64,1536]{1,0:T(8,128)(2,1)}, bf16[64,1536]{1,0:T(8,128)(2,1)S(1)}, u32[]{:S(2)}, u32[]{:S(2)}) collective-permute-start(bf16[64,1536]{1,0:T(8,128)(2,1)} %get-tuple-element.641), channel_id=1, source_target_pairs={{0,1},{1,2},{2,3},{3,0},{4,5},{5,6},{6,7},{7,4},{8,9},{9,10},{10,1... | collective-permute-start | bytes 589832 | tf_op jit(solution)/shard_map/cond/branch_1_fun/ppermute | solution.py:844
  500.4 13.1 %collective-permute-start.24 = (bf16[64,2048]{1,0:T(8,128)(2,1)}, bf16[64,2048]{1,0:T(8,128)(2,1)}, u32[]{:S(2)}, u32[]{:S(2)}) collective-permute-start(bf16[64,2048]{1,0:T(8,128)(2,1)} %get-tuple-element.656), channel_id=1, source_target_pairs={{0,0},{16,1},{2,2},{18,3},{4,4},{20,5},{6,6},{22,7},{8,8},{24,9},{... | collective-permute-start | bytes 786440 | tf_op jit(solution)/shard_map/cond/branch_1_fun/ppermute | solution.py:1179
  504.0 23.4 %collective-permute-start.23 = (bf16[64,2048]{1,0:T(8,128)(2,1)}, bf16[64,2048]{1,0:T(8,128)(2,1)}, u32[]{:S(2)}, u32[]{:S(2)}) collective-permute-start(bf16[64,2048]{1,0:T(8,128)(2,1)} %get-tuple-element.647), channel_id=1, source_target_pairs={{0,3},{1,0},{2,1},{3,2},{4,7},{5,4},{6,5},{7,6},{8,11},{9,8},{10,9... | collective-permute-start | bytes 786440 | tf_op jit(solution)/shard_map/cond/branch_1_fun/ppermute | solution.py:844
  506.7 14.0 %collective-permute-start.21 = (bf16[64,1536]{1,0:T(8,128)(2,1)}, bf16[64,1536]{1,0:T(8,128)(2,1)}, u32[]{:S(2)}, u32[]{:S(2)}) collective-permute-start(bf16[64,1536]{1,0:T(8,128)(2,1)} %get-tuple-element.642), channel_id=1, source_target_pairs={{0,2},{1,3},{2,0},{3,1},{4,6},{5,7},{6,4},{7,5},{8,10},{9,11},{10,... | collective-permute-start | bytes 589832 | tf_op jit(solution)/shard_map/cond/branch_1_fun/ppermute | solution.py:844
  506.7 20.7 %collective-permute-start.22 = (bf16[64,1536]{1,0:T(8,128)(2,1)}, bf16[64,1536]{1,0:T(8,128)(2,1)}, u32[]{:S(2)}, u32[]{:S(2)}) collective-permute-start(bf16[64,1536]{1,0:T(8,128)(2,1)} %get-tuple-element.643), channel_id=1, source_target_pairs={{0,3},{1,0},{2,1},{3,2},{4,7},{5,4},{6,5},{7,6},{8,11},{9,8},{10,9... | collective-permute-start | bytes 589832 | tf_op jit(solution)/shard_map/cond/branch_1_fun/ppermute | solution.py:844
  (92 other events, 506.1 us)
Sparse Core Ops, SparseCore 0:
  39.7 57.0 all-gather.3
  99.3 56.4 all-gather.5
  157.7 54.3 all-gather.7
  289.1 71.7 reduce-scatter.2
  388.2 43.7 reduce-scatter.4
where the time goes:
time: 550 us; the launch traced here: 539 us
  Pallas kernels  186 us (34%)
  waiting for transfers between devices  157 us (29%)
  starting transfers between devices  74.2 us (13%)
  other arithmetic  58.2 us (11%)
  local copies, waits for them, and re-layouts  40.5 us (7%)
  between operations  15 us (3%)
  matrix products  6.75 us (1%)
    ppermute x30, waiting for transfers between devices, ring_move(): return [lax.ppermute(half, 'seq', ring_next()) for half in halves]  89.8 us
    pallas_call x9, Pallas kernels, stream(): pl.pallas_call(partial(stream_kernel, work, len(operands), len(results)),...  48.5 us
    pallas_call x4, Pallas kernels, second_product(): pl.pallas_call(second_kernel, out_shape=results, grid=(1,), in_specs=[pl....  46.3 us
    ppermute x12, waiting for transfers between devices, swap_rank(): lax.ppermute(block, 'seq', [(place, (place + shift) % size) for place in...  46 us
    pallas_call x4, Pallas kernels, pair_product(): pl.pallas_call(partial(pair_kernel, len(lefts), len(rights), rows, kept),...  23.6 us
    ppermute x30, starting transfers between devices, ring_move(): return [lax.ppermute(half, 'seq', ring_next()) for half in halves]  21.8 us
    ppermute x12, starting transfers between devices, swap_rank(): lax.ppermute(block, 'seq', [(place, (place + shift) % size) for place in...  20.5 us
    ppermute x17, starting transfers between devices, swap_bit(): lax.ppermute(block, axis, [(place, place ^ 1 << bit) for place in range(l...  15.4 us
  transfers between devices with their start and end apart: 75, of which 41 were waited for; matrix products, arithmetic and copies ran while one was open for 16% of the time, Pallas kernels for 33%

commit v1 on v0

--- a/solution.py
+++ b/solution.py
@@ -1197,14 +1197,15 @@
 
         def attend_one(branch_lows, up_pieces):
             dense_sum = ring_step(dense_parts[1], dense_parts[2])
-            up_second = pair_second(up_pieces, pair_onward(up_pieces))
+            up_onward = pair_onward(up_pieces)
             mixture_grad = against(branch_lows, weight_out, LOW)
             out_table = rows_product([mixture_out], branch_lows)
-            return dense_sum, up_second, mixture_grad, out_table
-
-        def attend_two(dense_sum, up_second, mixture_grad):
+            return dense_sum, up_onward, mixture_grad, out_table
+
+        def attend_two(dense_sum, up_pieces, up_onward, mixture_grad):
             dense_sum = ring_step(dense_sum, dense_parts[3])
-            return dense_sum, pair_last(up_second), back(mixture_grad)
+            up_second = pair_last(pair_second(up_pieces, up_onward))
+            return dense_sum, up_second, back(mixture_grad)
 
         def attend_three(dense_sum, up_pieces, projected_grad):
             dense_sum = ring_step(dense_sum, dense_parts[0], WIDE)
@@ -1248,13 +1249,14 @@
             came_up = [came_up[shift] for shift in range(ranks)]
             came_in = swap_ranks(in_sent)
             first_grad, down_late = after((first_grad, down_early), [came_in[1]])
-            done = inputs_back(first_grad), down_late.astype(WIDE), out_back(out_early)
-            came_in, came_up, done = lax.optimization_barrier((came_in, came_up, done))
-            return (
-                collect(came_in, head_pieces, head_width),
+            done = (
                 collect(came_up, hidden_pieces, hidden_here),
-                *done,
+                inputs_back(first_grad),
+                down_late.astype(WIDE),
+                out_back(out_early),
             )
+            came_in, done = lax.optimization_barrier((came_in, done))
+            return collect(came_in, head_pieces, head_width), *done
 
         branch_lows = [branch_low]
         moved, up_sent = step(gather_one, branch_low)
@@ -1263,10 +1265,10 @@
         branch_lows.append(moved)
         moved, up_pieces = step(gather_three, moved, up_got)
         branch_lows.append(moved)
-        dense_sum, up_second, mixture_grad, out_table = step(attend_one, branch_lows, up_pieces)
+        dense_sum, up_onward, mixture_grad, out_table = step(attend_one, branch_lows, up_pieces)
         out_summed = scatter_groups(out_table)
         dense_sum, up_second, (projected_grad, bias_sums) = step(
-            attend_two, dense_sum, up_second, mixture_grad
+            attend_two, dense_sum, up_pieces, up_onward, mixture_grad
         )
         result_low, up_staying, in_sent, sent, sums_one = step(
             attend_three, dense_sum, up_pieces, projected_grad

time: 550 us -> 546 us (level)
  the two profiles are of different devices: /device:TPU:0 before, /device:TPU:4 now
where the time goes in v1:
time: 546 us; the launch traced here: 535 us
  Pallas kernels  187 us (34%)
  waiting for transfers between devices  145 us (27%)
  starting transfers between devices  81.8 us (15%)
  other arithmetic  58.2 us (11%)
  local copies, waits for them, and re-layouts  40 us (7%)
  between operations  15 us (3%)
  matrix products  6.67 us (1%)
    ppermute x30, waiting for transfers between devices, ring_move(): return [lax.ppermute(half, 'seq', ring_next()) for half in halves]  85.3 us
    pallas_call x9, Pallas kernels, stream(): pl.pallas_call(partial(stream_kernel, work, len(operands), len(results)),...  48.5 us
    pallas_call x4, Pallas kernels, second_product(): pl.pallas_call(second_kernel, out_shape=results, grid=(1,), in_specs=[pl....  47.6 us
    ppermute x12, waiting for transfers between devices, swap_rank(): lax.ppermute(block, 'seq', [(place, (place + shift) % size) for place in...  33.8 us
    ppermute x17, starting transfers between devices, swap_bit(): lax.ppermute(block, axis, [(place, place ^ 1 << bit) for place in range(l...  24.9 us
    ppermute x30, starting transfers between devices, ring_move(): return [lax.ppermute(half, 'seq', ring_next()) for half in halves]  24.9 us
    pallas_call x4, Pallas kernels, pair_product(): pl.pallas_call(partial(pair_kernel, len(lefts), len(rights), rows, kept),...  23.4 us
    ppermute x12, starting transfers between devices, swap_rank(): lax.ppermute(block, 'seq', [(place, (place + shift) % size) for place in...  17.4 us
  transfers between devices with their start and end apart: 75, of which 38 were waited for; matrix products, arithmetic and copies ran while one was open for 16% of the time, Pallas kernels for 34%

profile of v1, /device:TPU:4, one launch (start us, length us, event | category | flops | bytes accessed | tf_op | source)
XLA Modules:
  0.0 535.1 jit_solution(8587341182921465526)
XLA Ops:
  9.6 3.4 collective-permute-start.45
  18.6 5.9 %collective-permute-done.42.refs_1_ = bf16[64,1664]{1,0:T(8,128)(2,1)S(1)} collective-permute-done((bf16[64,1664]{1,0:T(8,128)(2,1)}, bf16[64,1664]{1,0:T(8,128)(2,1)S(1)}, u32[]{:S(2)}, u32[]{:S(2)}) %collective-permute-start.42) | collective-permute-done | bytes 213024 | tf_op jit(solution)/shard_map/ppermute | solution.py:844
  24.6 6.5 %collective-permute-done.43.refs_2_ = bf16[64,1664]{1,0:T(8,128)(2,1)S(1)} collective-permute-done((bf16[64,1664]{1,0:T(8,128)(2,1)}, bf16[64,1664]{1,0:T(8,128)(2,1)S(1)}, u32[]{:S(2)}, u32[]{:S(2)}) %collective-permute-start.43) | collective-permute-done | bytes 213024 | tf_op jit(solution)/shard_map/ppermute | solution.py:844
  39.2 9.1 %collective-permute-done.46 = bf16[64,2048]{1,0:T(8,128)(2,1)S(1)} collective-permute-done((bf16[64,2048]{1,0:T(8,128)(2,1)S(1)}, bf16[64,2048]{1,0:T(8,128)(2,1)S(1)}, u32[]{:S(2)}, u32[]{:S(2)}) %collective-permute-start.46) | collective-permute-done | bytes 262176 | tf_op jit(solution)/shard_map/ppermute | solution.py:73
  48.4 5.6 %collective-permute-done.47 = bf16[64,2048]{1,0:T(8,128)(2,1)S(1)} collective-permute-done((bf16[64,2048]{1,0:T(8,128)(2,1)S(1)}, bf16[64,2048]{1,0:T(8,128)(2,1)S(1)}, u32[]{:S(2)}, u32[]{:S(2)}) %collective-permute-start.47) | collective-permute-done | bytes 262176 | tf_op jit(solution)/shard_map/ppermute | solution.py:73
  54.0 5.6 %collective-permute-done.48 = bf16[64,2048]{1,0:T(8,128)(2,1)S(1)} collective-permute-done((bf16[64,2048]{1,0:T(8,128)(2,1)S(1)}, bf16[64,2048]{1,0:T(8,128)(2,1)S(1)}, u32[]{:S(2)}, u32[]{:S(2)}) %collective-permute-start.48) | collective-permute-done | bytes 262176 | tf_op jit(solution)/shard_map/ppermute | solution.py:73
  59.6 5.6 %collective-permute-done.49 = bf16[64,2048]{1,0:T(8,128)(2,1)S(1)} collective-permute-done((bf16[64,2048]{1,0:T(8,128)(2,1)S(1)}, bf16[64,2048]{1,0:T(8,128)(2,1)S(1)}, u32[]{:S(2)}, u32[]{:S(2)}) %collective-permute-start.49) | collective-permute-done | bytes 262176 | tf_op jit(solution)/shard_map/ppermute | solution.py:73
  70.8 3.4 collective-permute-done.51
  78.1 7.4 %collective-permute-done.52.refs_1_ = bf16[64,2048]{1,0:T(8,128)(2,1)S(1)} collective-permute-done((bf16[64,2048]{1,0:T(8,128)(2,1)}, bf16[64,2048]{1,0:T(8,128)(2,1)S(1)}, u32[]{:S(2)}, u32[]{:S(2)}) %collective-permute-start.52) | collective-permute-done | bytes 262176 | tf_op jit(solution)/shard_map/ppermute | solution.py:844
  85.5 8.2 %collective-permute-done.53.refs_2_ = bf16[64,2048]{1,0:T(8,128)(2,1)S(1)} collective-permute-done((bf16[64,2048]{1,0:T(8,128)(2,1)}, bf16[64,2048]{1,0:T(8,128)(2,1)S(1)}, u32[]{:S(2)}, u32[]{:S(2)}) %collective-permute-start.53) | collective-permute-done | bytes 262176 | tf_op jit(solution)/shard_map/ppermute | solution.py:844
  109.9 6.8 %project.1.query_ref.key_ref.value_ref = bf16[512,1536]{1,0:T(8,128)(2,1)S(1)} custom-call(bf16[512,2048]{1,0:T(8,128)(2,1)S(1)} %pad_maximum_fusion.left_ref, bf16[2048,2176]{1,0:T(8,128)(2,1)} %all-gather.4.cloned.1.call-done.weight_ref, f32[1,1536]{1,0:T(1,128)S(1)} %broadcast_in_dim.65.bias_ref), custom_call_target="tpu_custom_call" | custom-call | tf_op jit(solution)/shard_map/project/pallas_call | solution.py:459
  120.6 5.8 %attend.1 = (bf16[512,512]{1,0:T(8,128)(2,1)S(1)}, f32[4,512,1]{2,1,0:T(8,128)}) custom-call(bf16[512,1536]{1,0:T(8,128)(2,1)S(1)} %project.1.query_ref.key_ref.value_ref, bf16[512,1536]{1,0:T(8,128)(2,1)S(1)} %project.1.query_ref.key_ref.value_ref, bf16[512,1536]{1,0:T(8,128)(2,1)S(1)} %project.1.query_ref.key_ref.value_ref, ...), custom_call_target="tpu_custom_call" | custom-call | tf_op jit(solution)/shard_map/attend/pallas_call | solution.py:652
  127.5 5.8 %collective-permute-start.55 = (bf16[64,2048]{1,0:T(8,128)(2,1)}, bf16[64,2048]{1,0:T(8,128)(2,1)}, u32[]{:S(2)}, u32[]{:S(2)}) collective-permute-start(bf16[64,2048]{1,0:T(8,128)(2,1)} %get-tuple-element.1062), channel_id=1, source_target_pairs={{0,1},{1,2},{2,3},{3,0},{4,5},{5,6},{6,7},{7,4},{8,9},{9,10},{10,1... | collective-permute-start | bytes 786440 | tf_op jit(solution)/shard_map/ppermute | solution.py:73
  155.5 4.1 collective-permute-done.59
  160.8 4.6 collective-permute-done.57
  165.5 3.8 collective-permute-done.60
  172.8 6.0 %upward_product.5 = (f32[128,2048]{1,0:T(8,128)}, bf16[128,2048]{1,0:T(8,128)(2,1)}) custom-call(bf16[2048,2048]{1,0:T(8,128)(2,1)} %all-gather.6.cloned.1.call-done.refs_0_, bf16[64,2048]{1,0:T(8,128)(2,1)S(1)} %get-tuple-element.1061.refs_1_, bf16[64,2048]{1,0:T(8,128)(2,1)S(1)} %get-tuple-element.1060.refs_2_, f32[1,2048]{1,0:T(1,128)S(1)} %bitcast.178), custom_call_target="tpu_custom_call" | custom-call | flops 536870912 | bytes 8388608 | tf_op jit(solution)/shard_map/upward_product/pallas_call | solution.py:430
  178.8 4.6 collective-permute-done.62.refs_2_
  183.4 5.7 %collective-permute-done.61.refs_1_ = bf16[64,2048]{1,0:T(8,128)(2,1)} collective-permute-done((bf16[64,2048]{1,0:T(8,128)(2,1)S(1)}, bf16[64,2048]{1,0:T(8,128)(2,1)}, u32[]{:S(2)}, u32[]{:S(2)}) %collective-permute-start.61) | collective-permute-done | bytes 262176 | tf_op jit(solution)/shard_map/ppermute | solution.py:73
  189.1 7.0 %upward_product.6 = (f32[128,2048]{1,0:T(8,128)}, bf16[128,2048]{1,0:T(8,128)(2,1)}) custom-call(bf16[2048,2048]{1,0:T(8,128)(2,1)} %all-gather.6.cloned.1.call-done.refs_0_, bf16[64,2048]{1,0:T(8,128)(2,1)} %collective-permute-done.61.refs_1_, bf16[64,2048]{1,0:T(8,128)(2,1)S(1)} %collective-permute-done.62.refs_2_, f32[1,2048]{1,0:T(1,128)S(1)} %bitcast.179), custom_call_target="tpu_custom_call" | custom-call | flops 536870912 | bytes 8388608 | tf_op jit(solution)/shard_map/upward_product/pallas_call | solution.py:430
  196.2 4.1 collective-permute-done.63.refs_1_
  200.7 6.1 %upward_product.7 = (f32[128,2048]{1,0:T(8,128)}, bf16[128,2048]{1,0:T(8,128)(2,1)}) custom-call(bf16[2048,2048]{1,0:T(8,128)(2,1)} %all-gather.6.cloned.1.call-done.refs_0_, bf16[64,2048]{1,0:T(8,128)(2,1)S(1)} %collective-permute-done.63.refs_1_, bf16[64,2048]{1,0:T(8,128)(2,1)S(1)} %collective-permute-done.64.refs_2_, f32[1,2048]{1,0:T(1,128)S(1)} %bitcast.180), custom_call_target="tpu_custom_call" | custom-call | flops 536870912 | bytes 8388608 | tf_op jit(solution)/shard_map/upward_product/pallas_call | solution.py:430
  208.9 11.9 %conditional.16 = (f32[128,2048]{1,0:T(8,128)}, bf16[128,2048]{1,0:T(8,128)(2,1)}, bf16[128,2048]{1,0:T(8,128)(2,1)}) conditional(s32[]{:T(128)} %bitcast.20, () %tuple.191, (f32[8,1,256]{2,1,0:T(1,128)S(1)}, bf16[2048,2048]{1,0:T(8,128)(2,1)}, bf16[64,2048]{1,0:T(8,128)(2,1)}, bf16[64,2048]{1,0:T(8,128)(2,1)}, ...), branch_computations={%region_10.11_spmd, %region_11.12_spmd} | conditional | flops 536870912 | bytes 10485824 | solution.py:55
  208.9 7.0 %upward_product.4 = (f32[128,2048]{1,0:T(8,128)}, bf16[128,2048]{1,0:T(8,128)(2,1)}) custom-call(bf16[2048,2048]{1,0:T(8,128)(2,1)} %get-tuple-element.417.refs_0_, bf16[64,2048]{1,0:T(8,128)(2,1)} %get-tuple-element.418.refs_1_, bf16[64,2048]{1,0:T(8,128)(2,1)} %get-tuple-element.419.refs_2_, f32[1,2048]{1,0:T(1,128)S(1)} %bitcast.181), custom_call_target="tpu_custom_call" | custom-call | flops 536870912 | bytes 8388608 | tf_op jit(solution)/shard_map/cond/branch_1_fun/upward_product/pallas_call | solution.py:430
  215.9 4.8 collective-permute-done
  220.8 11.4 %conditional.17 = (bf16[128,2048]{1,0:T(8,128)(2,1)}, bf16[128,2048]{1,0:T(8,128)(2,1)}, bf16[128,2048]{1,0:T(8,128)(2,1)}, bf16[128,2048]{1,0:T(8,128)(2,1)}, f...) conditional(s32[]{:T(128)} %bitcast.20, () %tuple.180, (f32[32,64]{1,0:T(8,128)S(1)}, ...), branch_computations={%region_12.13_spmd, %region_13.14_spmd} | conditional | bytes 2883646 | solution.py:55
  220.8 10.6 %dense_product.1 = (bf16[128,2048]{1,0:T(8,128)(2,1)}, bf16[128,2048]{1,0:T(8,128)(2,1)}, bf16[128,2048]{1,0:T(8,128)(2,1)}, bf16[128,2048]{1,0:T(8,128)(2,1)}, f32[512,128]{1,0:T(8,128)S(1)}) custom-call(bf16[128,2048]{1,0:T(8,128)(2,1)} %get-tuple-element.424.refs_0_, bf16[128,2048]{1,0:T(8,128)(2,1)} %get-tuple-element.425.refs_1_, ...), custom_call_target="tpu_custom_call" | custom-call | tf_op jit(solution)/shard_map/cond/branch_1_fun/dense_product/pallas_call | solution.py:506
  232.4 3.6 collective-permute-start.68
  241.0 3.4 fusion.64
  244.4 13.7 %conditional.18 = (bf16[128,2048]{1,0:T(8,128)(2,1)}, bf16[128,2048]{1,0:T(8,128)(2,1)}, f32[8,2048]{1,0:T(8,128)}, bf16[128,2048]{1,0:T(8,128)(2,1)}) conditional(s32[]{:T(128)} %bitcast.20, () %tuple.199, (bf16[2048,2048]{1,0:T(8,128)(2,1)}, bf16[2048,2048]{1,0:T(8,128)(2,1)}, bf16[128,2048]{1,0:T(8,128)(2,1)S(1)}, f32[128,2048]{1,0:T(8,128)S(1)}, ...), branch_computations={%region_16.17_spmd, %region_17.18_spmd} | conditional | flops 2147745792 | bytes 20447304 | solution.py:55
  245.1 10.3 %second_product.4 = (f32[128,2048]{1,0:T(8,128)S(1)}, bf16[128,2048]{1,0:T(8,128)(2,1)}, f32[8,2048]{1,0:T(8,128)}) custom-call(bf16[2048,2048]{1,0:T(8,128)(2,1)} %get-tuple-element.436.down_ref, bf16[2048,2048]{1,0:T(8,128)(2,1)} %get-tuple-element.437.up_ref, bf16[128,2048]{1,0:T(8,128)(2,1)S(1)} %get-tuple-element.438.left_ref, ...), custom_call_target="tpu_custom_call" | custom-call | flops 2147483648 | bytes 16777216 | tf_op jit(solution)/shard_map/cond/branch_1_fun/second_product/pallas_call | solution.py:581
  258.1 23.6 %conditional.19 = (bf16[128,2048]{1,0:T(8,128)(2,1)}, bf16[128,2048]{1,0:T(8,128)(2,1)S(1)}, f32[8,2048]{1,0:T(8,128)S(1)}, bf16[128,2048]{1,0:T(8,128)(2,1)}, bf16[2048,2048]{1,0:T(8,128)(2,1)}) conditional(s32[]{:T(128)} %bitcast.20, () %tuple.198, (bf16[128,2048]{1,0:T(8,128)(2,1)}, bf16[2048,2048]{1,0:T(8,128)(2,1)}, ...), branch_computations={%region_18.19_spmd, %region_19.20_spmd} | conditional | flops 10739253248 | bytes 53502740 | solution.py:55
  260.3 11.5 %second_product.5 = (f32[128,2048]{1,0:T(8,128)S(1)}, bf16[128,2048]{1,0:T(8,128)(2,1)S(1)}, f32[8,2048]{1,0:T(8,128)S(1)}) custom-call(bf16[2048,2048]{1,0:T(8,128)(2,1)} %get-tuple-element.445.down_ref, bf16[2048,2048]{1,0:T(8,128)(2,1)} %get-tuple-element.446.up_ref, bf16[128,2048]{1,0:T(8,128)(2,1)} %get-tuple-element.447.left_ref.refs_6_, ...), custom_call_target="tpu_custom_call" | custom-call | flops 2147483648 | bytes 16777216 | tf_op jit(solution)/shard_map/cond/branch_1_fun/second_product/pallas_call | solution.py:581
  271.9 7.8 %rows_product.2 = bf16[2048,2048]{1,0:T(8,128)(2,1)} custom-call(bf16[128,2048]{1,0:T(8,128)(2,1)S(1)} %copy-done.38, bf16[128,2048]{1,0:T(8,128)(2,1)S(1)} %copy-done.39, bf16[128,2048]{1,0:T(8,128)(2,1)S(1)} %copy-done.40, bf16[128,2048]{1,0:T(8,128)(2,1)} %get-tuple-element.458.refs_3_, bf16[128,2048]{1,0:T(8,128)(2,1)S(1)} %copy-done.29, ...), custom_call_target="tpu_custom_call" | custom-call | flops 8589934592 | bytes 16777216 | tf_op jit(solution)/shard_map/cond/branch_1_fun/rows_product/pallas_call | solution.py:753
  281.7 13.7 %conditional.20 = (bf16[128,2048]{1,0:T(8,128)(2,1)S(1)}, bf16[128,2048]{1,0:T(8,128)(2,1)}, f32[8,2048]{1,0:T(8,128)}) conditional(s32[]{:T(128)} %bitcast.20, () %tuple.197, (bf16[128,2048]{1,0:T(8,128)(2,1)}, bf16[2048,2048]{1,0:T(8,128)(2,1)}, bf16[2048,2048]{1,0:T(8,128)(2,1)}, bf16[128,2048]{1,0:T(8,128)(2,1)}, f32[128,2048]{1,0:T(8,128)}) %tuple.202), branch_computations={%region_20.21_spmd, %region_21.22_spmd} | conditional | flops 2148270080 | bytes 20971584 | solution.py:55
  283.7 11.6 %second_product.6 = (f32[128,2048]{1,0:T(8,128)S(1)}, bf16[128,2048]{1,0:T(8,128)(2,1)}, f32[8,2048]{1,0:T(8,128)}) custom-call(bf16[2048,2048]{1,0:T(8,128)(2,1)} %get-tuple-element.462.down_ref, bf16[2048,2048]{1,0:T(8,128)(2,1)} %get-tuple-element.463.up_ref, bf16[128,2048]{1,0:T(8,128)(2,1)} %get-tuple-element.464.left_ref, ...), custom_call_target="tpu_custom_call" | custom-call | flops 2147483648 | bytes 16777216 | tf_op jit(solution)/shard_map/cond/branch_1_fun/second_product/pallas_call | solution.py:581
  295.5 15.7 %conditional.21 = (f32[128,2048]{1,0:T(8,128)S(1)}, bf16[128,2048]{1,0:T(8,128)(2,1)}, f32[8,2048]{1,0:T(8,128)}, f32[2048]{0:T(1024)S(1)}) conditional(s32[]{:T(128)} %bitcast.20, () %tuple.196, (bf16[128,2048]{1,0:T(8,128)(2,1)S(1)}, bf16[2048,2048]{1,0:T(8,128)(2,1)}, bf16[2048,2048]{1,0:T(8,128)(2,1)}, bf16[128,2048]{1,0:T(8,128)(2,1)}, ...), branch_computations={%region_22.23_spmd, %region_23.25_spmd} | conditional | flops 2148268032 | bytes 21504072 | solution.py:55
  296.4 14.2 %second_product.7 = (f32[128,2048]{1,0:T(8,128)S(1)}, bf16[128,2048]{1,0:T(8,128)(2,1)}, f32[8,2048]{1,0:T(8,128)}) custom-call(bf16[2048,2048]{1,0:T(8,128)(2,1)} %get-tuple-element.470.down_ref, bf16[2048,2048]{1,0:T(8,128)(2,1)} %get-tuple-element.471.up_ref, bf16[128,2048]{1,0:T(8,128)(2,1)} %get-tuple-element.472.left_ref, ...), custom_call_target="tpu_custom_call" | custom-call | flops 2147483648 | bytes 16777216 | tf_op jit(solution)/shard_map/cond/branch_1_fun/second_product/pallas_call | solution.py:581
  315.3 11.3 %conditional.22 = (bf16[128,2048]{1,0:T(8,128)(2,1)}, bf16[1024,2048]{1,0:T(8,128)(2,1)}) conditional(s32[]{:T(128)} %bitcast.20, () %tuple.176, (bf16[128,2048]{1,0:T(8,128)(2,1)}, bf16[64,2048]{1,0:T(8,128)(2,1)}, bf16[64,2048]{1,0:T(8,128)(2,1)S(1)}, bf16[64,2048]{1,0:T(8,128)(2,1)}, bf16[64,2048]{1,0:T(8,128)(2,1)}, ...), branch_computations={%region_27.28_spmd, %region_28.29_spmd} | conditional | flops 1073741824 | bytes 6291544 | solution.py:55
  317.7 6.4 %pair_product.4 = bf16[1024,2048]{1,0:T(8,128)(2,1)} custom-call(s32[1]{0:T(128)} %bitcast.1.me_ref, bf16[64,2048]{1,0:T(8,128)(2,1)} %get-tuple-element.478.refs_0_, bf16[64,2048]{1,0:T(8,128)(2,1)S(1)} %get-tuple-element.479.refs_1_, bf16[64,2048]{1,0:T(8,128)(2,1)} %get-tuple-element.480.refs_2_, bf16[64,2048]{1,0:T(8,128)(2,1)} %get-tuple-element.481.refs_3_, ...), custom_call_target="tpu_custom_call" | custom-call | flops 1073741824 | bytes 4194304 | tf_op jit(solution)/shard_map/cond/branch_1_fun/pair_product/pallas_call | solution.py:372
  327.8 16.5 %conditional.23 = (bf16[128,2048]{1,0:T(8,128)(2,1)}, bf16[1024,2048]{1,0:T(8,128)(2,1)}, f32[32,576]{1,0:T(8,128)S(1)}) conditional(s32[]{:T(128)} %bitcast.20, () %tuple.175, (bf16[128,2048]{1,0:T(8,128)(2,1)}, bf16[1024,2048]{1,0:T(8,128)(2,1)}, f32[128,2048]{1,0:T(8,128)}, f32[128,2048]{1,0:T(8,128)}, f32[128,2048]{1,0:T(8,128)}, ...), branch_computations={%region_29.30_spmd, %region_30.0_spmd} | conditional | flops 4716547 | bytes 30057196 | solution.py:55
  344.9 15.7 %conditional.24 = (bf16[128,2048]{1,0:T(8,128)(2,1)}, bf16[256,1024]{1,0:T(8,128)(2,1)}, bf16[256,1024]{1,0:T(8,128)(2,1)}, bf16[256,1024]{1,0:T(8,128)(2,1)}, b...) conditional(s32[]{:T(128)} %bitcast.20, () %tuple.174, ...), branch_computations={%region_39.40_spmd, %region_40.41_spmd} | conditional | flops 1073741824 | bytes 6291600 | solution.py:55
  344.9 7.0 %pair_product.5 = (bf16[256,1024]{1,0:T(8,128)(2,1)}, bf16[256,1024]{1,0:T(8,128)(2,1)}, bf16[256,1024]{1,0:T(8,128)(2,1)}, bf16[256,1024]{1,0:T(8,128)(2,1)}, b...) custom-call(s32[1]{0:T(128)} %bitcast.3.me_ref, ...), custom_call_target="tpu_custom_call" | custom-call | flops 1073741824 | bytes 4194304 | tf_op jit(solution)/shard_map/cond/branch_1_fun/pair_product/pallas_call | solution.py:372
  351.9 8.7 %collective-permute-done.4 = bf16[128,2048]{1,0:T(8,128)(2,1)} collective-permute-done((bf16[128,2048]{1,0:T(8,128)(2,1)}, bf16[128,2048]{1,0:T(8,128)(2,1)}, u32[]{:S(2)}, u32[]{:S(2)}) %collective-permute-start.4) | collective-permute-done | bytes 524320 | tf_op jit(solution)/shard_map/cond/branch_1_fun/ppermute | solution.py:73
  360.6 20.8 %conditional.25 = (bf16[128,2048]{1,0:T(8,128)(2,1)}, bf16[256,1024]{1,0:T(8,128)(2,1)}, bf16[256,1024]{1,0:T(8,128)(2,1)}, bf16[512,512]{1,0:T(8,128)(2,1)S(1)}, bf16[512,2048]{1,0:T(8,128)(2,1)}) conditional(s32[]{:T(128)} %bitcast.20, () %tuple.210, (bf16[128,2048]{1,0:T(8,128)(2,1)}, bf16[128,2048]{1,0:T(8,128)(2,1)}, ...), branch_computations={%region_41.42_spmd, %region_42.43_spmd} | conditional | flops 2416967680 | bytes 15204512 | solution.py:55
  362.2 7.3 %collective-permute-start.11 = (bf16[256,1024]{1,0:T(8,128)(2,1)}, bf16[256,1024]{1,0:T(8,128)(2,1)}, u32[]{:S(2)}, u32[]{:S(2)}) collective-permute-start(bf16[256,1024]{1,0:T(8,128)(2,1)} %get-tuple-element.536), channel_id=1, source_target_pairs={{0,16},{4,20},{8,24},{12,28},{16,0},{20,4},{24,8},{28,12},{1,17},{... | collective-permute-start | bytes 1572872 | tf_op jit(solution)/shard_map/cond/branch_1_fun/ppermute | solution.py:333
  370.7 4.1 rows_product.3
  374.8 4.4 against.1
  382.6 18.4 %conditional.26 = (bf16[128,2048]{1,0:T(8,128)(2,1)}, bf16[256,1024]{1,0:T(8,128)(2,1)}, bf16[256,1024]{1,0:T(8,128)(2,1)}, bf16[512,1536]{1,0:T(8,128)(2,1)}, f32[8,1536]{1,0:T(8,128)}) conditional(s32[]{:T(128)} %bitcast.20, () %tuple.209, (bf16[128,2048]{1,0:T(8,128)(2,1)}, bf16[128,2048]{1,0:T(8,128)(2,1)}, bf16[256,1024]{1,0:T(8,128)(2,1)}, ...), branch_computations={%region_43.44_spmd, %region_44.45_spmd} | conditional | flops 1074790400 | bytes 14164156 | solution.py:55
  390.3 8.4 %attend_back.1 = (bf16[512,1536]{1,0:T(8,128)(2,1)}, f32[8,1536]{1,0:T(8,128)}) custom-call(bf16[512,1536]{1,0:T(8,128)(2,1)S(1)} %get-tuple-element.551.query_ref.key_ref.value_ref, bf16[512,1536]{1,0:T(8,128)(2,1)S(1)} %get-tuple-element.551.query_ref.key_ref.value_ref, bf16[512,1536]{1,0:T(8,128)(2,1)S(1)} %get-tuple-element.551.query_ref.key_ref.value_ref, ...), custom_call_target="tpu_custom_call" | custom-call | tf_op jit(solution)/shard_map/cond/branch_1_fun/attend_back/pallas_call | solution.py:712
  401.0 17.7 %conditional.27 = (bf16[256,1024]{1,0:T(8,128)(2,1)}, bf16[256,1024]{1,0:T(8,128)(2,1)}, bf16[1024,1536]{1,0:T(8,128)(2,1)}, bf16[128,2048]{1,0:T(8,128)(2,1)}, ...) conditional(s32[]{:T(128)} %bitcast.20, () %tuple.173, (bf16[256,1024]{1,0:T(8,128)(2,1)}, ...), branch_computations={%region_45.46_spmd, %region_46.47_spmd} | conditional | flops 1880883200 | bytes 25977060 | solution.py:55
  405.0 5.7 %pair_product.6 = bf16[1024,1536]{1,0:T(8,128)(2,1)} custom-call(s32[1]{0:T(128)} %bitcast.4.me_ref, bf16[128,2048]{1,0:T(8,128)(2,1)} %get-tuple-element.560.refs_0_, bf16[128,2048]{1,0:T(8,128)(2,1)} %get-tuple-element.561.refs_1_, bf16[128,2048]{1,0:T(8,128)(2,1)} %get-tuple-element.562.refs_2_, bf16[128,2048]{1,0:T(8,128)(2,1)} %get-tuple-element.563.refs_3_, ...), custom_call_target="tpu_custom_call" | custom-call | flops 1073741824 | bytes 4194304 | tf_op jit(solution)/shard_map/cond/branch_1_fun/pair_product/pallas_call | solution.py:372
  410.7 4.2 against_sums.4
  419.9 19.7 %conditional.28 = (bf16[128,2048]{1,0:T(8,128)(2,1)}, bf16[256,768]{1,0:T(8,128)(2,1)}, bf16[256,768]{1,0:T(8,128)(2,1)}, bf16[256,768]{1,0:T(8,128)(2,1)}, bf16...) conditional(s32[]{:T(128)} %bitcast.20, () %tuple.218, ...), branch_computations={%region_48.49_spmd, %region_49.50_spmd} | conditional | flops 2953576448 | bytes 46924804 | solution.py:55
  425.9 5.5 %against_sums.5 = (f32[128,2048]{1,0:T(8,128)S(1)}, f32[8,2048]{1,0:T(8,128)}) custom-call(bf16[2048,1536]{1,0:T(8,128)(2,1)} %get-tuple-element.589.refs_0_, bf16[128,1536]{1,0:T(8,128)(2,1)S(1)} %slice.189.refs_1_, f32[128,2048]{1,0:T(8,128)} %get-tuple-element.590.refs_2_), custom_call_target="tpu_custom_call" | custom-call | flops 805306368 | bytes 6291456 | tf_op jit(solution)/shard_map/cond/branch_1_fun/against_sums/pallas_call | solution.py:430
  433.4 4.3 pair_product.7
  439.6 29.4 %conditional.29 = (bf16[128,2048]{1,0:T(8,128)(2,1)}, bf16[256,768]{1,0:T(8,128)(2,1)}, bf16[256,768]{1,0:T(8,128)(2,1)}, bf16[256,768]{1,0:T(8,128)(2,1)}, bf16...) conditional(s32[]{:T(128)} %bitcast.20, () %tuple.217, ...), branch_computations={%region_50.51_spmd, %region_51.52_spmd} | conditional | flops 2695718400 | bytes 39466204 | solution.py:55
  450.0 3.7 against_sums.6
  453.8 4.6 against_sums.7
  464.7 4.2 collective-permute-done.41
  469.0 27.2 %conditional.30 = (f32[128,2048]{1,0:T(8,128)S(1)}, bf16[64,1536]{1,0:T(8,128)(2,1)S(1)}, bf16[64,1536]{1,0:T(8,128)(2,1)}, bf16[64,1536]{1,0:T(8,128)(2,1)}, bf...) conditional(s32[]{:T(128)} %bitcast.20, () %tuple.216, ...), branch_computations={%region_53.54_spmd, %region_54.55_spmd} | conditional | flops 1074291968 | bytes 24517900 | solution.py:55
  471.0 7.4 %collective-permute-done.28.refs_2_ = bf16[256,768]{1,0:T(8,128)(2,1)S(1)} collective-permute-done((bf16[256,768]{1,0:T(8,128)(2,1)}, bf16[256,768]{1,0:T(8,128)(2,1)S(1)}, u32[]{:S(2)}, u32[]{:S(2)}) %collective-permute-start.28) | collective-permute-done | bytes 393248 | tf_op jit(solution)/shard_map/cond/branch_1_fun/ppermute | solution.py:333
  496.8 31.6 %conditional.31 = (f32[64,6144]{1,0:T(8,128)}, f32[64,8192]{1,0:T(8,128)}, f32[256,2048]{1,0:T(8,128)}, f32[64,2048]{1,0:T(8,128)}, f32[1,128,2048]{2,1,0:T(8,128)}) conditional(s32[]{:T(128)} %bitcast.20, () %tuple.215, (bf16[64,1536]{1,0:T(8,128)(2,1)}, bf16[64,1536]{1,0:T(8,128)(2,1)}, bf16[64,1536]{1,0:T(8,128)(2,1)}, ...), branch_computations={%region_55.56_spmd, %region_56.59_spmd} | conditional | flops 3277058 | bytes 19732312 | solution.py:55
  511.1 10.4 %collective-permute-done.24 = bf16[64,2048]{1,0:T(8,128)(2,1)} collective-permute-done((bf16[64,2048]{1,0:T(8,128)(2,1)}, bf16[64,2048]{1,0:T(8,128)(2,1)}, u32[]{:S(2)}, u32[]{:S(2)}) %collective-permute-start.24) | collective-permute-done | bytes 262176 | tf_op jit(solution)/shard_map/cond/branch_1_fun/ppermute | solution.py:1179
  (470 shorter events, 212.7 us)
Async XLA Ops:
  7.2 97.8 %all-gather.4.cloned.1.call-start = ((), (), s32[]{:S(2)}) async-start(), calls=%async_computation.2 | async-start | bytes 10027008 | tf_op jit(solution)/shard_map/all_gather | solution.py:329
  9.6 23.0 %collective-permute-start.45 = (bf16[64,2048]{1,0:T(8,128)(2,1)}, bf16[64,2048]{1,0:T(8,128)(2,1)S(1)}, u32[]{:S(2)}, u32[]{:S(2)}) collective-permute-start(bf16[64,2048]{1,0:T(8,128)(2,1)} %param.60), channel_id=1, source_target_pairs={{0,0},{1,16},{2,2},{3,18},{4,4},{5,20},{6,6},{7,22},{8,8},{9,24},{... | collective-permute-start | bytes 786440 | tf_op jit(solution)/shard_map/ppermute | solution.py:959
  13.0 11.6 %collective-permute-start.42 = (bf16[64,1664]{1,0:T(8,128)(2,1)}, bf16[64,1664]{1,0:T(8,128)(2,1)S(1)}, u32[]{:S(2)}, u32[]{:S(2)}) collective-permute-start(bf16[64,1664]{1,0:T(8,128)(2,1)} %get-tuple-element.825), channel_id=1, source_target_pairs={{0,1},{1,2},{2,3},{3,0},{4,5},{5,6},{6,7},{7,4},{8,9},{9,10},{10,1... | collective-permute-start | bytes 638984 | tf_op jit(solution)/shard_map/ppermute | solution.py:844
  13.1 18.0 %collective-permute-start.43 = (bf16[64,1664]{1,0:T(8,128)(2,1)}, bf16[64,1664]{1,0:T(8,128)(2,1)S(1)}, u32[]{:S(2)}, u32[]{:S(2)}) collective-permute-start(bf16[64,1664]{1,0:T(8,128)(2,1)} %get-tuple-element.826), channel_id=1, source_target_pairs={{0,2},{1,3},{2,0},{3,1},{4,6},{5,7},{6,4},{7,5},{8,10},{9,11},{10,... | collective-permute-start | bytes 638984 | tf_op jit(solution)/shard_map/ppermute | solution.py:844
  15.7 16.9 %collective-permute-start.44 = (bf16[64,1664]{1,0:T(8,128)(2,1)}, bf16[64,1664]{1,0:T(8,128)(2,1)S(1)}, u32[]{:S(2)}, u32[]{:S(2)}) collective-permute-start(bf16[64,1664]{1,0:T(8,128)(2,1)} %get-tuple-element.827), channel_id=1, source_target_pairs={{0,3},{1,0},{2,1},{3,2},{4,7},{5,4},{6,5},{7,6},{8,11},{9,8},{10,9... | collective-permute-start | bytes 638984 | tf_op jit(solution)/shard_map/ppermute | solution.py:844
  36.4 136.4 %all-gather.6.cloned.1.call-start = ((), (), s32[]{:S(2)}) async-start(), calls=%async_computation.3 | async-start | bytes 9437184 | tf_op jit(solution)/shard_map/all_gather | solution.py:329
  36.5 11.9 %collective-permute-start.46 = (bf16[64,2048]{1,0:T(8,128)(2,1)S(1)}, bf16[64,2048]{1,0:T(8,128)(2,1)S(1)}, u32[]{:S(2)}, u32[]{:S(2)}) collective-permute-start(bf16[64,2048]{1,0:T(8,128)(2,1)S(1)} %get-tuple-element.1064), channel_id=1, source_target_pairs={{0,1},{1,2},{2,3},{3,0},{4,5},{5,6},{6,7},{7,4},{8,9},{9,10},{10,1... | collective-permute-start | bytes 786440 | tf_op jit(solution)/shard_map/ppermute | solution.py:73
  39.2 14.8 %collective-permute-start.47 = (bf16[64,2048]{1,0:T(8,128)(2,1)S(1)}, bf16[64,2048]{1,0:T(8,128)(2,1)S(1)}, u32[]{:S(2)}, u32[]{:S(2)}) collective-permute-start(bf16[64,2048]{1,0:T(8,128)(2,1)S(1)} %get-tuple-element.1065), channel_id=1, source_target_pairs={{0,1},{1,2},{2,3},{3,0},{4,5},{5,6},{6,7},{7,4},{8,9},{9,10},{10,1... | collective-permute-start | bytes 786440 | tf_op jit(solution)/shard_map/ppermute | solution.py:73
  48.3 11.2 %collective-permute-start.48 = (bf16[64,2048]{1,0:T(8,128)(2,1)S(1)}, bf16[64,2048]{1,0:T(8,128)(2,1)S(1)}, u32[]{:S(2)}, u32[]{:S(2)}) collective-permute-start(bf16[64,2048]{1,0:T(8,128)(2,1)S(1)} %collective-permute-done.46), channel_id=1, source_target_pairs={{0,1},{1,2},{2,3},{3,0},{4,5},{5,6},{6,7},{7,4},{8,9},{9,10},{10,1... | collective-permute-start | bytes 786440 | tf_op jit(solution)/shard_map/ppermute | solution.py:73
  54.0 11.2 %collective-permute-start.49 = (bf16[64,2048]{1,0:T(8,128)(2,1)S(1)}, bf16[64,2048]{1,0:T(8,128)(2,1)S(1)}, u32[]{:S(2)}, u32[]{:S(2)}) collective-permute-start(bf16[64,2048]{1,0:T(8,128)(2,1)S(1)} %collective-permute-done.47), channel_id=1, source_target_pairs={{0,1},{1,2},{2,3},{3,0},{4,5},{5,6},{6,7},{7,4},{8,9},{9,10},{10,1... | collective-permute-start | bytes 786440 | tf_op jit(solution)/shard_map/ppermute | solution.py:73
  59.6 11.2 %collective-permute-start.50 = (bf16[64,2048]{1,0:T(8,128)(2,1)S(1)}, bf16[64,2048]{1,0:T(8,128)(2,1)S(1)}, u32[]{:S(2)}, u32[]{:S(2)}) collective-permute-start(bf16[64,2048]{1,0:T(8,128)(2,1)S(1)} %collective-permute-done.48), channel_id=1, source_target_pairs={{0,1},{1,2},{2,3},{3,0},{4,5},{5,6},{6,7},{7,4},{8,9},{9,10},{10,1... | collective-permute-start | bytes 786440 | tf_op jit(solution)/shard_map/ppermute | solution.py:73
  65.2 9.0 %collective-permute-start.51 = (bf16[64,2048]{1,0:T(8,128)(2,1)S(1)}, bf16[64,2048]{1,0:T(8,128)(2,1)S(1)}, u32[]{:S(2)}, u32[]{:S(2)}) collective-permute-start(bf16[64,2048]{1,0:T(8,128)(2,1)S(1)} %collective-permute-done.49), channel_id=1, source_target_pairs={{0,1},{1,2},{2,3},{3,0},{4,5},{5,6},{6,7},{7,4},{8,9},{9,10},{10,1... | collective-permute-start | bytes 786440 | tf_op jit(solution)/shard_map/ppermute | solution.py:73
  74.2 11.3 %collective-permute-start.52 = (bf16[64,2048]{1,0:T(8,128)(2,1)}, bf16[64,2048]{1,0:T(8,128)(2,1)S(1)}, u32[]{:S(2)}, u32[]{:S(2)}) collective-permute-start(bf16[64,2048]{1,0:T(8,128)(2,1)} %get-tuple-element.837), channel_id=1, source_target_pairs={{0,1},{1,2},{2,3},{3,0},{4,5},{5,6},{6,7},{7,4},{8,9},{9,10},{10,1... | collective-permute-start | bytes 786440 | tf_op jit(solution)/shard_map/ppermute | solution.py:844
  74.6 19.1 %collective-permute-start.53 = (bf16[64,2048]{1,0:T(8,128)(2,1)}, bf16[64,2048]{1,0:T(8,128)(2,1)S(1)}, u32[]{:S(2)}, u32[]{:S(2)}) collective-permute-start(bf16[64,2048]{1,0:T(8,128)(2,1)} %get-tuple-element.838), channel_id=1, source_target_pairs={{0,2},{1,3},{2,0},{3,1},{4,6},{5,7},{6,4},{7,5},{8,10},{9,11},{10,... | collective-permute-start | bytes 786440 | tf_op jit(solution)/shard_map/ppermute | solution.py:844
  76.5 17.2 %collective-permute-start.54 = (bf16[64,2048]{1,0:T(8,128)(2,1)}, bf16[64,2048]{1,0:T(8,128)(2,1)S(1)}, u32[]{:S(2)}, u32[]{:S(2)}) collective-permute-start(bf16[64,2048]{1,0:T(8,128)(2,1)} %get-tuple-element.839), channel_id=1, source_target_pairs={{0,3},{1,0},{2,1},{3,2},{4,7},{5,4},{6,5},{7,6},{8,11},{9,8},{10,9... | collective-permute-start | bytes 786440 | tf_op jit(solution)/shard_map/ppermute | solution.py:844
  96.4 124.3 %all-gather.8.cloned.1.call-start = ((), (), s32[]{:S(2)}) async-start(), calls=%async_computation.4 | async-start | bytes 9437184 | tf_op jit(solution)/shard_map/all_gather | solution.py:329
  97.1 322.7 %reduce-scatter.3.cloned.1.call-start = ((), (), s32[]{:S(2)}) async-start(), calls=%async_computation.5 | async-start | bytes 9437184 | tf_op jit(solution)/shard_map/reduce_scatter | solution.py:778
  127.5 13.7 %collective-permute-start.55 = (bf16[64,2048]{1,0:T(8,128)(2,1)}, bf16[64,2048]{1,0:T(8,128)(2,1)}, u32[]{:S(2)}, u32[]{:S(2)}) collective-permute-start(bf16[64,2048]{1,0:T(8,128)(2,1)} %get-tuple-element.1062), channel_id=1, source_target_pairs={{0,1},{1,2},{2,3},{3,0},{4,5},{5,6},{6,7},{7,4},{8,9},{9,10},{10,1... | collective-permute-start | bytes 786440 | tf_op jit(solution)/shard_map/ppermute | solution.py:73
  133.3 12.6 %collective-permute-start.58 = (bf16[64,2048]{1,0:T(8,128)(2,1)S(1)}, bf16[64,2048]{1,0:T(8,128)(2,1)}, u32[]{:S(2)}, u32[]{:S(2)}) collective-permute-start(bf16[64,2048]{1,0:T(8,128)(2,1)S(1)} %get-tuple-element.1063), channel_id=1, source_target_pairs={{0,1},{1,2},{2,3},{3,0},{4,5},{5,6},{6,7},{7,4},{8,9},{9,10},{10,1... | collective-permute-start | bytes 786440 | tf_op jit(solution)/shard_map/ppermute | solution.py:73
  142.9 11.4 %collective-permute-start.56 = (bf16[64,2048]{1,0:T(8,128)(2,1)}, bf16[64,2048]{1,0:T(8,128)(2,1)}, u32[]{:S(2)}, u32[]{:S(2)}) collective-permute-start(bf16[64,2048]{1,0:T(8,128)(2,1)} %fusion.35), channel_id=1, source_target_pairs={{0,1},{1,2},{2,3},{3,0},{4,5},{5,6},{6,7},{7,4},{8,9},{9,10},{10,1... | collective-permute-start | bytes 786440 | tf_op jit(solution)/shard_map/ppermute | solution.py:73
  146.9 12.7 %collective-permute-start.59 = (bf16[64,2048]{1,0:T(8,128)(2,1)S(1)}, bf16[64,2048]{1,0:T(8,128)(2,1)}, u32[]{:S(2)}, u32[]{:S(2)}) collective-permute-start(bf16[64,2048]{1,0:T(8,128)(2,1)S(1)} %fusion.33), channel_id=1, source_target_pairs={{0,1},{1,2},{2,3},{3,0},{4,5},{5,6},{6,7},{7,4},{8,9},{9,10},{10,1... | collective-permute-start | bytes 786440 | tf_op jit(solution)/shard_map/ppermute | solution.py:73
  155.4 10.0 %collective-permute-start.57 = (bf16[64,2048]{1,0:T(8,128)(2,1)S(1)}, bf16[64,2048]{1,0:T(8,128)(2,1)S(1)}, u32[]{:S(2)}, u32[]{:S(2)}) collective-permute-start(bf16[64,2048]{1,0:T(8,128)(2,1)S(1)} %fusion.34), channel_id=1, source_target_pairs={{0,1},{1,2},{2,3},{3,0},{4,5},{5,6},{6,7},{7,4},{8,9},{9,10},{10,1... | collective-permute-start | bytes 786440 | tf_op jit(solution)/shard_map/ppermute | solution.py:73
  172.3 11.1 %collective-permute-start.62 = (bf16[64,2048]{1,0:T(8,128)(2,1)S(1)}, bf16[64,2048]{1,0:T(8,128)(2,1)S(1)}, u32[]{:S(2)}, u32[]{:S(2)}) collective-permute-start(bf16[64,2048]{1,0:T(8,128)(2,1)S(1)} %get-tuple-element.1060.refs_2_), channel_id=1, source_target_pairs={{0,1},{1,2},{2,3},{3,0},{4,5},{5,6},{6,7},{7,4},{8,9},{9,10},{10,1... | collective-permute-start | bytes 786440 | tf_op jit(solution)/shard_map/ppermute | solution.py:73
  172.4 16.7 %collective-permute-start.61 = (bf16[64,2048]{1,0:T(8,128)(2,1)S(1)}, bf16[64,2048]{1,0:T(8,128)(2,1)}, u32[]{:S(2)}, u32[]{:S(2)}) collective-permute-start(bf16[64,2048]{1,0:T(8,128)(2,1)S(1)} %get-tuple-element.1061.refs_1_), channel_id=1, source_target_pairs={{0,1},{1,2},{2,3},{3,0},{4,5},{5,6},{6,7},{7,4},{8,9},{9,10},{10,1... | collective-permute-start | bytes 786440 | tf_op jit(solution)/shard_map/ppermute | solution.py:73
  183.4 12.7 %collective-permute-start.64 = (bf16[64,2048]{1,0:T(8,128)(2,1)S(1)}, bf16[64,2048]{1,0:T(8,128)(2,1)S(1)}, u32[]{:S(2)}, u32[]{:S(2)}) collective-permute-start(bf16[64,2048]{1,0:T(8,128)(2,1)S(1)} %collective-permute-done.62.refs_2_), channel_id=1, source_target_pairs={{0,1},{1,2},{2,3},{3,0},{4,5},{5,6},{6,7},{7,4},{8,9},{9,10},{10,1... | collective-permute-start | bytes 786440 | tf_op jit(solution)/shard_map/ppermute | solution.py:73
  189.1 11.1 %collective-permute-start.63 = (bf16[64,2048]{1,0:T(8,128)(2,1)}, bf16[64,2048]{1,0:T(8,128)(2,1)S(1)}, u32[]{:S(2)}, u32[]{:S(2)}) collective-permute-start(bf16[64,2048]{1,0:T(8,128)(2,1)} %collective-permute-done.61.refs_1_), channel_id=1, source_target_pairs={{0,1},{1,2},{2,3},{3,0},{4,5},{5,6},{6,7},{7,4},{8,9},{9,10},{10,1... | collective-permute-start | bytes 786440 | tf_op jit(solution)/shard_map/ppermute | solution.py:73
  196.1 10.7 %collective-permute-start.66 = (bf16[64,2048]{1,0:T(8,128)(2,1)S(1)}, bf16[64,2048]{1,0:T(8,128)(2,1)}, u32[]{:S(2)}, u32[]{:S(2)}) collective-permute-start(bf16[64,2048]{1,0:T(8,128)(2,1)S(1)} %collective-permute-done.64.refs_2_), channel_id=1, source_target_pairs={{0,1},{1,2},{2,3},{3,0},{4,5},{5,6},{6,7},{7,4},{8,9},{9,10},{10,1... | collective-permute-start | bytes 786440 | tf_op jit(solution)/shard_map/ppermute | solution.py:73
  208.9 11.9 %collective-permute-start = (bf16[128,2048]{1,0:T(8,128)(2,1)S(1)}, bf16[128,2048]{1,0:T(8,128)(2,1)}, u32[]{:S(2)}, u32[]{:S(2)}) collective-permute-start(bf16[128,2048]{1,0:T(8,128)(2,1)S(1)} %get-tuple-element.423), channel_id=1, source_target_pairs={{0,1},{1,2},{2,3},{3,0},{4,5},{5,6},{6,7},{7,4},{8,9},{9,10},{10,1... | collective-permute-start | bytes 1572872 | tf_op jit(solution)/shard_map/cond/branch_1_fun/ppermute | solution.py:73
  220.8 11.4 %collective-permute-start.1 = (bf16[128,2048]{1,0:T(8,128)(2,1)}, bf16[128,2048]{1,0:T(8,128)(2,1)}, u32[]{:S(2)}, u32[]{:S(2)}) collective-permute-start(bf16[128,2048]{1,0:T(8,128)(2,1)} %get-tuple-element.435), channel_id=1, source_target_pairs={{0,1},{1,2},{2,3},{3,0},{4,5},{5,6},{6,7},{7,4},{8,9},{9,10},{10,1... | collective-permute-start | bytes 1572872 | tf_op jit(solution)/shard_map/cond/branch_1_fun/ppermute | solution.py:73
  244.4 13.5 %collective-permute-start.2 = (bf16[128,2048]{1,0:T(8,128)(2,1)}, bf16[128,2048]{1,0:T(8,128)(2,1)}, u32[]{:S(2)}, u32[]{:S(2)}) collective-permute-start(bf16[128,2048]{1,0:T(8,128)(2,1)} %get-tuple-element.443), channel_id=1, source_target_pairs={{0,1},{1,2},{2,3},{3,0},{4,5},{5,6},{6,7},{7,4},{8,9},{9,10},{10,1... | collective-permute-start | bytes 1572872 | tf_op jit(solution)/shard_map/cond/branch_1_fun/ppermute | solution.py:73
  258.1 21.6 %collective-permute-start.5 = (bf16[128,2048]{1,0:T(8,128)(2,1)}, bf16[128,2048]{1,0:T(8,128)(2,1)}, u32[]{:S(2)}, u32[]{:S(2)}) collective-permute-start(bf16[128,2048]{1,0:T(8,128)(2,1)} %get-tuple-element.444), channel_id=1, source_target_pairs={{0,1},{1,2},{2,3},{3,0},{4,5},{5,6},{6,7},{7,4},{8,9},{9,10},{10,1... | collective-permute-start | bytes 1572872 | tf_op jit(solution)/shard_map/cond/branch_1_fun/ppermute | solution.py:73
  281.7 187.3 %reduce-scatter.5.cloned.1.call-start = ((), (), s32[]{:S(2)}) async-start(), calls=%async_computation.6 | async-start | bytes 2359296 | tf_op jit(solution)/shard_map/reduce_scatter | solution.py:778
  281.8 13.6 %collective-permute-start.6 = (bf16[128,2048]{1,0:T(8,128)(2,1)}, bf16[128,2048]{1,0:T(8,128)(2,1)S(1)}, u32[]{:S(2)}, u32[]{:S(2)}) collective-permute-start(bf16[128,2048]{1,0:T(8,128)(2,1)} %get-tuple-element.461), channel_id=1, source_target_pairs={{0,1},{1,2},{2,3},{3,0},{4,5},{5,6},{6,7},{7,4},{8,9},{9,10},{10,1... | collective-permute-start | bytes 1572872 | tf_op jit(solution)/shard_map/cond/branch_1_fun/ppermute | solution.py:73
  295.5 15.1 %collective-permute-start.25 = (bf16[128,2048]{1,0:T(8,128)(2,1)S(1)}, bf16[128,2048]{1,0:T(8,128)(2,1)S(1)}, u32[]{:S(2)}, u32[]{:S(2)}) collective-permute-start(bf16[128,2048]{1,0:T(8,128)(2,1)S(1)} %get-tuple-element.469), channel_id=1, source_target_pairs={{0,1},{1,2},{2,3},{3,0},{4,5},{5,6},{6,7},{7,4},{8,9},{9,10},{10,1... | collective-permute-start | bytes 1572872 | tf_op jit(solution)/shard_map/cond/branch_1_fun/ppermute | solution.py:73
  315.3 11.3 %collective-permute-start.3 = (bf16[128,2048]{1,0:T(8,128)(2,1)}, bf16[128,2048]{1,0:T(8,128)(2,1)}, u32[]{:S(2)}, u32[]{:S(2)}) collective-permute-start(bf16[128,2048]{1,0:T(8,128)(2,1)} %get-tuple-element.477), channel_id=1, source_target_pairs={{0,1},{1,2},{2,3},{3,0},{4,5},{5,6},{6,7},{7,4},{8,9},{9,10},{10,1... | collective-permute-start | bytes 1572872 | tf_op jit(solution)/shard_map/cond/branch_1_fun/ppermute | solution.py:73
  327.8 16.5 %collective-permute-start.8 = (bf16[1024,2048]{1,0:T(8,128)(2,1)}, bf16[1024,2048]{1,0:T(8,128)(2,1)}, u32[]{:S(2)}, u32[]{:S(2)}) collective-permute-start(bf16[1024,2048]{1,0:T(8,128)(2,1)} %get-tuple-element.491), channel_id=1, source_target_pairs={{0,4},{4,0},{8,12},{12,8},{16,20},{20,16},{24,28},{28,24},{1,5},{5... | collective-permute-start | bytes 12582920 | tf_op jit(solution)/shard_map/cond/branch_1_fun/ppermute | solution.py:333
  327.8 16.4 %collective-permute-start.7 = (bf16[128,2048]{1,0:T(8,128)(2,1)}, bf16[128,2048]{1,0:T(8,128)(2,1)}, u32[]{:S(2)}, u32[]{:S(2)}) collective-permute-start(bf16[128,2048]{1,0:T(8,128)(2,1)} %get-tuple-element.490), channel_id=1, source_target_pairs={{0,1},{1,2},{2,3},{3,0},{4,5},{5,6},{6,7},{7,4},{8,9},{9,10},{10,1... | collective-permute-start | bytes 1572872 | tf_op jit(solution)/shard_map/cond/branch_1_fun/ppermute | solution.py:73
  344.9 15.7 %collective-permute-start.4 = (bf16[128,2048]{1,0:T(8,128)(2,1)}, bf16[128,2048]{1,0:T(8,128)(2,1)}, u32[]{:S(2)}, u32[]{:S(2)}) collective-permute-start(bf16[128,2048]{1,0:T(8,128)(2,1)} %get-tuple-element.511), channel_id=1, source_target_pairs={{0,1},{1,2},{2,3},{3,0},{4,5},{5,6},{6,7},{7,4},{8,9},{9,10},{10,1... | collective-permute-start | bytes 1572872 | tf_op jit(solution)/shard_map/cond/branch_1_fun/ppermute | solution.py:73
  360.6 18.7 %collective-permute-start.9 = (bf16[128,2048]{1,0:T(8,128)(2,1)}, bf16[128,2048]{1,0:T(8,128)(2,1)}, u32[]{:S(2)}, u32[]{:S(2)}) collective-permute-start(bf16[128,2048]{1,0:T(8,128)(2,1)} %get-tuple-element.533), channel_id=1, source_target_pairs={{0,1},{1,2},{2,3},{3,0},{4,5},{5,6},{6,7},{7,4},{8,9},{9,10},{10,1... | collective-permute-start | bytes 1572872 | tf_op jit(solution)/shard_map/cond/branch_1_fun/ppermute | solution.py:109
  360.6 20.8 %collective-permute-start.10 = (bf16[256,1024]{1,0:T(8,128)(2,1)}, bf16[256,1024]{1,0:T(8,128)(2,1)}, u32[]{:S(2)}, u32[]{:S(2)}) collective-permute-start(bf16[256,1024]{1,0:T(8,128)(2,1)} %get-tuple-element.535), channel_id=1, source_target_pairs={{0,8},{4,12},{8,0},{12,4},{16,24},{20,28},{24,16},{28,20},{1,9},{5... | collective-permute-start | bytes 1572872 | tf_op jit(solution)/shard_map/cond/branch_1_fun/ppermute | solution.py:333
  362.2 19.2 %collective-permute-start.11 = (bf16[256,1024]{1,0:T(8,128)(2,1)}, bf16[256,1024]{1,0:T(8,128)(2,1)}, u32[]{:S(2)}, u32[]{:S(2)}) collective-permute-start(bf16[256,1024]{1,0:T(8,128)(2,1)} %get-tuple-element.536), channel_id=1, source_target_pairs={{0,16},{4,20},{8,24},{12,28},{16,0},{20,4},{24,8},{28,12},{1,17},{... | collective-permute-start | bytes 1572872 | tf_op jit(solution)/shard_map/cond/branch_1_fun/ppermute | solution.py:333
  382.6 16.1 %collective-permute-start.12 = (bf16[128,2048]{1,0:T(8,128)(2,1)}, bf16[128,2048]{1,0:T(8,128)(2,1)}, u32[]{:S(2)}, u32[]{:S(2)}) collective-permute-start(bf16[128,2048]{1,0:T(8,128)(2,1)} %get-tuple-element.543), channel_id=1, source_target_pairs={{0,1},{1,2},{2,3},{3,0},{4,5},{5,6},{6,7},{7,4},{8,9},{9,10},{10,1... | collective-permute-start | bytes 1572872 | tf_op jit(solution)/shard_map/cond/branch_1_fun/ppermute | solution.py:109
  385.2 15.7 %collective-permute-start.13 = (bf16[256,1024]{1,0:T(8,128)(2,1)}, bf16[256,1024]{1,0:T(8,128)(2,1)}, u32[]{:S(2)}, u32[]{:S(2)}) collective-permute-start(bf16[256,1024]{1,0:T(8,128)(2,1)} %get-tuple-element.549), channel_id=1, source_target_pairs={{0,16},{4,20},{8,24},{12,28},{16,0},{20,4},{24,8},{28,12},{1,17},{... | collective-permute-start | bytes 1572872 | tf_op jit(solution)/shard_map/cond/branch_1_fun/ppermute | solution.py:333
  388.6 12.3 %collective-permute-start.14 = (bf16[256,1024]{1,0:T(8,128)(2,1)}, bf16[256,1024]{1,0:T(8,128)(2,1)}, u32[]{:S(2)}, u32[]{:S(2)}) collective-permute-start(bf16[256,1024]{1,0:T(8,128)(2,1)} %get-tuple-element.550), channel_id=1, source_target_pairs={{0,8},{4,12},{8,0},{12,4},{16,24},{20,28},{24,16},{28,20},{1,9},{5... | collective-permute-start | bytes 1572872 | tf_op jit(solution)/shard_map/cond/branch_1_fun/ppermute | solution.py:333
  401.1 14.8 %collective-permute-start.17 = (bf16[128,2048]{1,0:T(8,128)(2,1)}, bf16[128,2048]{1,0:T(8,128)(2,1)S(1)}, u32[]{:S(2)}, u32[]{:S(2)}) collective-permute-start(bf16[128,2048]{1,0:T(8,128)(2,1)} %get-tuple-element.570), channel_id=1, source_target_pairs={{0,1},{1,2},{2,3},{3,0},{4,5},{5,6},{6,7},{7,4},{8,9},{9,10},{10,1... | collective-permute-start | bytes 1572872 | tf_op jit(solution)/shard_map/cond/branch_1_fun/ppermute | solution.py:109
  401.1 17.2 %collective-permute-start.15 = (bf16[256,1024]{1,0:T(8,128)(2,1)}, bf16[256,1024]{1,0:T(8,128)(2,1)}, u32[]{:S(2)}, u32[]{:S(2)}) collective-permute-start(bf16[256,1024]{1,0:T(8,128)(2,1)} %get-tuple-element.558), channel_id=1, source_target_pairs={{0,8},{4,12},{8,0},{12,4},{16,24},{20,28},{24,16},{28,20},{1,9},{5... | collective-permute-start | bytes 1572872 | tf_op jit(solution)/shard_map/cond/branch_1_fun/ppermute | solution.py:333
  402.3 16.4 %collective-permute-start.16 = (bf16[256,1024]{1,0:T(8,128)(2,1)}, bf16[256,1024]{1,0:T(8,128)(2,1)}, u32[]{:S(2)}, u32[]{:S(2)}) collective-permute-start(bf16[256,1024]{1,0:T(8,128)(2,1)} %get-tuple-element.559), channel_id=1, source_target_pairs={{0,16},{4,20},{8,24},{12,28},{16,0},{20,4},{24,8},{28,12},{1,17},{... | collective-permute-start | bytes 1572872 | tf_op jit(solution)/shard_map/cond/branch_1_fun/ppermute | solution.py:333
  419.9 12.7 %collective-permute-start.19 = (bf16[1024,1536]{1,0:T(8,128)(2,1)}, bf16[1024,1536]{1,0:T(8,128)(2,1)S(1)}, u32[]{:S(2)}, u32[]{:S(2)}) collective-permute-start(bf16[1024,1536]{1,0:T(8,128)(2,1)} %get-tuple-element.579), channel_id=1, source_target_pairs={{0,4},{4,0},{8,12},{12,8},{16,20},{20,16},{24,28},{28,24},{1,5},{5... | collective-permute-start | bytes 9437192 | tf_op jit(solution)/shard_map/cond/branch_1_fun/ppermute | solution.py:333
  419.9 17.8 %collective-permute-start.18 = (bf16[128,2048]{1,0:T(8,128)(2,1)}, bf16[128,2048]{1,0:T(8,128)(2,1)}, u32[]{:S(2)}, u32[]{:S(2)}) collective-permute-start(bf16[128,2048]{1,0:T(8,128)(2,1)} %get-tuple-element.573), channel_id=1, source_target_pairs={{0,1},{1,2},{2,3},{3,0},{4,5},{5,6},{6,7},{7,4},{8,9},{9,10},{10,1... | collective-permute-start | bytes 1572872 | tf_op jit(solution)/shard_map/cond/branch_1_fun/ppermute | solution.py:73
  439.6 23.2 %collective-permute-start.36 = (bf16[128,2048]{1,0:T(8,128)(2,1)}, bf16[128,2048]{1,0:T(8,128)(2,1)}, u32[]{:S(2)}, u32[]{:S(2)}) collective-permute-start(bf16[128,2048]{1,0:T(8,128)(2,1)} %get-tuple-element.601), channel_id=1, source_target_pairs={{0,1},{1,2},{2,3},{3,0},{4,5},{5,6},{6,7},{7,4},{8,9},{9,10},{10,1... | collective-permute-start | bytes 1572872 | tf_op jit(solution)/shard_map/cond/branch_1_fun/ppermute | solution.py:73
  442.4 17.4 %collective-permute-start.39 = (bf16[256,768]{1,0:T(8,128)(2,1)}, bf16[256,768]{1,0:T(8,128)(2,1)}, u32[]{:S(2)}, u32[]{:S(2)}) collective-permute-start(bf16[256,768]{1,0:T(8,128)(2,1)} %get-tuple-element.609), channel_id=1, source_target_pairs={{0,8},{4,12},{8,0},{12,4},{16,24},{20,28},{24,16},{28,20},{1,9},{5... | collective-permute-start | bytes 1179656 | tf_op jit(solution)/shard_map/cond/branch_1_fun/ppermute | solution.py:333
  444.0 16.5 %collective-permute-start.40 = (bf16[256,768]{1,0:T(8,128)(2,1)}, bf16[256,768]{1,0:T(8,128)(2,1)}, u32[]{:S(2)}, u32[]{:S(2)}) collective-permute-start(bf16[256,768]{1,0:T(8,128)(2,1)} %get-tuple-element.611), channel_id=1, source_target_pairs={{0,16},{4,20},{8,24},{12,28},{16,0},{20,4},{24,8},{28,12},{1,17},{... | collective-permute-start | bytes 1179656 | tf_op jit(solution)/shard_map/cond/branch_1_fun/ppermute | solution.py:333
  444.4 20.3 %collective-permute-start.37 = (bf16[256,768]{1,0:T(8,128)(2,1)}, bf16[256,768]{1,0:T(8,128)(2,1)}, u32[]{:S(2)}, u32[]{:S(2)}) collective-permute-start(bf16[256,768]{1,0:T(8,128)(2,1)} %get-tuple-element.606), channel_id=1, source_target_pairs={{0,8},{4,12},{8,0},{12,4},{16,24},{20,28},{24,16},{28,20},{1,9},{5... | collective-permute-start | bytes 1179656 | tf_op jit(solution)/shard_map/cond/branch_1_fun/ppermute | solution.py:333
  444.8 20.0 %collective-permute-start.38 = (bf16[256,768]{1,0:T(8,128)(2,1)}, bf16[256,768]{1,0:T(8,128)(2,1)}, u32[]{:S(2)}, u32[]{:S(2)}) collective-permute-start(bf16[256,768]{1,0:T(8,128)(2,1)} %get-tuple-element.607), channel_id=1, source_target_pairs={{0,16},{4,20},{8,24},{12,28},{16,0},{20,4},{24,8},{28,12},{1,17},{... | collective-permute-start | bytes 1179656 | tf_op jit(solution)/shard_map/cond/branch_1_fun/ppermute | solution.py:333
  459.8 9.2 %collective-permute-start.41 = (bf16[64,2048]{1,0:T(8,128)(2,1)}, bf16[64,2048]{1,0:T(8,128)(2,1)}, u32[]{:S(2)}, u32[]{:S(2)}) collective-permute-start(bf16[64,2048]{1,0:T(8,128)(2,1)} %get-tuple-element.615), channel_id=1, source_target_pairs={{0,1},{1,2},{2,3},{3,0},{4,5},{5,6},{6,7},{7,4},{8,9},{9,10},{10,1... | collective-permute-start | bytes 786440 | tf_op jit(solution)/shard_map/cond/branch_1_fun/ppermute | solution.py:844
  469.0 9.5 %collective-permute-start.28 = (bf16[256,768]{1,0:T(8,128)(2,1)}, bf16[256,768]{1,0:T(8,128)(2,1)S(1)}, u32[]{:S(2)}, u32[]{:S(2)}) collective-permute-start(bf16[256,768]{1,0:T(8,128)(2,1)} %get-tuple-element.631), channel_id=1, source_target_pairs={{0,16},{4,20},{8,24},{12,28},{16,0},{20,4},{24,8},{28,12},{1,17},{... | collective-permute-start | bytes 1179656 | tf_op jit(solution)/shard_map/cond/branch_1_fun/ppermute | solution.py:333
  469.4 9.5 %collective-permute-start.29 = (bf16[256,768]{1,0:T(8,128)(2,1)}, bf16[256,768]{1,0:T(8,128)(2,1)S(1)}, u32[]{:S(2)}, u32[]{:S(2)}) collective-permute-start(bf16[256,768]{1,0:T(8,128)(2,1)} %get-tuple-element.634), channel_id=1, source_target_pairs={{0,8},{4,12},{8,0},{12,4},{16,24},{20,28},{24,16},{28,20},{1,9},{5... | collective-permute-start | bytes 1179656 | tf_op jit(solution)/shard_map/cond/branch_1_fun/ppermute | solution.py:333
  471.0 24.0 %collective-permute-start.26 = (bf16[128,2048]{1,0:T(8,128)(2,1)}, bf16[128,2048]{1,0:T(8,128)(2,1)}, u32[]{:S(2)}, u32[]{:S(2)}) collective-permute-start(bf16[128,2048]{1,0:T(8,128)(2,1)} %get-tuple-element.625), channel_id=1, source_target_pairs={{0,1},{1,2},{2,3},{3,0},{4,5},{5,6},{6,7},{7,4},{8,9},{9,10},{10,1... | collective-permute-start | bytes 1572872 | tf_op jit(solution)/shard_map/cond/branch_1_fun/ppermute | solution.py:73
  471.0 24.0 %collective-permute-start.27 = (bf16[64,2048]{1,0:T(8,128)(2,1)}, bf16[64,2048]{1,0:T(8,128)(2,1)}, u32[]{:S(2)}, u32[]{:S(2)}) collective-permute-start(bf16[64,2048]{1,0:T(8,128)(2,1)} %get-tuple-element.626), channel_id=1, source_target_pairs={{0,2},{1,3},{2,0},{3,1},{4,6},{5,7},{6,4},{7,5},{8,10},{9,11},{10,... | collective-permute-start | bytes 786440 | tf_op jit(solution)/shard_map/cond/branch_1_fun/ppermute | solution.py:844
  496.8 10.5 %collective-permute-start.20 = (bf16[64,1536]{1,0:T(8,128)(2,1)}, bf16[64,1536]{1,0:T(8,128)(2,1)S(1)}, u32[]{:S(2)}, u32[]{:S(2)}) collective-permute-start(bf16[64,1536]{1,0:T(8,128)(2,1)} %get-tuple-element.641), channel_id=1, source_target_pairs={{0,1},{1,2},{2,3},{3,0},{4,5},{5,6},{6,7},{7,4},{8,9},{9,10},{10,1... | collective-permute-start | bytes 589832 | tf_op jit(solution)/shard_map/cond/branch_1_fun/ppermute | solution.py:844
  498.0 25.3 %collective-permute-start.23 = (bf16[64,2048]{1,0:T(8,128)(2,1)}, bf16[64,2048]{1,0:T(8,128)(2,1)}, u32[]{:S(2)}, u32[]{:S(2)}) collective-permute-start(bf16[64,2048]{1,0:T(8,128)(2,1)} %get-tuple-element.647), channel_id=1, source_target_pairs={{0,3},{1,0},{2,1},{3,2},{4,7},{5,4},{6,5},{7,6},{8,11},{9,8},{10,9... | collective-permute-start | bytes 786440 | tf_op jit(solution)/shard_map/cond/branch_1_fun/ppermute | solution.py:844
  500.7 20.9 %collective-permute-start.24 = (bf16[64,2048]{1,0:T(8,128)(2,1)}, bf16[64,2048]{1,0:T(8,128)(2,1)}, u32[]{:S(2)}, u32[]{:S(2)}) collective-permute-start(bf16[64,2048]{1,0:T(8,128)(2,1)} %get-tuple-element.656), channel_id=1, source_target_pairs={{0,0},{16,1},{2,2},{18,3},{4,4},{20,5},{6,6},{22,7},{8,8},{24,9},{... | collective-permute-start | bytes 786440 | tf_op jit(solution)/shard_map/cond/branch_1_fun/ppermute | solution.py:1179
  502.6 23.4 %collective-permute-start.21 = (bf16[64,1536]{1,0:T(8,128)(2,1)}, bf16[64,1536]{1,0:T(8,128)(2,1)}, u32[]{:S(2)}, u32[]{:S(2)}) collective-permute-start(bf16[64,1536]{1,0:T(8,128)(2,1)} %get-tuple-element.642), channel_id=1, source_target_pairs={{0,2},{1,3},{2,0},{3,1},{4,6},{5,7},{6,4},{7,5},{8,10},{9,11},{10,... | collective-permute-start | bytes 589832 | tf_op jit(solution)/shard_map/cond/branch_1_fun/ppermute | solution.py:844
  504.4 21.6 %collective-permute-start.22 = (bf16[64,1536]{1,0:T(8,128)(2,1)}, bf16[64,1536]{1,0:T(8,128)(2,1)}, u32[]{:S(2)}, u32[]{:S(2)}) collective-permute-start(bf16[64,1536]{1,0:T(8,128)(2,1)} %get-tuple-element.643), channel_id=1, source_target_pairs={{0,3},{1,0},{2,1},{3,2},{4,7},{5,4},{6,5},{7,6},{8,11},{9,8},{10,9... | collective-permute-start | bytes 589832 | tf_op jit(solution)/shard_map/cond/branch_1_fun/ppermute | solution.py:844
  (92 other events, 509.0 us)
Sparse Core Ops, SparseCore 0:
  36.5 58.4 all-gather.3
  97.4 56.5 all-gather.5
  155.9 54.3 all-gather.7
  281.8 77.4 reduce-scatter.2
  381.5 46.8 reduce-scatter.4
